TPU v7x, 256 devices: a whole 4x4x8 slice. The times are simulated.
256 devices in a mesh: space: 8 (over x, y_lo), tm: 32 (over y_hi, z, core).
Axes of the slice: x: 4, y: 4 (y_hi: 2, y_lo: 2; y = y_hi * 2 + y_lo), z: 8, core: 2. Of those that a mesh axis runs over, the one named last changes fastest.
Arguments:
- volume: float32 [32, 32, 128, 128], P('tm', 'space'), may hold values from -6 to 6
- lift_weights: bfloat16 [3, 64, 27], replicated, may hold values from -1.25 to 1.25
- lift_bias: float32 [3, 64], replicated, may hold values from -3 to 3
- mix_weights: bfloat16 [3, 64, 64], replicated, may hold values from -0.75 to 0.75
- out_weights: bfloat16 [3, 64], replicated, may hold values from -0.75 to 0.75
- projector: bfloat16 [2048, 16384], P(None, 'tm'), may hold values from -0.046875 to 0.046875
- measured: float32 [32, 32, 2048], P('tm', 'space'), may hold values from -6 to 6
Outputs:
- updated: float32 [32, 32, 16384], P(None, 'space', 'tm')
All inputs are finite; a program needn't handle non-finite values.
Results may differ from a plain program's by a relative error of at most 0.0027.
Values may be sent and summed in bfloat16 or wider, within the bound.
No kernel may reach another device: no remote copies, remote signals or barrier semaphores. Data moves between devices by JAX's collectives and lax.ppermute only.
A program may use at most 64 MiB of HBM per device.

v0:
```python
import jax
import jax.numpy as jnp
from jax import lax
from jax.sharding import PartitionSpec as P


def extended(x, sides, width):
    for axis, dim in sides:
        size, length = (lax.axis_size(axis), x.shape[dim])
        up = [(i, (i + 1) % size) for i in range(size - 1)]
        down = [(j, i) for i, j in up]
        last = lax.slice_in_dim(x, length - width, length, axis=dim)
        first = lax.slice_in_dim(x, 0, width, axis=dim)
        before = lax.ppermute(last, axis, up)
        after = lax.ppermute(first, axis, down)
        x = jnp.concatenate([before, x, after], axis=dim)
    return x


def lift_taps(block, planes):
    pads = [(0, 0)] + [(1, 1) if d in planes else (0, 0) for d in (1, 2, 3)]
    padded = jnp.pad(block, pads)
    frames = block.shape[0] - 2
    shape = block.shape
    taps = []
    for dt in range(3):
        for da in range(3):
            for db in range(3):
                start = [dt, 0, 0, 0]
                start[planes[0]] = da
                start[planes[1]] = db
                limit = [dt + frames] + [start[i] + shape[i] for i in (1, 2, 3)]
                taps.append(lax.slice(padded, start, limit))
    return jnp.stack(taps, 0)


def correction(block, planes, which, lift_weights, lift_bias, mix_weights, out_weights):
    taps = lift_taps(block, planes)
    pre = jnp.einsum(
        "ck,kfpqr->cfpqr", lift_weights[which], taps, preferred_element_type=jnp.float32
    )
    pre = pre + lift_bias[which][:, None, None, None, None]
    first = jax.nn.relu(pre).astype(jnp.bfloat16)
    second = jnp.einsum(
        "cd,dfpqr->cfpqr", mix_weights[which], first, preferred_element_type=jnp.float32
    )
    second = jax.nn.relu(second).astype(jnp.bfloat16)
    return jnp.einsum(
        "c,cfpqr->fpqr", out_weights[which], second, preferred_element_type=jnp.float32
    )


def extend_frames(block):
    return extended(block, (("tm", 0),), 1)


def shards(volume, lift_weights, lift_bias, mix_weights, out_weights, projector, measured):
    frames, zslab, width_x, width_y = volume.shape
    coarse = volume.astype(jnp.bfloat16)
    turned = jnp.transpose(coarse, (0, 1, 3, 2))
    yz_block = extend_frames(
        lax.all_to_all(coarse, "space", split_axis=2, concat_axis=1, tiled=True)
    )
    zx_block = extend_frames(
        lax.all_to_all(turned, "space", split_axis=2, concat_axis=1, tiled=True)
    )
    corr_yz = correction(yz_block, (3, 1), 1, lift_weights, lift_bias, mix_weights, out_weights)
    corr_zx = correction(zx_block, (1, 3), 2, lift_weights, lift_bias, mix_weights, out_weights)
    back_yz = lax.all_to_all(corr_yz, "space", split_axis=1, concat_axis=2, tiled=True)
    back_zx = jnp.transpose(
        lax.all_to_all(corr_zx, "space", split_axis=1, concat_axis=2, tiled=True), (0, 1, 3, 2)
    )
    corr_xy = correction(
        extend_frames(coarse), (2, 3), 0, lift_weights, lift_bias, mix_weights, out_weights
    )
    consensus = volume + (corr_xy + back_yz + back_zx) / 3.0
    flat = consensus.reshape(frames, zslab, width_x * width_y)
    regrouped = lax.all_to_all(flat, "tm", split_axis=2, concat_axis=0, tiled=True)
    pixels = regrouped.shape[2]
    rows = regrouped.reshape(-1, pixels)
    image = rows.astype(jnp.bfloat16)
    ray_count = measured.shape[2]
    measured_rows = measured.reshape(-1, ray_count)
    owned = lax.psum_scatter(
        jnp.dot(image, projector.T, preferred_element_type=jnp.float32),
        "tm",
        scatter_dimension=0,
        tiled=True,
    )
    misfit = (owned - measured_rows).astype(jnp.bfloat16)
    gradient = jnp.dot(
        lax.all_gather(misfit, "tm", axis=0, tiled=True),
        projector,
        preferred_element_type=jnp.float32,
    )
    return (rows - gradient).reshape(regrouped.shape)


def solution(mesh):
    placed = (
        P("tm", "space", None, None),
        P(),
        P(),
        P(),
        P(),
        P(None, "tm"),
        P("tm", "space", None),
    )
    return jax.shard_map(
        shards, mesh=mesh, in_specs=placed, out_specs=P(None, "space", "tm"), check_vma=False
    )
```

profile of v0, /device:TPU:41, one launch (start us, length us, event | category | flops | bytes accessed | tf_op | source)
XLA Modules:
  0.0 565.4 jit_solution(8941142086595586288)
XLA Ops:
  7.7 4.2 collective-permute-start
  11.9 1.9 collective-permute-start.1
  14.6 5.2 all-to-all-start
  21.6 3.1 all-to-all-done
  24.6 3.8 all-to-all-start.2
  29.3 5.3 collective-permute-start.2
  34.6 1.9 collective-permute-start.3
  36.6 3.6 collective-permute-start.4
  45.7 7.1 %maximum_convert_fusion.5 = bf16[4,128,128,64]{2,3,1,0:T(8,128)(2,1)} fusion(f32[64]{0:T(128)S(1)} %get-tuple-element.6, bf16[27,1,4,128,128]{4,3,2,1,0:T(8,128)(2,1)S(1)} %constant_dynamic-update-slice_fusion, bf16[3,64,27]{1,2,0:T(8,128)(2,1)S(1)} %copy-done.4), kind=kOutput, calls=%fused_computation.5 | convolution fusion | flops 239075328 | bytes 11936256 | tf_op jit(solution)/shard_map/ck,kfpqr->cfpqr/dot_general | solution.py:39
  55.6 6.6 %maximum_convert_fusion.3 = bf16[32,16,128,64]{2,3,1,0:T(8,128)(2,1)} fusion(f32[64]{0:T(128)S(1)} %get-tuple-element.5, bf16[27,1,32,16,128]{4,3,2,1,0:T(8,128)(2,1)S(1)} %constant_dynamic-update-slice_fusion.27, bf16[3,64,27]{1,2,0:T(8,128)(2,1)S(1)} %copy-done.4), kind=kOutput, calls=%fused_computation.3 | convolution fusion | flops 239075328 | bytes 11936256 | tf_op jit(solution)/shard_map/ck,kfpqr->cfpqr/dot_general | solution.py:39
  62.2 7.5 %fusion.3 = f32[1,32,16,128]{3,0,2,1:T(1,128)} fusion(bf16[32,16,128,64]{2,3,1,0:T(8,128)(2,1)} %maximum_convert_fusion.3, bf16[3,64,64]{2,1,0:T(8,128)(2,1)S(1)} %copy-done.3, bf16[3,64]{1,0:T(4,128)(2,1)S(1)} %copy-done.5), kind=kOutput, calls=%fused_computation.9 | convolution fusion | flops 553648128 | bytes 8667648 | tf_op jit(solution)/shard_map/c,cfpqr->fpqr/dot_general | solution.py:48
  69.7 5.4 all-to-all-start.1
  77.9 6.6 %maximum_convert_fusion.1 = bf16[32,16,128,64]{2,3,1,0:T(8,128)(2,1)} fusion(f32[64]{0:T(128)S(1)} %get-tuple-element.7, bf16[27,1,32,16,128]{4,3,2,1,0:T(8,128)(2,1)S(1)} %constant_dynamic-update-slice_fusion.54, bf16[3,64,27]{1,2,0:T(8,128)(2,1)S(1)} %copy-done.4), kind=kOutput, calls=%fused_computation.1 | convolution fusion | flops 239075328 | bytes 11936256 | tf_op jit(solution)/shard_map/ck,kfpqr->cfpqr/dot_general | solution.py:39
  84.5 7.5 %fusion = f32[1,32,16,128]{3,0,2,1:T(1,128)} fusion(bf16[32,16,128,64]{2,3,1,0:T(8,128)(2,1)} %maximum_convert_fusion.1, bf16[3,64,64]{2,1,0:T(8,128)(2,1)S(1)} %copy-done.3, bf16[3,64]{1,0:T(4,128)(2,1)S(1)} %copy-done.5), kind=kOutput, calls=%fused_computation.6 | convolution fusion | flops 553648128 | bytes 8667648 | tf_op jit(solution)/shard_map/c,cfpqr->fpqr/dot_general | solution.py:48
  92.0 5.1 all-to-all-start.3
  97.1 7.5 %fusion.6 = f32[1,4,128,128]{3,0,2,1:T(1,128)} fusion(bf16[4,128,128,64]{2,3,1,0:T(8,128)(2,1)} %maximum_convert_fusion.5, bf16[3,64,64]{2,1,0:T(8,128)(2,1)S(1)} %copy-done.3, bf16[3,64]{1,0:T(4,128)(2,1)S(1)} %copy-done.5), kind=kOutput, calls=%fused_computation.12 | convolution fusion | flops 553648128 | bytes 8667648 | tf_op jit(solution)/shard_map/c,cfpqr->fpqr/dot_general | solution.py:48
  105.8 12.3 %copy.2579 = f32[1,4,16384]{1,0,2:T(1,128)} copy(f32[1,4,16384]{2,0,1:T(1,128)S(1)} %bitcast.480) | data formatting | bytes 524288 | tf_op jit(solution)/shard_map/reshape | solution.py:77
  118.6 74.5 %reduce = f32[16384,4]{1,0:T(8,128)} reduce(f32[16384,1,4]{2,1,0:T(1,128)} %bitcast.470, f32[]{:T(128)} %broadcast.97), dimensions={1}, to_apply=%bitcast.462.reduce_sub_computation | reduce | bytes 524292
  193.1 8.5 %reshape.93 = f32[32,1,2048]{2,1,0:T(1,128)S(1)} reshape(f32[16384,4]{1,0:T(8,128)} %reduce) | data formatting | bytes 524288
  201.6 28.7 %all_to_all.87 = f32[32,1,2048]{2,1,0:T(1,128)S(1)} all-to-all(f32[32,1,2048]{2,1,0:T(1,128)S(1)} %reshape.93), channel_id=1, replica_groups=mesh['space'=8,'tm'=32] {'tm'}, dimensions={0} | all-to-all | bytes 524288 | tf_op jit(solution)/shard_map/all_to_all | solution.py:78
  231.5 14.8 %reshape.94 = f32[16384,1,4]{2,1,0:T(1,128)} reshape(f32[32,2048]{1,0:T(8,128)S(1)} %reduce.1) | data formatting | bytes 524288
  246.3 5.2 copy.2594
  254.9 257.7 %all-reduce.6.cloned.1.call-done = f32[128,2048]{1,0:T(8,128)} async-done(((f32[128,2048]{1,0:T(8,128)}), f32[128,2048]{1,0:T(8,128)}) %all-reduce.6.cloned.1.call-update) | async-done | bytes 1048592
  513.5 43.5 %all-gather = bf16[32,4,2048]{2,1,0:T(4,128)(2,1)S(1)} all-gather(bf16[1,4,2048]{2,1,0:T(4,128)(2,1)S(1)} %fusion.42), channel_id=1, replica_groups=mesh['space'=8,'tm'=32] {'tm'}, dimensions={0}, use_global_device_ids=true | all-gather | bytes 540672 | tf_op jit(solution)/shard_map/all_gather | solution.py:92
  (133 shorter events, 22.9 us)
Async XLA Ops:
  6.5 245.3 %copy-start = (bf16[2048,512]{1,0:T(8,128)(2,1)S(1)}, bf16[2048,512]{1,0:T(8,128)(2,1)}, u32[]{:S(2)}) copy-start(bf16[2048,512]{1,0:T(8,128)(2,1)} %param.12) | copy-start | bytes 6291460
  7.7 36.4 %copy-start.1 = (f32[1,4,128,128]{3,2,1,0:T(8,128)S(1)}, f32[1,4,128,128]{3,2,1,0:T(8,128)}, u32[]{:S(2)}) copy-start(f32[1,4,128,128]{3,2,1,0:T(8,128)} %param.7) | copy-start | bytes 786436
  7.7 32.5 %collective-permute-start = (bf16[1,4,128,128]{3,2,1,0:T(8,128)(2,1)S(1)}, bf16[1,4,128,128]{3,2,1,0:T(8,128)(2,1)S(1)}, u32[]{:S(2)}, u32[]{:S(2)}) collective-permute-start(bf16[1,4,128,128]{3,2,1,0:T(8,128)(2,1)S(1)} %convert_element_type.56), channel_id=1, source_target_pairs={{0,1},{1,2},{2,3},{3,4},{4,5},{5,6},{6,7},{7,8},{8,9},{9,10},{10,1... | collective-permute-start | bytes 393224 | tf_op jit(solution)/shard_map/ppermute | solution.py:14
  11.9 30.2 %collective-permute-start.1 = (bf16[1,4,128,128]{3,2,1,0:T(8,128)(2,1)S(1)}, bf16[1,4,128,128]{3,2,1,0:T(8,128)(2,1)S(1)}, u32[]{:S(2)}, u32[]{:S(2)}) collective-permute-start(bf16[1,4,128,128]{3,2,1,0:T(8,128)(2,1)S(1)} %convert_element_type.56), channel_id=1, source_target_pairs={{1,0},{2,1},{3,2},{4,3},{5,4},{6,5},{7,6},{8,7},{9,8},{10,9},{11,1... | collective-permute-start | bytes 393224 | tf_op jit(solution)/shard_map/ppermute | solution.py:15
  14.6 10.0 %all-to-all-start = ((bf16[1,4,128,128]{3,1,0,2:T(4,128)(2,1)}), bf16[1,4,128,128]{3,1,0,2:T(4,128)(2,1)S(1)}, u32[]{:S(2)}, u32[]{:S(2)}) async-start(bf16[1,4,128,128]{3,1,0,2:T(4,128)(2,1)} %copy.2566), calls=%async_computation | async-start | bytes 262144 | tf_op jit(solution)/shard_map/all_to_all | solution.py:62
  24.6 11.9 %all-to-all-start.2 = ((bf16[1,4,128,128]{3,1,0,2:T(4,128)(2,1)}), bf16[1,4,128,128]{3,1,0,2:T(4,128)(2,1)S(1)}, u32[]{:S(2)}, u32[]{:S(2)}) async-start(bf16[1,4,128,128]{3,1,0,2:T(4,128)(2,1)} %copy.2572), calls=%async_computation.2 | async-start | bytes 262144 | tf_op jit(solution)/shard_map/all_to_all | solution.py:65
  29.3 23.6 %collective-permute-start.2 = (bf16[1,32,16,128]{3,2,1,0:T(8,128)(2,1)S(1)}, bf16[1,32,16,128]{3,2,1,0:T(8,128)(2,1)S(1)}, u32[]{:S(2)}, u32[]{:S(2)}) collective-permute-start(bf16[1,32,16,128]{3,2,1,0:T(8,128)(2,1)S(1)} %bitcast.476), channel_id=1, source_target_pairs={{0,1},{1,2},{2,3},{3,4},{4,5},{5,6},{6,7},{7,8},{8,9},{9,10},{10,1... | collective-permute-start | bytes 393224 | tf_op jit(solution)/shard_map/ppermute | solution.py:14
  34.6 18.3 %collective-permute-start.3 = (bf16[1,32,16,128]{3,2,1,0:T(8,128)(2,1)S(1)}, bf16[1,32,16,128]{3,2,1,0:T(8,128)(2,1)S(1)}, u32[]{:S(2)}, u32[]{:S(2)}) collective-permute-start(bf16[1,32,16,128]{3,2,1,0:T(8,128)(2,1)S(1)} %bitcast.477), channel_id=1, source_target_pairs={{1,0},{2,1},{3,2},{4,3},{5,4},{6,5},{7,6},{8,7},{9,8},{10,9},{11,1... | collective-permute-start | bytes 393224 | tf_op jit(solution)/shard_map/ppermute | solution.py:15
  36.6 38.5 %collective-permute-start.4 = (bf16[1,32,16,128]{3,2,1,0:T(8,128)(2,1)S(1)}, bf16[1,32,16,128]{3,2,1,0:T(8,128)(2,1)S(1)}, u32[]{:S(2)}, u32[]{:S(2)}) collective-permute-start(bf16[1,32,16,128]{3,2,1,0:T(8,128)(2,1)S(1)} %bitcast.472), channel_id=1, source_target_pairs={{0,1},{1,2},{2,3},{3,4},{4,5},{5,6},{6,7},{7,8},{8,9},{9,10},{10,1... | collective-permute-start | bytes 393224 | tf_op jit(solution)/shard_map/ppermute | solution.py:14
  40.2 34.9 %collective-permute-start.5 = (bf16[1,32,16,128]{3,2,1,0:T(8,128)(2,1)S(1)}, bf16[1,32,16,128]{3,2,1,0:T(8,128)(2,1)S(1)}, u32[]{:S(2)}, u32[]{:S(2)}) collective-permute-start(bf16[1,32,16,128]{3,2,1,0:T(8,128)(2,1)S(1)} %bitcast.473), channel_id=1, source_target_pairs={{1,0},{2,1},{3,2},{4,3},{5,4},{6,5},{7,6},{8,7},{9,8},{10,9},{11,1... | collective-permute-start | bytes 393224 | tf_op jit(solution)/shard_map/ppermute | solution.py:15
  42.8 2.9 copy-start.4
  55.6 6.7 %copy-start.3 = (bf16[3,64,64]{2,1,0:T(8,128)(2,1)S(1)}, bf16[3,64,64]{2,1,0:T(8,128)(2,1)}, u32[]{:S(2)}) copy-start(bf16[3,64,64]{2,1,0:T(8,128)(2,1)} %param.10) | copy-start | bytes 73732
  55.6 6.6 %copy-start.5 = (bf16[3,64]{1,0:T(4,128)(2,1)S(1)}, bf16[3,64]{1,0:T(4,128)(2,1)}, u32[]{:S(2)}) copy-start(bf16[3,64]{1,0:T(4,128)(2,1)} %param.11) | copy-start | bytes 1156
  69.7 22.3 %all-to-all-start.1 = ((f32[1,32,16,128]{3,2,0,1:T(8,128)}), f32[1,32,16,128]{3,2,0,1:T(8,128)S(1)}, u32[]{:S(2)}, u32[]{:S(2)}) async-start(f32[1,32,16,128]{3,2,0,1:T(8,128)} %bitcast.88), calls=%async_computation.1 | async-start | bytes 524288 | tf_op jit(solution)/shard_map/all_to_all | solution.py:69
  92.0 12.7 %all-to-all-start.3 = ((f32[1,32,16,128]{3,2,0,1:T(8,128)}), f32[1,32,16,128]{3,2,0,1:T(8,128)S(1)}, u32[]{:S(2)}, u32[]{:S(2)}) async-start(f32[1,32,16,128]{3,2,0,1:T(8,128)} %bitcast.140), calls=%async_computation.3 | async-start | bytes 524288 | tf_op jit(solution)/shard_map/all_to_all | solution.py:71
  97.1 415.5 %all-reduce.6.cloned.1.call-start = ((), (), s32[]{:S(2)}) async-start(), calls=%async_computation.5 | async-start | bytes 2097152
  251.5 2.1 copy-start.6
  251.5 261.1 %copy-start.2 = (f32[1,4,2048]{2,1,0:T(4,128)S(1)}, f32[1,4,2048]{2,1,0:T(4,128)}, u32[]{:S(2)}) copy-start(f32[1,4,2048]{2,1,0:T(4,128)} %param.13) | copy-start | bytes 98308
Sparse Core Ops, SparseCore 0:
  253.8 258.8 all-reduce.5
where the time goes:
time: 572 us; the launch traced here: 565 us
  waiting for transfers between devices  261 us (46%)
  other arithmetic  81.1 us (14%)
  blocking collectives  72.1 us (13%)
  local copies, waits for them, and re-layouts  52.8 us (9%)
  matrix products  45.1 us (8%)
  starting transfers between devices  38.4 us (7%)
  between operations  15 us (3%)
    unnamed x2, waiting for transfers between devices  258 us
    unnamed x3, other arithmetic  75.4 us
    all_gather x1, blocking collectives, shards(): lax.all_gather(misfit, 'tm', axis=0, tiled=True)  43.5 us
    unnamed x96, local copies, waits for them, and re-layouts  31.3 us
    all_to_all x1, blocking collectives, shards(): lax.all_to_all(flat, 'tm', split_axis=2, concat_axis=0, tiled=True)  28.7 us
    dot_general x3, matrix products, correction(): jnp.einsum('c,cfpqr->fpqr', out_weights[which], second, preferred_element...  22.4 us
    dot_general x3, matrix products, correction(): jnp.einsum('ck,kfpqr->cfpqr', lift_weights[which], taps, preferred_elemen...  20.4 us
    ppermute x3, starting transfers between devices, extended(): before = lax.ppermute(last, axis, up)  13.2 us
  transfers between devices with their start and end apart: 11, of which 2 were waited for; matrix products, arithmetic and copies ran while one was open for 10% of the time, Pallas kernels for 0%

commit v1 on v0

v1 whole, which is shorter than its diff:
```python
import functools

import jax
import jax.numpy as jnp
from jax import lax
from jax.experimental import pallas as pl
from jax.experimental.pallas import tpu as pltpu
from jax.sharding import Mesh, PartitionSpec as P

F32, BF16 = jnp.float32, jnp.bfloat16
VM = pl.BlockSpec(memory_space=pltpu.VMEM)
SM = pl.BlockSpec(memory_space=pltpu.SMEM)
SWAP = [(0, 1), (1, 0)]


def call(kernel, outs, scratch=(), specs=None, flops=0, nbytes=0, vmem=40):
    return pl.pallas_call(
        kernel,
        out_shape=outs,
        in_specs=specs,
        out_specs=jax.tree.map(lambda _: VM, outs),
        scratch_shapes=list(scratch),
        compiler_params=pltpu.CompilerParams(vmem_limit_bytes=vmem << 20),
        cost_estimate=pl.CostEstimate(flops=flops, bytes_accessed=nbytes, transcendentals=0),
    )


def shaped(shape, dtype):
    return jax.ShapeDtypeStruct(shape, dtype)


def iota(shape, dim):
    return lax.broadcasted_iota(jnp.int32, shape, dim)


def weights_kernel(lift, mix, outw, a1, a2, a3):
    spread = (iota((256, 64), 0) >> 2 == iota((256, 64), 1)).astype(F32).astype(BF16)
    spread_t = (iota((64, 256), 1) >> 2 == iota((64, 256), 0)).astype(F32).astype(BF16)
    taps = (iota((32, 256), 1) >> 3 == iota((32, 256), 0)).astype(F32).astype(BF16)
    row, col = iota((256, 256), 0) & 3, iota((256, 256), 1)
    part = iota((64, 32), 1)
    for k in range(3):
        full = lift[k]
        high = full.astype(BF16).astype(F32)
        mid = (full - high).astype(BF16).astype(F32)
        low = full - high - mid
        split = jnp.where(part == 28, mid, jnp.where(part == 29, low, high)).astype(BF16)
        base = jnp.dot(spread, split, preferred_element_type=F32).astype(BF16)
        base = jnp.dot(base, taps, preferred_element_type=F32)
        for half in range(2):
            a1[k, half * 256 : half * 256 + 256] = jnp.where(
                row + 4 * half == (col & 7), base, 0.0
            ).astype(BF16)
        mixed = jnp.dot(spread, mix[k], preferred_element_type=F32).astype(BF16)
        mixed = jnp.dot(mixed, spread_t, preferred_element_type=F32)
        a2[k] = jnp.where(row == (col & 3), mixed, 0.0).astype(BF16)
        a3[k] = jnp.dot(spread, outw[k], preferred_element_type=F32)


def pack_kernel(vol, out):
    zero = jnp.zeros((1, 128), F32)
    for p in range(32):
        for z in range(4):
            lo, hi = max(4 * p - 1, 0), min(4 * p + 5, 128)
            at = z * 6 + lo - (4 * p - 1)
            out[p, at : at + hi - lo] = vol[z, lo:hi]
            if p == 0:
                out[p, z * 6 : z * 6 + 1] = zero
            if p == 31:
                out[p, z * 6 + 5 : z * 6 + 6] = zero


def turn_kernel(rows, vol, first, last):
    zero = jnp.zeros((8, 128), F32)
    for r in range(24):
        x = rows[pl.ds(r, 32, stride=24), :]
        vol[r, 0:8] = zero
        vol[r, 8:40] = x
        vol[r, 40:48] = zero
        if r < 6:
            first[r] = x.astype(BF16)
        if r >= 18:
            last[r - 18] = x.astype(BF16)


def spread_y(s, pos, v):
    lane = iota(v.shape, 1)
    s[0, pos] = jnp.where(lane == 0, 0.0, pltpu.roll(v, 1, 1))
    s[1, pos] = v
    s[2, pos] = jnp.where(lane == 127, 0.0, pltpu.roll(v, 127, 1))


OFFSETS = (
    [(dt, db, da - 1) for dt in range(3) for da in range(3) for db in range(3)],
    [(dt, da, 6 * (db - 1)) for dt in range(3) for da in range(3) for db in range(3)],
    [(dt, 1, 6 * (da - 1) + db - 1) for dt in range(3) for da in range(3) for db in range(3)],
)


def corrected(s, a1, a2, a3, which, weight, pos, block):
    rows = []
    for dt, dy, step in OFFSETS[which]:
        at = pl.ds(7 + dt + 8 * block, 8)
        rows.append(
            jnp.concatenate([s[dy, pos + step, at, :], s[dy, pos + step + 1, at, :]], axis=1)
        )
    rows.append(jnp.ones((24, 256), F32))
    rows.append(jnp.zeros((16, 256), F32))
    taps = jnp.concatenate(rows, axis=0).astype(BF16)
    first = jnp.dot(a1[weight], taps, preferred_element_type=F32)
    first = jnp.maximum(first, 0.0).astype(BF16)
    w = a3[weight]
    w = jnp.concatenate([w, w], axis=1)
    sums = []
    for half in range(2):
        second = jnp.dot(
            a2[weight], first[half * 256 : half * 256 + 256], preferred_element_type=F32
        )
        second = jnp.maximum(second, 0.0) * w
        total = jnp.sum(second.reshape(32, 8, 256), axis=0)
        sums.append(total + pltpu.roll(total, 4, 0))
    return jnp.where(iota((8, 256), 0) < 4, sums[0], sums[1])


def xy_kernel(vol, a1, a2, a3, out, s):
    def fill(r, carry):
        spread_y(s, r + 6, vol[r])
        return carry

    lax.fori_loop(0, 24, fill, 0)

    def step(i, carry):
        z, x = i // 2, 2 * (i % 2)
        pos = (z + 1) * 6 + 1 + x
        for block in range(4):
            got = corrected(s, a1, a2, a3, 0, 0, pos, block)
            out[z * 4 + x, 8 * block : 8 * block + 8] = got[:, :128]
            out[z * 4 + x + 1, 8 * block : 8 * block + 8] = got[:, 128:]
        return carry

    lax.fori_loop(0, 8, step, 0)


def rest_kernel(core, vol, before, after, xy, a1, a2, a3, cons, mine, other, s):
    def fill(r, carry):
        spread_y(s, r + 6, vol[r])
        return carry

    lax.fori_loop(0, 24, fill, 0)
    edge = jnp.zeros((8, 128), F32)

    def fill_edge(r, carry):
        spread_y(s, r, jnp.concatenate([edge, before[r].astype(F32), edge], axis=0))
        spread_y(s, r + 30, jnp.concatenate([edge, after[r].astype(F32), edge], axis=0))
        return carry

    lax.fori_loop(0, 6, fill_edge, 0)

    def step(i, carry):
        z, x = i // 2, 2 * (i % 2)
        pos = (z + 1) * 6 + 1 + x
        for block in range(4):
            at = slice(8 * block, 8 * block + 8)
            got = corrected(s, a1, a2, a3, 1, 1, pos, block)
            got = got + corrected(s, a1, a2, a3, 2, 2, pos, block)
            for j in range(2):
                total = xy[z * 4 + x + j, at] + got[:, 128 * j : 128 * j + 128]
                here = vol[pos - 6 + j, 8 + 8 * block : 16 + 8 * block]
                cons[z * 4 + x + j, at] = here + total / 3.0
        return carry

    lax.fori_loop(0, 8, step, 0)
    c = core[0]
    for z in range(4):
        for x in range(4):
            at = (slice(16 * z, 16 * z + 16), slice(128 * x, 128 * x + 128))
            even = cons[z * 4 + x, pl.ds(0, 16, stride=2), :].astype(BF16)
            odd = cons[z * 4 + x, pl.ds(1, 16, stride=2), :].astype(BF16)

            @pl.when(c == 0)
            def _():
                mine[at] = even
                other[at] = odd

            @pl.when(c == 1)
            def _():
                mine[at] = odd
                other[at] = even


NT = (((1,), (1,)), ((), ()))


def project_kernel(mine, theirs, own, pair, out, turned):
    for j in range(8):
        rays = slice(256 * j, 256 * j + 256)
        got = lax.dot_general(mine[...], own[rays], NT, preferred_element_type=F32)
        got = got + lax.dot_general(theirs[...], pair[rays], NT, preferred_element_type=F32)
        for z in range(4):
            for n in range(2):
                turned[2 * (j % 4) + n, pl.ds(z * 2 + j // 4, 16, stride=8), :] = got[
                    16 * z : 16 * z + 16, 128 * n : 128 * n + 128
                ]
    for n in range(8):
        lanes = slice(128 * n, 128 * n + 128)
        for t in range(16):
            out[t, :, lanes] = turned[n, 8 * t : 8 * t + 8].astype(BF16)


def misfit_kernel(parts, measured, out):
    total = parts[0].astype(F32)
    for t in range(1, 16):
        total = total + parts[t].astype(F32)
    misfit = (total - measured[...]).astype(BF16)
    for t in range(16):
        out[t] = misfit


def gradient_kernel(misfit, own, pair, near, far, turned, rows):
    for n in range(8):
        for t in range(16):
            turned[n, 8 * t : 8 * t + 8] = misfit[t, :, 128 * n : 128 * n + 128].astype(F32)
    for z in range(4):
        for half in range(2):
            for n in range(8):
                rows[16 * z : 16 * z + 16, 1024 * half + 128 * n : 1024 * half + 128 * n + 128] = (
                    turned[n, pl.ds(z * 2 + half, 16, stride=8), :].astype(BF16)
                )
    left = rows[...]
    far[...] = jnp.dot(left, pair[...], preferred_element_type=F32)
    near[...] = jnp.dot(left, own[...], preferred_element_type=F32)


def update_kernel(core, cons, near, far, out, turned):
    def write(parity, gradient):
        for z in range(4):
            for x in range(4):
                lanes = slice(128 * x, 128 * x + 128)
                old = cons[z * 4 + x, pl.ds(parity, 16, stride=2), :]
                turned[x, pl.ds(4 * parity + z, 16, stride=8), :] = (
                    old - gradient[16 * z : 16 * z + 16, lanes]
                )

    @pl.when(core[0] == 0)
    def _():
        write(0, near)
        write(1, far)

    @pl.when(core[0] == 1)
    def _():
        write(1, near)
        write(0, far)

    for x in range(4):
        out[:, 128 * x : 128 * x + 128] = turned[x]


def shards(volume, lift_weights, lift_bias, mix_weights, out_weights, projector, measured):
    core = lax.axis_index("c").reshape(1)
    pair = lax.ppermute(projector, "c", SWAP)

    packed = call(pack_kernel, shaped((32, 24, 128), F32), specs=[VM], nbytes=1 << 20)(volume[0])
    frames = lax.all_to_all(packed, ("q", "c"), split_axis=0, concat_axis=0, tiled=True)

    bias = jnp.broadcast_to(lift_bias[:, :, None], (3, 64, 3))
    lift = jnp.concatenate(
        [lift_weights.astype(F32), bias, jnp.zeros((3, 64, 2), F32)], axis=2
    )
    outw = jnp.broadcast_to(out_weights[:, :, None], (3, 64, 128))
    a1, a2, a3 = call(
        weights_kernel,
        (shaped((3, 512, 256), BF16), shaped((3, 256, 256), BF16), shaped((3, 256, 128), F32)),
        specs=[VM] * 3,
        flops=10**8,
        nbytes=1 << 20,
    )(lift, mix_weights, outw)

    vol, first, last = call(
        turn_kernel,
        (shaped((24, 48, 128), F32), shaped((6, 32, 128), BF16), shaped((6, 32, 128), BF16)),
        specs=[VM],
        nbytes=1 << 20,
    )(frames.reshape(768, 128))
    up = [(i, i + 1) for i in range(7)]
    before = lax.ppermute(last, "space", up)
    after = lax.ppermute(first, "space", [(j, i) for i, j in up])

    spread = pltpu.VMEM((3, 36, 48, 128), F32)
    xy = call(
        xy_kernel, shaped((16, 32, 128), F32), [spread], [VM] * 4, flops=12 * 10**9, nbytes=1 << 20
    )(vol, a1, a2, a3)
    cons, mine, other = call(
        rest_kernel,
        (shaped((16, 32, 128), F32), shaped((64, 512), BF16), shaped((64, 512), BF16)),
        [spread],
        [SM] + [VM] * 7,
        flops=24 * 10**9,
        nbytes=1 << 20,
    )(core, vol, before, after, xy, a1, a2, a3)

    theirs = lax.ppermute(other, "c", SWAP)
    partial = call(
        project_kernel,
        shaped((16, 8, 1024), BF16),
        [pltpu.VMEM((8, 128, 128), F32)],
        [VM] * 4,
        flops=3 * 10**8,
        nbytes=5 << 20,
    )(mine, theirs, projector, pair)
    parts = lax.all_to_all(partial, "q", split_axis=0, concat_axis=0, tiled=True)
    misfit = call(misfit_kernel, shaped((16, 8, 1024), BF16), specs=[VM] * 2)(
        parts, measured.reshape(8, 1024)
    )
    misfit = lax.all_to_all(misfit, "q", split_axis=0, concat_axis=0, tiled=True)
    near, far = call(
        gradient_kernel,
        (shaped((64, 512), F32), shaped((64, 512), F32)),
        [pltpu.VMEM((8, 128, 128), F32), pltpu.VMEM((64, 2048), BF16)],
        [VM] * 3,
        flops=3 * 10**8,
        nbytes=5 << 20,
    )(misfit, projector, pair)
    far = lax.ppermute(far, "c", SWAP)
    updated = call(
        update_kernel,
        shaped((128, 512), F32),
        [pltpu.VMEM((4, 128, 128), F32)],
        [SM] + [VM] * 3,
    )(core, cons, near, far)
    return updated.reshape(32, 4, 512)


def solution(mesh):
    fine = Mesh(mesh.devices.reshape(8, 16, 2), ("space", "q", "c"))
    tm = ("q", "c")
    placed = (
        P(tm, "space", None, None),
        P(),
        P(),
        P(),
        P(),
        P(None, tm),
        P(tm, "space", None),
    )
    return jax.shard_map(
        shards, mesh=fine, in_specs=placed, out_specs=P(None, "space", tm), check_vma=False
    )
```

time: 572 us -> 105 us (0.18)
  the two profiles are of different devices: /device:TPU:41 before, /device:TPU:37 now
where the time goes in v1:
time: 105 us
  Pallas kernels  31.4 us (30%)
  starting transfers between devices  27.2 us (26%)
  waiting for transfers between devices  23.6 us (22%)
  blocking collectives  15.1 us (14%)
  local copies, waits for them, and re-layouts  6.98 us (7%)
    all_to_all x1, blocking collectives, shards(): lax.all_to_all(misfit, 'q', split_axis=0, concat_axis=0, tiled=True)  15.1 us
    pallas_call x1, Pallas kernels, shards(): call(rest_kernel, (shaped((16, 32, 128), F32), shaped((64, 512), BF16), s...  14.3 us
    all_to_all x1, starting transfers between devices, shards(): lax.all_to_all(packed, ('q', 'c'), split_axis=0, concat_axis=0, tiled=True)  11.7 us
    all_to_all x1, waiting for transfers between devices, shards(): lax.all_to_all(partial, 'q', split_axis=0, concat_axis=0, tiled=True)  11 us
    all_to_all x1, waiting for transfers between devices, shards(): lax.all_to_all(packed, ('q', 'c'), split_axis=0, concat_axis=0, tiled=True)  10.7 us
    pallas_call x1, Pallas kernels, shards(): call(xy_kernel, shaped((16, 32, 128), F32), [spread], [VM] * 4, flops=12...  9.07 us
    all_to_all x1, starting transfers between devices, shards(): lax.all_to_all(partial, 'q', split_axis=0, concat_axis=0, tiled=True)  4.22 us
    ppermute x1, starting transfers between devices, shards(): after = lax.ppermute(first, 'space', [(j, i) for i, j in up])  3.88 us
  transfers between devices with their start and end apart: 7, of which 4 were waited for; matrix products, arithmetic and copies ran while one was open for 2% of the time, Pallas kernels for 23%

profile of v1, /device:TPU:37, one launch (start us, length us, event | category | flops | bytes accessed | tf_op | source)
XLA Modules:
  0.0 104.6 jit_solution(13578279749225864508)
XLA Ops:
  0.0 0.9 copy-done.1
  1.0 0.8 shard_map.73
  1.8 11.7 %all-to-all-start = ((f32[32,24,128]{2,1,0:T(8,128)}), f32[32,24,128]{2,1,0:T(8,128)S(1)}, u32[]{:S(2)}, u32[]{:S(2)}) async-start(f32[32,24,128]{2,1,0:T(8,128)} %shard_map.73), calls=%async_computation | async-start | bytes 786432 | tf_op jit(solution)/shard_map/all_to_all | solution.py:263
  13.9 0.8 copy.9
  15.7 0.8 broadcast_in_dim.8.outw
  16.5 0.8 copy-done.2
  17.3 0.8 shard_map.75
  18.1 10.7 %all-to-all-done = f32[32,24,128]{2,1,0:T(8,128)S(1)} async-done(((f32[32,24,128]{2,1,0:T(8,128)}), f32[32,24,128]{2,1,0:T(8,128)S(1)}, u32[]{:S(2)}, u32[]{:S(2)}) %all-to-all-start) | async-done | bytes 393248 | tf_op jit(solution)/shard_map/all_to_all | solution.py:263
  28.9 2.3 %collective-permute-start = (bf16[6,32,128]{2,1,0:T(8,128)(2,1)S(1)}, bf16[6,32,128]{2,1,0:T(8,128)(2,1)S(1)}, u32[]{:S(2)}, u32[]{:S(2)}) collective-permute-start(bf16[6,32,128]{2,1,0:T(8,128)(2,1)S(1)} %get-tuple-element.17), channel_id=1, source_target_pairs={{0,32},{32,64},{64,96},{96,128},{128,160},{160,192},{192,224},{1,3... | collective-permute-start | bytes 147464 | tf_op jit(solution)/shard_map/ppermute | solution.py:285
  31.2 3.9 %collective-permute-start.1 = (bf16[6,32,128]{2,1,0:T(8,128)(2,1)S(1)}, bf16[6,32,128]{2,1,0:T(8,128)(2,1)S(1)}, u32[]{:S(2)}, u32[]{:S(2)}) collective-permute-start(bf16[6,32,128]{2,1,0:T(8,128)(2,1)S(1)} %get-tuple-element.18), channel_id=1, source_target_pairs={{32,0},{64,32},{96,64},{128,96},{160,128},{192,160},{224,192},{33,... | collective-permute-start | bytes 147464 | tf_op jit(solution)/shard_map/ppermute | solution.py:286
  35.1 9.1 %shard_map.76.xy = f32[16,32,128]{2,1,0:T(8,128)S(1)} custom-call(f32[24,48,128]{2,1,0:T(8,128)S(1)} %get-tuple-element.16.vol, bf16[3,512,256]{2,1,0:T(8,128)(2,1)S(1)} %get-tuple-element.19.a1, bf16[3,256,256]{2,1,0:T(8,128)(2,1)S(1)} %get-tuple-element.20.a2, f32[3,256,128]{2,1,0:T(8,128)S(1)} %get-tuple-element.21.a3), custom_call_target="tpu_custom_call" | custom-call | flops 12000000000 | bytes 1048576 | tf_op jit(solution)/shard_map/pallas_call | solution.py:289
  44.2 1.0 copy-done.4
  45.2 1.0 copy-done.6
  46.2 14.3 %shard_map.77 = (f32[16,32,128]{2,1,0:T(8,128)S(1)}, bf16[64,512]{1,0:T(8,128)(2,1)S(1)}, bf16[64,512]{1,0:T(8,128)(2,1)S(1)}) custom-call(s32[1]{0:T(128)} %bitcast.core, f32[24,48,128]{2,1,0:T(8,128)S(1)} %get-tuple-element.16.vol, bf16[6,32,128]{2,1,0:T(8,128)(2,1)S(1)} %collective-permute-done.before, ...), custom_call_target="tpu_custom_call" | custom-call | flops 24000000000 | bytes 1048576 | tf_op jit(solution)/shard_map/pallas_call | solution.py:292
  60.5 2.1 %collective-permute-start.2 = (bf16[64,512]{1,0:T(8,128)(2,1)S(1)}, bf16[64,512]{1,0:T(8,128)(2,1)S(1)}, u32[]{:S(2)}, u32[]{:S(2)}) collective-permute-start(bf16[64,512]{1,0:T(8,128)(2,1)S(1)} %get-tuple-element.24), channel_id=1, source_target_pairs={{0,1},{1,0},{2,3},{3,2},{4,5},{5,4},{6,7},{7,6},{8,9},{9,8},{10,11... | collective-permute-start | bytes 196616 | tf_op jit(solution)/shard_map/ppermute | solution.py:301
  62.6 0.9 collective-permute-done.2.theirs
  63.5 3.7 %shard_map.78 = bf16[16,8,1024]{2,1,0:T(8,128)(2,1)} custom-call(bf16[64,512]{1,0:T(8,128)(2,1)S(1)} %get-tuple-element.23.mine, bf16[64,512]{1,0:T(8,128)(2,1)S(1)} %collective-permute-done.2.theirs, bf16[2048,512]{1,0:T(8,128)(2,1)S(1)} %copy-done, bf16[2048,512]{1,0:T(8,128)(2,1)} %collective-permute-done.3.pair), custom_call_target="tpu_custom_call" | custom-call | flops 300000000 | bytes 5242880 | tf_op jit(solution)/shard_map/pallas_call | solution.py:302
  67.2 4.2 %all-to-all-start.1 = ((bf16[16,8,1024]{2,1,0:T(8,128)(2,1)}), bf16[16,8,1024]{2,1,0:T(8,128)(2,1)S(1)}, u32[]{:S(2)}, u32[]{:S(2)}) async-start(bf16[16,8,1024]{2,1,0:T(8,128)(2,1)} %shard_map.78), calls=%async_computation.1 | async-start | bytes 524288 | tf_op jit(solution)/shard_map/all_to_all | solution.py:310
  71.5 11.0 %all-to-all-done.1.parts = bf16[16,8,1024]{2,1,0:T(8,128)(2,1)S(1)} async-done(((bf16[16,8,1024]{2,1,0:T(8,128)(2,1)}), bf16[16,8,1024]{2,1,0:T(8,128)(2,1)S(1)}, u32[]{:S(2)}, u32[]{:S(2)}) %all-to-all-start.1) | async-done | bytes 262176 | tf_op jit(solution)/shard_map/all_to_all | solution.py:310
  82.5 15.1 %all_to_all.15.misfit = bf16[16,8,1024]{2,1,0:T(8,128)(2,1)S(1)} all-to-all(bf16[16,8,1024]{2,1,0:T(8,128)(2,1)S(1)} %shard_map.79), channel_id=1, replica_groups=mesh['space'=8,'q'=16,'c'=2] {'q'}, dimensions={0} | all-to-all | bytes 524288 | tf_op jit(solution)/shard_map/all_to_all | solution.py:314
  97.7 2.4 %shard_map.80 = (f32[64,512]{1,0:T(8,128)S(1)}, f32[64,512]{1,0:T(8,128)S(1)}) custom-call(bf16[16,8,1024]{2,1,0:T(8,128)(2,1)S(1)} %all_to_all.15.misfit, bf16[2048,512]{1,0:T(8,128)(2,1)S(1)} %copy-done, bf16[2048,512]{1,0:T(8,128)(2,1)} %collective-permute-done.3.pair), custom_call_target="tpu_custom_call" | custom-call | flops 300000000 | bytes 5242880 | tf_op jit(solution)/shard_map/pallas_call | solution.py:315
  100.1 2.6 %collective-permute-start.4 = (f32[64,512]{1,0:T(8,128)S(1)}, f32[64,512]{1,0:T(8,128)S(1)}, u32[]{:S(2)}, u32[]{:S(2)}) collective-permute-start(f32[64,512]{1,0:T(8,128)S(1)} %get-tuple-element.26), channel_id=1, source_target_pairs={{0,1},{1,0},{2,3},{3,2},{4,5},{5,4},{6,7},{7,6},{8,9},{9,8},{10,11... | collective-permute-start | bytes 393224 | tf_op jit(solution)/shard_map/ppermute | solution.py:323
  102.7 1.0 collective-permute-done.4.far
  103.8 0.8 reshape.17
  (24 shorter events, 1.6 us)
Async XLA Ops:
  0.0 0.9 copy-start.1
  1.8 27.1 %all-to-all-start = ((f32[32,24,128]{2,1,0:T(8,128)}), f32[32,24,128]{2,1,0:T(8,128)S(1)}, u32[]{:S(2)}, u32[]{:S(2)}) async-start(f32[32,24,128]{2,1,0:T(8,128)} %shard_map.73), calls=%async_computation | async-start | bytes 786432 | tf_op jit(solution)/shard_map/all_to_all | solution.py:263
  13.4 50.1 %collective-permute-start.3 = (bf16[2048,512]{1,0:T(8,128)(2,1)}, bf16[2048,512]{1,0:T(8,128)(2,1)}, u32[]{:S(2)}, u32[]{:S(2)}) collective-permute-start(bf16[2048,512]{1,0:T(8,128)(2,1)} %own.3), channel_id=1, source_target_pairs={{0,1},{1,0},{2,3},{3,2},{4,5},{5,4},{6,7},{7,6},{8,9},{9,8},{10,11... | collective-permute-start | bytes 6291464 | tf_op jit(solution)/shard_map/ppermute | solution.py:260
  16.5 0.8 copy-start.2
  18.1 26.1 %copy-start.3 = (bf16[3,256,256]{2,1,0:T(8,128)(2,1)}, bf16[3,256,256]{2,1,0:T(8,128)(2,1)S(1)}, u32[]{:S(2)}) copy-start(bf16[3,256,256]{2,1,0:T(8,128)(2,1)S(1)} %get-tuple-element.20.a2) | copy-start | bytes 1179652
  18.1 26.1 %copy-start.5 = (f32[3,256,128]{2,1,0:T(8,128)}, f32[3,256,128]{2,1,0:T(8,128)S(1)}, u32[]{:S(2)}) copy-start(f32[3,256,128]{2,1,0:T(8,128)S(1)} %get-tuple-element.21.a3) | copy-start | bytes 1179652
  28.9 15.3 %collective-permute-start = (bf16[6,32,128]{2,1,0:T(8,128)(2,1)S(1)}, bf16[6,32,128]{2,1,0:T(8,128)(2,1)S(1)}, u32[]{:S(2)}, u32[]{:S(2)}) collective-permute-start(bf16[6,32,128]{2,1,0:T(8,128)(2,1)S(1)} %get-tuple-element.17), channel_id=1, source_target_pairs={{0,32},{32,64},{64,96},{96,128},{128,160},{160,192},{192,224},{1,3... | collective-permute-start | bytes 147464 | tf_op jit(solution)/shard_map/ppermute | solution.py:285
  31.2 13.0 %collective-permute-start.1 = (bf16[6,32,128]{2,1,0:T(8,128)(2,1)S(1)}, bf16[6,32,128]{2,1,0:T(8,128)(2,1)S(1)}, u32[]{:S(2)}, u32[]{:S(2)}) collective-permute-start(bf16[6,32,128]{2,1,0:T(8,128)(2,1)S(1)} %get-tuple-element.18), channel_id=1, source_target_pairs={{32,0},{64,32},{96,64},{128,96},{160,128},{192,160},{224,192},{33,... | collective-permute-start | bytes 147464 | tf_op jit(solution)/shard_map/ppermute | solution.py:286
  44.2 1.0 copy-start.4
  45.2 1.0 copy-start.6
  46.2 17.3 %copy-start = (bf16[2048,512]{1,0:T(8,128)(2,1)S(1)}, bf16[2048,512]{1,0:T(8,128)(2,1)}, u32[]{:S(2)}) copy-start(bf16[2048,512]{1,0:T(8,128)(2,1)} %own.3) | copy-start | bytes 6291460
  60.5 3.0 %collective-permute-start.2 = (bf16[64,512]{1,0:T(8,128)(2,1)S(1)}, bf16[64,512]{1,0:T(8,128)(2,1)S(1)}, u32[]{:S(2)}, u32[]{:S(2)}) collective-permute-start(bf16[64,512]{1,0:T(8,128)(2,1)S(1)} %get-tuple-element.24), channel_id=1, source_target_pairs={{0,1},{1,0},{2,3},{3,2},{4,5},{5,4},{6,7},{7,6},{8,9},{9,8},{10,11... | collective-permute-start | bytes 196616 | tf_op jit(solution)/shard_map/ppermute | solution.py:301
  63.5 8.0 %copy-start.7 = (f32[1,4,2048]{2,1,0:T(4,128)S(1)}, f32[1,4,2048]{2,1,0:T(4,128)}, u32[]{:S(2)}) copy-start(f32[1,4,2048]{2,1,0:T(4,128)} %param.13) | copy-start | bytes 98308
  67.2 15.2 %all-to-all-start.1 = ((bf16[16,8,1024]{2,1,0:T(8,128)(2,1)}), bf16[16,8,1024]{2,1,0:T(8,128)(2,1)S(1)}, u32[]{:S(2)}, u32[]{:S(2)}) async-start(bf16[16,8,1024]{2,1,0:T(8,128)(2,1)} %shard_map.78), calls=%async_computation.1 | async-start | bytes 524288 | tf_op jit(solution)/shard_map/all_to_all | solution.py:310
  100.1 3.6 %collective-permute-start.4 = (f32[64,512]{1,0:T(8,128)S(1)}, f32[64,512]{1,0:T(8,128)S(1)}, u32[]{:S(2)}, u32[]{:S(2)}) collective-permute-start(f32[64,512]{1,0:T(8,128)S(1)} %get-tuple-element.26), channel_id=1, source_target_pairs={{0,1},{1,0},{2,3},{3,2},{4,5},{5,4},{6,7},{7,6},{8,9},{9,8},{10,11... | collective-permute-start | bytes 393224 | tf_op jit(solution)/shard_map/ppermute | solution.py:323

commit v2 on v1

v2 whole, which is shorter than its diff:
```python
import jax
import jax.numpy as jnp
from jax import lax
from jax.experimental import pallas as pl
from jax.experimental.pallas import tpu as pltpu
from jax.sharding import Mesh, PartitionSpec as P

F32, BF16 = jnp.float32, jnp.bfloat16
VM = pl.BlockSpec(memory_space=pltpu.VMEM)
SM = pl.BlockSpec(memory_space=pltpu.SMEM)
SWAP = [(0, 1), (1, 0)]


def call(kernel, outs, scratch=(), specs=None, flops=0, nbytes=0, vmem=24):
    return pl.pallas_call(
        kernel,
        out_shape=outs,
        in_specs=specs,
        out_specs=jax.tree.map(lambda _: VM, outs),
        scratch_shapes=list(scratch),
        compiler_params=pltpu.CompilerParams(vmem_limit_bytes=vmem << 20),
        cost_estimate=pl.CostEstimate(flops=flops, bytes_accessed=nbytes, transcendentals=0),
    )


def shaped(shape, dtype):
    return jax.ShapeDtypeStruct(shape, dtype)


def iota(shape, dim):
    return lax.broadcasted_iota(jnp.int32, shape, dim)


def weights_kernel(lift, mix, outw, a1, a2, a3):
    spread = (iota((256, 64), 0) >> 2 == iota((256, 64), 1)).astype(F32).astype(BF16)
    spread_t = (iota((64, 256), 1) >> 2 == iota((64, 256), 0)).astype(F32).astype(BF16)
    taps = (iota((32, 256), 1) >> 3 == iota((32, 256), 0)).astype(F32).astype(BF16)
    row, col = iota((256, 256), 0) & 3, iota((256, 256), 1)
    part = iota((64, 32), 1)
    for k in range(3):
        full = lift[k]
        high = full.astype(BF16).astype(F32)
        mid = (full - high).astype(BF16).astype(F32)
        low = full - high - mid
        split = jnp.where(part == 28, mid, jnp.where(part == 29, low, high)).astype(BF16)
        base = jnp.dot(spread, split, preferred_element_type=F32).astype(BF16)
        base = jnp.dot(base, taps, preferred_element_type=F32)
        for half in range(2):
            a1[k, half * 256 : half * 256 + 256] = jnp.where(
                row + 4 * half == (col & 7), base, 0.0
            ).astype(BF16)
        mixed = jnp.dot(spread, mix[k], preferred_element_type=F32).astype(BF16)
        mixed = jnp.dot(mixed, spread_t, preferred_element_type=F32)
        a2[k] = jnp.where(row == (col & 3), mixed, 0.0).astype(BF16)
        a3[k] = jnp.dot(spread, outw[k], preferred_element_type=F32)


def pack_kernel(vol, out):
    zero = jnp.zeros((1, 128), F32)
    for p in range(16):
        for z in range(4):
            lo, hi = max(8 * p - 1, 0), min(8 * p + 9, 128)
            at = z * 10 + lo - (8 * p - 1)
            out[p, at : at + hi - lo] = vol[z, lo:hi]
            if p == 0:
                out[p, z * 10 : z * 10 + 1] = zero
            if p == 15:
                out[p, z * 10 + 9 : z * 10 + 10] = zero


def turn_kernel(rows, vol, half):
    for r in range(40):
        x = rows[pl.ds(r, 16, stride=40), :]
        vol[r] = x
        half[r] = x.astype(BF16)


def edges_kernel(vol, other, first, last):
    for r in range(10):
        first[r] = vol[r].astype(BF16)
        last[r] = vol[r + 30].astype(BF16)
        first[r + 10] = other[r]
        last[r + 10] = other[r + 30]


def spread_y(s, pos, v):
    lane = iota(v.shape, 1)
    s[0, pos] = jnp.where(lane == 0, 0.0, pltpu.roll(v, 1, 1))
    s[1, pos] = v
    s[2, pos] = jnp.where(lane == 127, 0.0, pltpu.roll(v, 127, 1))


def fill(c, own, theirs, pos, mine, other):
    spread_y(own, pos, mine)
    other = other.astype(F32)
    early = jnp.concatenate([jnp.zeros((1, 128), F32), other, jnp.zeros((7, 128), F32)], axis=0)
    late = jnp.concatenate([other, jnp.zeros((8, 128), F32)], axis=0)
    spread_y(theirs, pos, jnp.where(c == 0, early, late))


OFFSETS = (
    [(dt, db, da - 1) for dt in range(3) for da in range(3) for db in range(3)],
    [(dt, da, 10 * (db - 1)) for dt in range(3) for da in range(3) for db in range(3)],
    [(dt, 1, 10 * (da - 1) + db - 1) for dt in range(3) for da in range(3) for db in range(3)],
)


def corrected(own, theirs, a1, a2, a3, which, weight, pos, block):
    rows = []
    for dt, dy, step in OFFSETS[which]:
        s = own if dt == 1 else theirs
        at = pl.ds(8 * block + (dt == 2), 8)
        rows.append(
            jnp.concatenate([s[dy, pos + step, at, :], s[dy, pos + step + 1, at, :]], axis=1)
        )
    rows.append(jnp.ones((24, 256), F32))
    rows.append(jnp.zeros((16, 256), F32))
    taps = jnp.concatenate(rows, axis=0).astype(BF16)
    first = jnp.dot(a1[weight], taps, preferred_element_type=F32)
    first = jnp.maximum(first, 0.0).astype(BF16)
    w = a3[weight]
    w = jnp.concatenate([w, w], axis=1)
    sums = []
    for half in range(2):
        second = jnp.dot(
            a2[weight], first[half * 256 : half * 256 + 256], preferred_element_type=F32
        )
        second = jnp.maximum(second, 0.0) * w
        total = jnp.sum(second.reshape(32, 8, 256), axis=0)
        sums.append(total + pltpu.roll(total, 4, 0))
    return jnp.where(iota((8, 256), 0) < 4, sums[0], sums[1])


def xy_kernel(core, vol, other, a1, a2, a3, out, own, theirs):
    def load(r, carry):
        fill(core[0], own, theirs, r + 10, vol[r], other[r])
        return carry

    lax.fori_loop(0, 40, load, 0)

    def step(i, carry):
        z, x = i // 4, 2 * (i % 4)
        pos = (z + 1) * 10 + 1 + x
        for block in range(2):
            got = corrected(own, theirs, a1, a2, a3, 0, 0, pos, block)
            for j in range(2):
                out[z * 8 + x + j, 8 * block : 8 * block + 8] = got[:, 128 * j : 128 * j + 128]
        return carry

    lax.fori_loop(0, 16, step, 0)


def rest_kernel(core, vol, other, before, after, xy, a1, a2, a3, cons, image, own, theirs):
    def load(r, carry):
        fill(core[0], own, theirs, r + 10, vol[r], other[r])
        return carry

    lax.fori_loop(0, 40, load, 0)

    def load_edge(r, carry):
        fill(core[0], own, theirs, r, before[r].astype(F32), before[r + 10])
        fill(core[0], own, theirs, r + 50, after[r].astype(F32), after[r + 10])
        return carry

    lax.fori_loop(0, 10, load_edge, 0)

    def step(i, carry):
        z, x = i // 4, 2 * (i % 4)
        pos = (z + 1) * 10 + 1 + x
        for block in range(2):
            at = slice(8 * block, 8 * block + 8)
            got = corrected(own, theirs, a1, a2, a3, 1, 1, pos, block)
            got = got + corrected(own, theirs, a1, a2, a3, 2, 2, pos, block)
            for j in range(2):
                total = xy[z * 8 + x + j, at] + got[:, 128 * j : 128 * j + 128]
                cons[z * 8 + x + j, at] = vol[pos - 10 + j, at] + total / 3.0
        return carry

    lax.fori_loop(0, 16, step, 0)
    for z in range(4):
        for x in range(8):
            image[16 * z : 16 * z + 16, 128 * x : 128 * x + 128] = cons[z * 8 + x].astype(BF16)


def transpose_kernel(core, own, pair, out):
    c = core[0]

    def step(j, carry):
        rays = pl.ds(pl.multiple_of(256 * j, 256), 256)
        out[c, :, rays] = own[rays, :].T
        out[1 - c, :, rays] = pair[rays, :].T
        return carry

    lax.fori_loop(0, 8, step, 0)


def project_kernel(image, pixels, out, turned):
    for j in range(8):
        rays = slice(256 * j, 256 * j + 256)
        got = jnp.dot(image[:, :512], pixels[0, :, rays], preferred_element_type=F32)
        got = got + jnp.dot(image[:, 512:], pixels[1, :, rays], preferred_element_type=F32)
        for z in range(4):
            for n in range(2):
                turned[2 * (j % 4) + n, pl.ds(z * 2 + j // 4, 16, stride=8), :] = got[
                    16 * z : 16 * z + 16, 128 * n : 128 * n + 128
                ]
    for n in range(8):
        lanes = slice(128 * n, 128 * n + 128)
        for t in range(16):
            out[t, :, lanes] = turned[n, 8 * t : 8 * t + 8].astype(BF16)


def misfit_kernel(parts, measured, out):
    total = parts[0].astype(F32)
    for t in range(1, 16):
        total = total + parts[t].astype(F32)
    misfit = (total - measured[...]).astype(BF16)
    for t in range(16):
        out[t] = misfit


def far_kernel(core, misfit, pair, cons, far, rows, turned):
    for n in range(8):
        for t in range(16):
            turned[n, 8 * t : 8 * t + 8] = misfit[t, :, 128 * n : 128 * n + 128].astype(F32)
    for z in range(4):
        for half in range(2):
            for n in range(8):
                rows[16 * z : 16 * z + 16, 1024 * half + 128 * n : 1024 * half + 128 * n + 128] = (
                    turned[n, pl.ds(z * 2 + half, 16, stride=8), :].astype(BF16)
                )
    got = jnp.dot(rows[...], pair[...], preferred_element_type=F32)
    stepped(1 - core[0], cons, got, far)


def stepped(c, cons, gradient, out):
    for z in range(4):
        for x in range(4):
            at = (slice(16 * z, 16 * z + 16), slice(128 * x, 128 * x + 128))
            out[at] = cons[z * 8 + x + 4 * c] - gradient[at]


def near_kernel(core, rows, own, cons, near):
    got = jnp.dot(rows[...], own[...], preferred_element_type=F32)
    stepped(core[0], cons, got, near)


def merge_kernel(core, near, far, out, turned):
    def write(parity, rows):
        for z in range(4):
            for x in range(4):
                turned[x, pl.ds(4 * parity + z, 16, stride=8), :] = rows[
                    16 * z : 16 * z + 16, 128 * x : 128 * x + 128
                ]

    @pl.when(core[0] == 0)
    def _():
        write(0, near)
        write(1, far)

    @pl.when(core[0] == 1)
    def _():
        write(1, near)
        write(0, far)

    for x in range(4):
        for t in range(32):
            out[t, :, 128 * x : 128 * x + 128] = turned[x, 4 * t : 4 * t + 4]


def shards(volume, lift_weights, lift_bias, mix_weights, out_weights, projector, measured):
    core = lax.axis_index("c").reshape(1)
    packed = call(pack_kernel, shaped((16, 40, 128), F32), specs=[VM], nbytes=1 << 20)(volume[0])
    frames = lax.all_to_all(packed, "q", split_axis=0, concat_axis=0, tiled=True)

    pair = lax.ppermute(projector, "c", SWAP)
    bias = jnp.broadcast_to(lift_bias[:, :, None], (3, 64, 3))
    lift = jnp.concatenate(
        [lift_weights.astype(F32), bias, jnp.zeros((3, 64, 2), F32)], axis=2
    )
    outw = jnp.broadcast_to(out_weights[:, :, None], (3, 64, 128))
    a1, a2, a3 = call(
        weights_kernel,
        (shaped((3, 512, 256), BF16), shaped((3, 256, 256), BF16), shaped((3, 256, 128), F32)),
        specs=[VM] * 3,
        flops=10**8,
        nbytes=1 << 20,
    )(lift, mix_weights, outw)
    pixels = call(
        transpose_kernel,
        shaped((2, 512, 2048), BF16),
        specs=[SM, VM, VM],
        nbytes=8 << 20,
    )(core, projector, pair)

    vol, half = call(
        turn_kernel,
        (shaped((40, 16, 128), F32), shaped((40, 16, 128), BF16)),
        specs=[VM],
        nbytes=1 << 20,
    )(frames.reshape(640, 128))
    other = lax.ppermute(half, "c", SWAP)
    plane = shaped((20, 16, 128), BF16)
    first, last = call(edges_kernel, (plane, plane), specs=[VM] * 2)(vol, other)
    up = [(i, i + 1) for i in range(7)]
    before = lax.ppermute(last, "space", up)
    after = lax.ppermute(first, "space", [(j, i) for i, j in up])

    spread = [pltpu.VMEM((3, 60, 16, 128), F32), pltpu.VMEM((3, 60, 24, 128), F32)]
    xy = call(
        xy_kernel, shaped((32, 16, 128), F32), spread, [SM] + [VM] * 5, flops=12 * 10**9, nbytes=1 << 20
    )(core, vol, other, a1, a2, a3)
    cons, image = call(
        rest_kernel,
        (shaped((32, 16, 128), F32), shaped((64, 1024), BF16)),
        spread,
        [SM] + [VM] * 8,
        flops=24 * 10**9,
        nbytes=1 << 20,
    )(core, vol, other, before, after, xy, a1, a2, a3)

    partial = call(
        project_kernel,
        shaped((16, 8, 1024), BF16),
        [pltpu.VMEM((8, 128, 128), F32)],
        [VM] * 2,
        flops=3 * 10**8,
        nbytes=5 << 20,
    )(image, pixels)
    parts = lax.all_to_all(partial, "q", split_axis=0, concat_axis=0, tiled=True)
    misfit = call(misfit_kernel, shaped((16, 8, 1024), BF16), specs=[VM] * 2)(
        parts, measured.reshape(8, 1024)
    )
    misfit = lax.all_to_all(misfit, "q", split_axis=0, concat_axis=0, tiled=True)
    far, rows = call(
        far_kernel,
        (shaped((64, 512), F32), shaped((64, 2048), BF16)),
        [pltpu.VMEM((8, 128, 128), F32)],
        [SM] + [VM] * 3,
        flops=15 * 10**7,
        nbytes=3 << 20,
    )(core, misfit, pair, cons)
    far = lax.ppermute(far, "c", SWAP)
    near = call(
        near_kernel,
        shaped((64, 512), F32),
        specs=[SM] + [VM] * 3,
        flops=15 * 10**7,
        nbytes=3 << 20,
    )(core, rows, projector, cons)
    return call(
        merge_kernel,
        shaped((32, 4, 512), F32),
        [pltpu.VMEM((4, 128, 128), F32)],
        [SM] + [VM] * 2,
    )(core, near, far)


def solution(mesh):
    fine = Mesh(mesh.devices.reshape(8, 16, 2), ("space", "q", "c"))
    tm = ("q", "c")
    placed = (
        P(tm, "space", None, None),
        P(),
        P(),
        P(),
        P(),
        P(None, tm),
        P(tm, "space", None),
    )
    return jax.shard_map(
        shards, mesh=fine, in_specs=placed, out_specs=P(None, "space", tm), check_vma=False
    )
```

time: 105 us -> 108 us (1.029)
  the two profiles are of different devices: /device:TPU:37 before, /device:TPU:41 now
where the time goes in v2:
time: 108 us; the launch traced here: 106 us
  Pallas kernels  41.4 us (38%)
  starting transfers between devices  26.6 us (25%)
  waiting for transfers between devices  20.4 us (19%)
  blocking collectives  15 us (14%)
  local copies, waits for them, and re-layouts  2.76 us (3%)
    pallas_call x1, Pallas kernels, shards(): call(rest_kernel, (shaped((32, 16, 128), F32), shaped((64, 1024), BF16)),...  18.4 us
    all_to_all x1, blocking collectives, shards(): lax.all_to_all(misfit, 'q', split_axis=0, concat_axis=0, tiled=True)  15 us
    pallas_call x1, Pallas kernels, shards(): call(xy_kernel, shaped((32, 16, 128), F32), spread, [SM] + [VM] * 5, flop...  13.1 us
    all_to_all x1, waiting for transfers between devices, shards(): lax.all_to_all(partial, 'q', split_axis=0, concat_axis=0, tiled=True)  10.9 us
    all_to_all x1, starting transfers between devices, shards(): lax.all_to_all(packed, 'q', split_axis=0, concat_axis=0, tiled=True)  9.76 us
    all_to_all x1, waiting for transfers between devices, shards(): lax.all_to_all(packed, 'q', split_axis=0, concat_axis=0, tiled=True)  8.97 us
    all_to_all x1, starting transfers between devices, shards(): lax.all_to_all(partial, 'q', split_axis=0, concat_axis=0, tiled=True)  4.07 us
    ppermute x1, starting transfers between devices, shards(): before = lax.ppermute(last, 'space', up)  3.9 us
  transfers between devices with their start and end apart: 7, of which 3 were waited for; matrix products, arithmetic and copies ran while one was open for 2% of the time, Pallas kernels for 31%

profile of v2, /device:TPU:41, one launch (start us, length us, event | category | flops | bytes accessed | tf_op | source)
XLA Modules:
  0.0 106.4 jit_solution(7817974054273194505)
XLA Ops:
  0.0 1.0 copy-done.1
  1.0 0.8 shard_map.73
  1.7 9.8 %all-to-all-start = ((f32[16,40,128]{2,1,0:T(8,128)}), f32[16,40,128]{2,1,0:T(8,128)S(1)}, u32[]{:S(2)}, u32[]{:S(2)}) async-start(f32[16,40,128]{2,1,0:T(8,128)} %shard_map.73), calls=%async_computation | async-start | bytes 655360 | tf_op jit(solution)/shard_map/all_to_all | solution.py:274
  11.5 1.2 %collective-permute-start.3 = (bf16[2048,512]{1,0:T(8,128)(2,1)}, bf16[2048,512]{1,0:T(8,128)(2,1)}, u32[]{:S(2)}, u32[]{:S(2)}) collective-permute-start(bf16[2048,512]{1,0:T(8,128)(2,1)} %own.3), channel_id=1, source_target_pairs={{0,1},{1,0},{2,3},{3,2},{4,5},{5,4},{6,7},{7,6},{8,9},{9,8},{10,11... | collective-permute-start | bytes 6291464 | tf_op jit(solution)/shard_map/ppermute | solution.py:276
  12.7 0.8 copy.9
  13.7 9.0 %all-to-all-done = f32[16,40,128]{2,1,0:T(8,128)S(1)} async-done(((f32[16,40,128]{2,1,0:T(8,128)}), f32[16,40,128]{2,1,0:T(8,128)S(1)}, u32[]{:S(2)}, u32[]{:S(2)}) %all-to-all-start) | async-done | bytes 327712 | tf_op jit(solution)/shard_map/all_to_all | solution.py:274
  22.7 2.9 %collective-permute-start = (bf16[40,16,128]{2,1,0:T(8,128)(2,1)S(1)}, bf16[40,16,128]{2,1,0:T(8,128)(2,1)S(1)}, u32[]{:S(2)}, u32[]{:S(2)}) collective-permute-start(bf16[40,16,128]{2,1,0:T(8,128)(2,1)S(1)} %get-tuple-element.17), channel_id=1, source_target_pairs={{0,1},{1,0},{2,3},{3,2},{4,5},{5,4},{6,7},{7,6},{8,9},{9,8},{10,11... | collective-permute-start | bytes 491528 | tf_op jit(solution)/shard_map/ppermute | solution.py:302
  25.6 0.8 broadcast_in_dim.6
  26.3 0.1 maximum_maximum_fusion.lift
  26.6 0.8 shard_map.76
  27.4 3.9 %collective-permute-start.1 = (bf16[20,16,128]{2,1,0:T(8,128)(2,1)S(1)}, bf16[20,16,128]{2,1,0:T(8,128)(2,1)S(1)}, u32[]{:S(2)}, u32[]{:S(2)}) collective-permute-start(bf16[20,16,128]{2,1,0:T(8,128)(2,1)S(1)} %get-tuple-element.18), channel_id=1, source_target_pairs={{0,32},{32,64},{64,96},{96,128},{128,160},{160,192},{192,224},{1,3... | collective-permute-start | bytes 245768 | tf_op jit(solution)/shard_map/ppermute | solution.py:306
  31.3 1.9 %collective-permute-start.2 = (bf16[20,16,128]{2,1,0:T(8,128)(2,1)S(1)}, bf16[20,16,128]{2,1,0:T(8,128)(2,1)S(1)}, u32[]{:S(2)}, u32[]{:S(2)}) collective-permute-start(bf16[20,16,128]{2,1,0:T(8,128)(2,1)S(1)} %get-tuple-element.19), channel_id=1, source_target_pairs={{32,0},{64,32},{96,64},{128,96},{160,128},{192,160},{224,192},{33,... | collective-permute-start | bytes 245768 | tf_op jit(solution)/shard_map/ppermute | solution.py:307
  33.3 13.1 %shard_map.77.xy = f32[32,16,128]{2,1,0:T(8,128)S(1)} custom-call(s32[1]{0:T(128)} %bitcast.core, f32[40,16,128]{2,1,0:T(8,128)S(1)} %get-tuple-element.16.vol, bf16[40,16,128]{2,1,0:T(8,128)(2,1)S(1)} %collective-permute-done.other, bf16[3,512,256]{2,1,0:T(8,128)(2,1)S(1)} %get-tuple-element.20.a1, bf16[3,256,256]{2,1,0:T(8,128)(2,1)S(1)} %get-tuple-element.21.a2, ...), custom_call_target="tpu_custom_call" | custom-call | flops 12000000000 | bytes 1048576 | tf_op jit(solution)/shard_map/pallas_call | solution.py:310
  46.4 18.4 %shard_map.78 = (f32[32,16,128]{2,1,0:T(8,128)S(1)}, bf16[64,1024]{1,0:T(8,128)(2,1)S(1)}) custom-call(s32[1]{0:T(128)} %bitcast.core, f32[40,16,128]{2,1,0:T(8,128)S(1)} %get-tuple-element.16.vol, bf16[40,16,128]{2,1,0:T(8,128)(2,1)S(1)} %collective-permute-done.other, bf16[20,16,128]{2,1,0:T(8,128)(2,1)S(1)} %collective-permute-done.1.before, ...), custom_call_target="tpu_custom_call" | custom-call | flops 24000000000 | bytes 1048576 | tf_op jit(solution)/shard_map/pallas_call | solution.py:313
  64.8 3.2 %shard_map.79.pixels = bf16[2,512,2048]{2,1,0:T(8,128)(2,1)S(1)} custom-call(s32[1]{0:T(128)} %bitcast.core, bf16[2048,512]{1,0:T(8,128)(2,1)S(1)} %copy-done, bf16[2048,512]{1,0:T(8,128)(2,1)} %collective-permute-done.3.pair), custom_call_target="tpu_custom_call" | custom-call | bytes 8388608 | tf_op jit(solution)/shard_map/pallas_call | solution.py:289
  68.0 1.6 %shard_map.80 = bf16[16,8,1024]{2,1,0:T(8,128)(2,1)} custom-call(bf16[64,1024]{1,0:T(8,128)(2,1)S(1)} %get-tuple-element.23.image, bf16[2,512,2048]{2,1,0:T(8,128)(2,1)S(1)} %shard_map.79.pixels), custom_call_target="tpu_custom_call" | custom-call | flops 300000000 | bytes 5242880 | tf_op jit(solution)/shard_map/pallas_call | solution.py:322
  69.6 4.1 %all-to-all-start.1 = ((bf16[16,8,1024]{2,1,0:T(8,128)(2,1)}), bf16[16,8,1024]{2,1,0:T(8,128)(2,1)S(1)}, u32[]{:S(2)}, u32[]{:S(2)}) async-start(bf16[16,8,1024]{2,1,0:T(8,128)(2,1)} %shard_map.80), calls=%async_computation.1 | async-start | bytes 524288 | tf_op jit(solution)/shard_map/all_to_all | solution.py:330
  73.7 10.9 %all-to-all-done.1.parts = bf16[16,8,1024]{2,1,0:T(8,128)(2,1)S(1)} async-done(((bf16[16,8,1024]{2,1,0:T(8,128)(2,1)}), bf16[16,8,1024]{2,1,0:T(8,128)(2,1)S(1)}, u32[]{:S(2)}, u32[]{:S(2)}) %all-to-all-start.1) | async-done | bytes 262176 | tf_op jit(solution)/shard_map/all_to_all | solution.py:330
  84.7 15.0 %all_to_all.15.misfit = bf16[16,8,1024]{2,1,0:T(8,128)(2,1)S(1)} all-to-all(bf16[16,8,1024]{2,1,0:T(8,128)(2,1)S(1)} %shard_map.81), channel_id=1, replica_groups=mesh['space'=8,'q'=16,'c'=2] {'q'}, dimensions={0} | all-to-all | bytes 524288 | tf_op jit(solution)/shard_map/all_to_all | solution.py:334
  99.7 2.1 %shard_map.82 = (f32[64,512]{1,0:T(8,128)S(1)}, bf16[64,2048]{1,0:T(8,128)(2,1)S(1)}) custom-call(s32[1]{0:T(128)} %bitcast.core, bf16[16,8,1024]{2,1,0:T(8,128)(2,1)S(1)} %all_to_all.15.misfit, bf16[2048,512]{1,0:T(8,128)(2,1)} %collective-permute-done.3.pair, f32[32,16,128]{2,1,0:T(8,128)S(1)} %get-tuple-element.24.cons), custom_call_target="tpu_custom_call" | custom-call | flops 150000000 | bytes 3145728 | tf_op jit(solution)/shard_map/pallas_call | solution.py:335
  101.8 2.8 %collective-permute-start.4 = (f32[64,512]{1,0:T(8,128)S(1)}, f32[64,512]{1,0:T(8,128)S(1)}, u32[]{:S(2)}, u32[]{:S(2)}) collective-permute-start(f32[64,512]{1,0:T(8,128)S(1)} %get-tuple-element.26), channel_id=1, source_target_pairs={{0,1},{1,0},{2,3},{3,2},{4,5},{5,4},{6,7},{7,6},{8,9},{9,8},{10,11... | collective-permute-start | bytes 393224 | tf_op jit(solution)/shard_map/ppermute | solution.py:343
  104.6 0.5 shard_map.83.near
  105.1 0.5 collective-permute-done.4.far
  105.6 0.8 shard_map.84
  (20 shorter events, 0.3 us)
Async XLA Ops:
  0.0 26.5 %copy-start.4 = (bf16[3,64]{1,0:T(4,128)(2,1)S(1)}, bf16[3,64]{1,0:T(4,128)(2,1)}, u32[]{:S(2)}) copy-start(bf16[3,64]{1,0:T(4,128)(2,1)} %param.11) | copy-start | bytes 1156
  0.0 1.0 copy-start.1
  1.0 25.6 %copy-start.2 = (bf16[3,64,64]{2,1,0:T(8,128)(2,1)S(1)}, bf16[3,64,64]{2,1,0:T(8,128)(2,1)}, u32[]{:S(2)}) copy-start(bf16[3,64,64]{2,1,0:T(8,128)(2,1)} %mix.1) | copy-start | bytes 73732
  1.7 20.9 %all-to-all-start = ((f32[16,40,128]{2,1,0:T(8,128)}), f32[16,40,128]{2,1,0:T(8,128)S(1)}, u32[]{:S(2)}, u32[]{:S(2)}) async-start(f32[16,40,128]{2,1,0:T(8,128)} %shard_map.73), calls=%async_computation | async-start | bytes 655360 | tf_op jit(solution)/shard_map/all_to_all | solution.py:274
  11.5 53.3 %collective-permute-start.3 = (bf16[2048,512]{1,0:T(8,128)(2,1)}, bf16[2048,512]{1,0:T(8,128)(2,1)}, u32[]{:S(2)}, u32[]{:S(2)}) collective-permute-start(bf16[2048,512]{1,0:T(8,128)(2,1)} %own.3), channel_id=1, source_target_pairs={{0,1},{1,0},{2,3},{3,2},{4,5},{5,4},{6,7},{7,6},{8,9},{9,8},{10,11... | collective-permute-start | bytes 6291464 | tf_op jit(solution)/shard_map/ppermute | solution.py:276
  22.7 4.7 %collective-permute-start = (bf16[40,16,128]{2,1,0:T(8,128)(2,1)S(1)}, bf16[40,16,128]{2,1,0:T(8,128)(2,1)S(1)}, u32[]{:S(2)}, u32[]{:S(2)}) collective-permute-start(bf16[40,16,128]{2,1,0:T(8,128)(2,1)S(1)} %get-tuple-element.17), channel_id=1, source_target_pairs={{0,1},{1,0},{2,3},{3,2},{4,5},{5,4},{6,7},{7,6},{8,9},{9,8},{10,11... | collective-permute-start | bytes 491528 | tf_op jit(solution)/shard_map/ppermute | solution.py:302
  27.4 18.9 %collective-permute-start.1 = (bf16[20,16,128]{2,1,0:T(8,128)(2,1)S(1)}, bf16[20,16,128]{2,1,0:T(8,128)(2,1)S(1)}, u32[]{:S(2)}, u32[]{:S(2)}) collective-permute-start(bf16[20,16,128]{2,1,0:T(8,128)(2,1)S(1)} %get-tuple-element.18), channel_id=1, source_target_pairs={{0,32},{32,64},{64,96},{96,128},{128,160},{160,192},{192,224},{1,3... | collective-permute-start | bytes 245768 | tf_op jit(solution)/shard_map/ppermute | solution.py:306
  31.3 15.0 %collective-permute-start.2 = (bf16[20,16,128]{2,1,0:T(8,128)(2,1)S(1)}, bf16[20,16,128]{2,1,0:T(8,128)(2,1)S(1)}, u32[]{:S(2)}, u32[]{:S(2)}) collective-permute-start(bf16[20,16,128]{2,1,0:T(8,128)(2,1)S(1)} %get-tuple-element.19), channel_id=1, source_target_pairs={{32,0},{64,32},{96,64},{128,96},{160,128},{192,160},{224,192},{33,... | collective-permute-start | bytes 245768 | tf_op jit(solution)/shard_map/ppermute | solution.py:307
  46.3 18.5 %copy-start = (bf16[2048,512]{1,0:T(8,128)(2,1)S(1)}, bf16[2048,512]{1,0:T(8,128)(2,1)}, u32[]{:S(2)}) copy-start(bf16[2048,512]{1,0:T(8,128)(2,1)} %own.3) | copy-start | bytes 6291460
  68.0 5.7 %copy-start.3 = (f32[1,4,2048]{2,1,0:T(4,128)S(1)}, f32[1,4,2048]{2,1,0:T(4,128)}, u32[]{:S(2)}) copy-start(f32[1,4,2048]{2,1,0:T(4,128)} %param.13) | copy-start | bytes 98308
  69.6 15.0 %all-to-all-start.1 = ((bf16[16,8,1024]{2,1,0:T(8,128)(2,1)}), bf16[16,8,1024]{2,1,0:T(8,128)(2,1)S(1)}, u32[]{:S(2)}, u32[]{:S(2)}) async-start(bf16[16,8,1024]{2,1,0:T(8,128)(2,1)} %shard_map.80), calls=%async_computation.1 | async-start | bytes 524288 | tf_op jit(solution)/shard_map/all_to_all | solution.py:330
  101.8 3.8 %collective-permute-start.4 = (f32[64,512]{1,0:T(8,128)S(1)}, f32[64,512]{1,0:T(8,128)S(1)}, u32[]{:S(2)}, u32[]{:S(2)}) collective-permute-start(f32[64,512]{1,0:T(8,128)S(1)} %get-tuple-element.26), channel_id=1, source_target_pairs={{0,1},{1,0},{2,3},{3,2},{4,5},{5,4},{6,7},{7,6},{8,9},{9,8},{10,11... | collective-permute-start | bytes 393224 | tf_op jit(solution)/shard_map/ppermute | solution.py:343

commit v3 on v2

--- a/solution.py
+++ b/solution.py
@@ -11,13 +11,14 @@
 SWAP = [(0, 1), (1, 0)]
 
 
-def call(kernel, outs, scratch=(), specs=None, flops=0, nbytes=0, vmem=24):
+def call(kernel, outs, scratch=(), specs=None, flops=0, nbytes=0, vmem=24, aliases=None):
     return pl.pallas_call(
         kernel,
         out_shape=outs,
         in_specs=specs,
         out_specs=jax.tree.map(lambda _: VM, outs),
         scratch_shapes=list(scratch),
+        input_output_aliases=aliases or {},
         compiler_params=pltpu.CompilerParams(vmem_limit_bytes=vmem << 20),
         cost_estimate=pl.CostEstimate(flops=flops, bytes_accessed=nbytes, transcendentals=0),
     )
@@ -75,27 +76,46 @@
         half[r] = x.astype(BF16)
 
 
-def edges_kernel(vol, other, first, last):
+def spread_y(s, pos, at, v):
+    lane = iota((8, 128), 1)
+    s[0, pos, at] = jnp.where(lane == 0, 0.0, pltpu.roll(v, 1, 1))
+    s[1, pos, at] = v
+    s[2, pos, at] = jnp.where(lane == 127, 0.0, pltpu.roll(v, 127, 1))
+
+
+def spread_frames(core, padded, places, own, theirs, mine, other):
+    zero = jnp.zeros((8, 128), F32)
+    for r, pos in enumerate(places):
+        padded[r, 0:8] = zero
+        padded[r, 8:24] = other(r).astype(F32)
+        padded[r, 24:32] = zero
+        for j in range(2):
+            spread_y(own, pos, slice(8 * j, 8 * j + 8), mine(r)[8 * j : 8 * j + 8].astype(F32))
+
+    def write(start):
+        for r, pos in enumerate(places):
+            for j in range(3):
+                got = padded[r, pl.ds(start + 8 * j, 8), :]
+                spread_y(theirs, pos, slice(8 * j, 8 * j + 8), got)
+
+    @pl.when(core[0] == 0)
+    def _():
+        write(7)
+
+    @pl.when(core[0] == 1)
+    def _():
+        write(8)
+
+
+def spread_kernel(core, vol, other, own, theirs, first, last, padded):
     for r in range(10):
         first[r] = vol[r].astype(BF16)
         last[r] = vol[r + 30].astype(BF16)
         first[r + 10] = other[r]
         last[r + 10] = other[r + 30]
-
-
-def spread_y(s, pos, v):
-    lane = iota(v.shape, 1)
-    s[0, pos] = jnp.where(lane == 0, 0.0, pltpu.roll(v, 1, 1))
-    s[1, pos] = v
-    s[2, pos] = jnp.where(lane == 127, 0.0, pltpu.roll(v, 127, 1))
-
-
-def fill(c, own, theirs, pos, mine, other):
-    spread_y(own, pos, mine)
-    other = other.astype(F32)
-    early = jnp.concatenate([jnp.zeros((1, 128), F32), other, jnp.zeros((7, 128), F32)], axis=0)
-    late = jnp.concatenate([other, jnp.zeros((8, 128), F32)], axis=0)
-    spread_y(theirs, pos, jnp.where(c == 0, early, late))
+    spread_frames(
+        core, padded, range(10, 50), own, theirs, lambda r: vol[r], lambda r: other[r]
+    )
 
 
 OFFSETS = (
@@ -131,13 +151,7 @@
     return jnp.where(iota((8, 256), 0) < 4, sums[0], sums[1])
 
 
-def xy_kernel(core, vol, other, a1, a2, a3, out, own, theirs):
-    def load(r, carry):
-        fill(core[0], own, theirs, r + 10, vol[r], other[r])
-        return carry
-
-    lax.fori_loop(0, 40, load, 0)
-
+def xy_kernel(own, theirs, a1, a2, a3, out):
     def step(i, carry):
         z, x = i // 4, 2 * (i % 4)
         pos = (z + 1) * 10 + 1 + x
@@ -150,19 +164,14 @@
     lax.fori_loop(0, 16, step, 0)
 
 
-def rest_kernel(core, vol, other, before, after, xy, a1, a2, a3, cons, image, own, theirs):
-    def load(r, carry):
-        fill(core[0], own, theirs, r + 10, vol[r], other[r])
-        return carry
-
-    lax.fori_loop(0, 40, load, 0)
-
-    def load_edge(r, carry):
-        fill(core[0], own, theirs, r, before[r].astype(F32), before[r + 10])
-        fill(core[0], own, theirs, r + 50, after[r].astype(F32), after[r + 10])
-        return carry
-
-    lax.fori_loop(0, 10, load_edge, 0)
+def rest_kernel(
+    core, vol, before, after, xy, a1, a2, a3, own_in, theirs_in, cons, image, own, theirs, padded
+):
+    def pick(offset):
+        return lambda r: before[r + offset] if r < 10 else after[r - 10 + offset]
+
+    places = list(range(10)) + list(range(50, 60))
+    spread_frames(core, padded, places, own, theirs, pick(0), pick(10))
 
     def step(i, carry):
         z, x = i // 4, 2 * (i % 4)
@@ -292,6 +301,7 @@
         specs=[SM, VM, VM],
         nbytes=8 << 20,
     )(core, projector, pair)
+    frames, a1, a2, a3, pixels = lax.optimization_barrier((frames, a1, a2, a3, pixels))
 
     vol, half = call(
         turn_kernel,
@@ -301,23 +311,35 @@
     )(frames.reshape(640, 128))
     other = lax.ppermute(half, "c", SWAP)
     plane = shaped((20, 16, 128), BF16)
-    first, last = call(edges_kernel, (plane, plane), specs=[VM] * 2)(vol, other)
+    own, theirs = shaped((3, 60, 16, 128), F32), shaped((3, 60, 24, 128), F32)
+    own, theirs, first, last = call(
+        spread_kernel,
+        (own, theirs, plane, plane),
+        [pltpu.VMEM((40, 32, 128), F32)],
+        [SM, VM, VM],
+        nbytes=8 << 20,
+    )(core, vol, other)
     up = [(i, i + 1) for i in range(7)]
     before = lax.ppermute(last, "space", up)
     after = lax.ppermute(first, "space", [(j, i) for i, j in up])
 
-    spread = [pltpu.VMEM((3, 60, 16, 128), F32), pltpu.VMEM((3, 60, 24, 128), F32)]
     xy = call(
-        xy_kernel, shaped((32, 16, 128), F32), spread, [SM] + [VM] * 5, flops=12 * 10**9, nbytes=1 << 20
-    )(core, vol, other, a1, a2, a3)
-    cons, image = call(
+        xy_kernel, shaped((32, 16, 128), F32), (), [VM] * 5, flops=12 * 10**9, nbytes=1 << 20
+    )(own, theirs, a1, a2, a3)
+    cons, image, _, _ = call(
         rest_kernel,
-        (shaped((32, 16, 128), F32), shaped((64, 1024), BF16)),
-        spread,
-        [SM] + [VM] * 8,
+        (
+            shaped((32, 16, 128), F32),
+            shaped((64, 1024), BF16),
+            shaped((3, 60, 16, 128), F32),
+            shaped((3, 60, 24, 128), F32),
+        ),
+        [pltpu.VMEM((20, 32, 128), F32)],
+        [SM] + [VM] * 9,
         flops=24 * 10**9,
         nbytes=1 << 20,
-    )(core, vol, other, before, after, xy, a1, a2, a3)
+        aliases={8: 2, 9: 3},
+    )(core, vol, before, after, xy, a1, a2, a3, own, theirs)
 
     partial = call(
         project_kernel,

time: 108 us -> 103 us (0.954)
  the two profiles are of different devices: /device:TPU:41 before, /device:TPU:39 now
where the time goes in v3:
time: 103 us
  Pallas kernels  35.1 us (34%)
  starting transfers between devices  29.7 us (29%)
  blocking collectives  14.9 us (14%)
  waiting for transfers between devices  12.9 us (13%)
  local copies, waits for them, and re-layouts  9.68 us (9%)
    all_to_all x1, blocking collectives, shards(): lax.all_to_all(misfit, 'q', split_axis=0, concat_axis=0, tiled=True)  14.9 us
    pallas_call x1, Pallas kernels, shards(): call(rest_kernel, (shaped((32, 16, 128), F32), shaped((64, 1024), BF16),...  14.7 us
    all_to_all x1, starting transfers between devices, shards(): lax.all_to_all(packed, 'q', split_axis=0, concat_axis=0, tiled=True)  10.7 us
    all_to_all x1, waiting for transfers between devices, shards(): lax.all_to_all(partial, 'q', split_axis=0, concat_axis=0, tiled=True)  10.2 us
    pallas_call x1, Pallas kernels, shards(): call(xy_kernel, shaped((32, 16, 128), F32), (), [VM] * 5, flops=12 * 10 *...  9.94 us
    unnamed x22, local copies, waits for them, and re-layouts  7.21 us
    all_to_all x1, starting transfers between devices, shards(): lax.all_to_all(partial, 'q', split_axis=0, concat_axis=0, tiled=True)  6.91 us
    ppermute x1, starting transfers between devices, shards(): after = lax.ppermute(first, 'space', [(j, i) for i, j in up])  3.88 us
  transfers between devices with their start and end apart: 7, of which 4 were waited for; matrix products, arithmetic and copies ran while one was open for 2% of the time, Pallas kernels for 15%

profile of v3, /device:TPU:39, one launch (start us, length us, event | category | flops | bytes accessed | tf_op | source)
XLA Modules:
  0.0 102.6 jit_solution(8693042659143098523)
XLA Ops:
  0.7 0.9 copy-done.3
  2.4 10.7 %all-to-all-start = ((f32[16,40,128]{2,1,0:T(8,128)}), f32[16,40,128]{2,1,0:T(8,128)S(1)}, u32[]{:S(2)}, u32[]{:S(2)}) async-start(f32[16,40,128]{2,1,0:T(8,128)} %shard_map.73), calls=%async_computation | async-start | bytes 655360 | tf_op jit(solution)/shard_map/all_to_all | solution.py:283
  13.0 0.8 copy.11
  14.8 0.8 broadcast_in_dim.8.outw
  15.6 0.8 copy-done.4
  16.4 0.8 shard_map.74
  18.8 3.2 %shard_map.75.pixels = bf16[2,512,2048]{2,1,0:T(8,128)(2,1)S(1)} custom-call(s32[1]{0:T(128)} %bitcast.core, bf16[2048,512]{1,0:T(8,128)(2,1)S(1)} %copy-done.2, bf16[2048,512]{1,0:T(8,128)(2,1)} %collective-permute-done.pair), custom_call_target="tpu_custom_call" | custom-call | bytes 8388608 | tf_op jit(solution)/shard_map/pallas_call | solution.py:298
  22.0 1.9 %copy-done = bf16[2,512,2048]{2,1,0:T(8,128)(2,1)} copy-done((bf16[2,512,2048]{2,1,0:T(8,128)(2,1)}, bf16[2,512,2048]{2,1,0:T(8,128)(2,1)S(1)}, u32[]{:S(2)}) %copy-start) | copy-done | bytes 4194328
  23.9 1.2 %all-to-all-done = f32[16,40,128]{2,1,0:T(8,128)S(1)} async-done(((f32[16,40,128]{2,1,0:T(8,128)}), f32[16,40,128]{2,1,0:T(8,128)S(1)}, u32[]{:S(2)}, u32[]{:S(2)}) %all-to-all-start) | async-done | bytes 327712 | tf_op jit(solution)/shard_map/all_to_all | solution.py:283
  25.1 1.8 %collective-permute-start.1 = (bf16[40,16,128]{2,1,0:T(8,128)(2,1)S(1)}, bf16[40,16,128]{2,1,0:T(8,128)(2,1)S(1)}, u32[]{:S(2)}, u32[]{:S(2)}) collective-permute-start(bf16[40,16,128]{2,1,0:T(8,128)(2,1)S(1)} %get-tuple-element.28), channel_id=1, source_target_pairs={{0,1},{1,0},{2,3},{3,2},{4,5},{5,4},{6,7},{7,6},{8,9},{9,8},{10,11... | collective-permute-start | bytes 491528 | tf_op jit(solution)/shard_map/ppermute | solution.py:312
  27.0 1.0 %collective-permute-done.1.other = bf16[40,16,128]{2,1,0:T(8,128)(2,1)S(1)} collective-permute-done((bf16[40,16,128]{2,1,0:T(8,128)(2,1)S(1)}, bf16[40,16,128]{2,1,0:T(8,128)(2,1)S(1)}, u32[]{:S(2)}, u32[]{:S(2)}) %collective-permute-start.1) | collective-permute-done | bytes 163872 | tf_op jit(solution)/shard_map/ppermute | solution.py:312
  28.6 2.3 %collective-permute-start.2 = (bf16[20,16,128]{2,1,0:T(8,128)(2,1)S(1)}, bf16[20,16,128]{2,1,0:T(8,128)(2,1)S(1)}, u32[]{:S(2)}, u32[]{:S(2)}) collective-permute-start(bf16[20,16,128]{2,1,0:T(8,128)(2,1)S(1)} %get-tuple-element.29), channel_id=1, source_target_pairs={{0,32},{32,64},{64,96},{96,128},{128,160},{160,192},{192,224},{1,3... | collective-permute-start | bytes 245768 | tf_op jit(solution)/shard_map/ppermute | solution.py:323
  30.9 3.9 %collective-permute-start.3 = (bf16[20,16,128]{2,1,0:T(8,128)(2,1)S(1)}, bf16[20,16,128]{2,1,0:T(8,128)(2,1)S(1)}, u32[]{:S(2)}, u32[]{:S(2)}) collective-permute-start(bf16[20,16,128]{2,1,0:T(8,128)(2,1)S(1)} %get-tuple-element.30), channel_id=1, source_target_pairs={{32,0},{64,32},{96,64},{128,96},{160,128},{192,160},{224,192},{33,... | collective-permute-start | bytes 245768 | tf_op jit(solution)/shard_map/ppermute | solution.py:324
  34.8 1.0 copy-done.6
  35.8 1.0 copy-done.9
  36.8 9.9 %shard_map.78.xy = f32[32,16,128]{2,1,0:T(8,128)S(1)} custom-call(f32[3,60,16,128]{3,2,1,0:T(8,128)S(1)} %get-tuple-element.31.own.own_in, f32[3,60,24,128]{3,2,1,0:T(8,128)S(1)} %get-tuple-element.32.theirs.theirs_in, bf16[3,512,256]{2,1,0:T(8,128)(2,1)S(1)} %get-tuple-element.33.a1, bf16[3,256,256]{2,1,0:T(8,128)(2,1)S(1)} %copy-done.6, ...), custom_call_target="tpu_custom_call" | custom-call | flops 12000000000 | bytes 1048576 | tf_op jit(solution)/shard_map/pallas_call | solution.py:326
  46.8 14.7 %shard_map.79 = (f32[32,16,128]{2,1,0:T(8,128)S(1)}, bf16[64,1024]{1,0:T(8,128)(2,1)S(1)}, f32[3,60,16,128]{3,2,1,0:T(8,128)S(1)}, f32[3,60,24,128]{3,2,1,0:T(8,128)S(1)}) custom-call(s32[1]{0:T(128)} %bitcast.core, f32[40,16,128]{2,1,0:T(8,128)S(1)} %get-tuple-element.27.vol, ...), custom_call_target="tpu_custom_call", output_to_operand_aliasing={{2}: (8, {}), {3}: (9, {})} | custom-call | flops 24000000000 | bytes 1048576 | tf_op jit(solution)/shard_map/pallas_call | solution.py:329
  61.5 1.6 %shard_map.80 = bf16[16,8,1024]{2,1,0:T(8,128)(2,1)} custom-call(bf16[64,1024]{1,0:T(8,128)(2,1)S(1)} %get-tuple-element.36.image, bf16[2,512,2048]{2,1,0:T(8,128)(2,1)S(1)} %copy-done.1), custom_call_target="tpu_custom_call" | custom-call | flops 300000000 | bytes 5242880 | tf_op jit(solution)/shard_map/pallas_call | solution.py:344
  63.1 6.9 %all-to-all-start.1 = ((bf16[16,8,1024]{2,1,0:T(8,128)(2,1)}), bf16[16,8,1024]{2,1,0:T(8,128)(2,1)S(1)}, u32[]{:S(2)}, u32[]{:S(2)}) async-start(bf16[16,8,1024]{2,1,0:T(8,128)(2,1)} %shard_map.80), calls=%async_computation.1 | async-start | bytes 524288 | tf_op jit(solution)/shard_map/all_to_all | solution.py:352
  70.1 10.2 %all-to-all-done.1.parts = bf16[16,8,1024]{2,1,0:T(8,128)(2,1)S(1)} async-done(((bf16[16,8,1024]{2,1,0:T(8,128)(2,1)}), bf16[16,8,1024]{2,1,0:T(8,128)(2,1)S(1)}, u32[]{:S(2)}, u32[]{:S(2)}) %all-to-all-start.1) | async-done | bytes 262176 | tf_op jit(solution)/shard_map/all_to_all | solution.py:352
  80.3 14.9 %all_to_all.15.misfit = bf16[16,8,1024]{2,1,0:T(8,128)(2,1)S(1)} all-to-all(bf16[16,8,1024]{2,1,0:T(8,128)(2,1)S(1)} %shard_map.81), channel_id=1, replica_groups=mesh['space'=8,'q'=16,'c'=2] {'q'}, dimensions={0} | all-to-all | bytes 524288 | tf_op jit(solution)/shard_map/all_to_all | solution.py:356
  95.2 2.1 %shard_map.82 = (f32[64,512]{1,0:T(8,128)S(1)}, bf16[64,2048]{1,0:T(8,128)(2,1)S(1)}) custom-call(s32[1]{0:T(128)} %bitcast.core, bf16[16,8,1024]{2,1,0:T(8,128)(2,1)S(1)} %all_to_all.15.misfit, bf16[2048,512]{1,0:T(8,128)(2,1)} %collective-permute-done.pair, f32[32,16,128]{2,1,0:T(8,128)S(1)} %get-tuple-element.38.cons), custom_call_target="tpu_custom_call" | custom-call | flops 150000000 | bytes 3145728 | tf_op jit(solution)/shard_map/pallas_call | solution.py:357
  97.3 3.5 %collective-permute-start.4 = (f32[64,512]{1,0:T(8,128)S(1)}, f32[64,512]{1,0:T(8,128)S(1)}, u32[]{:S(2)}, u32[]{:S(2)}) collective-permute-start(f32[64,512]{1,0:T(8,128)S(1)} %get-tuple-element.40), channel_id=1, source_target_pairs={{0,1},{1,0},{2,3},{3,2},{4,5},{5,4},{6,7},{7,6},{8,9},{9,8},{10,11... | collective-permute-start | bytes 393224 | tf_op jit(solution)/shard_map/ppermute | solution.py:365
  101.8 0.8 shard_map.84
  (32 shorter events, 5.6 us)
Async XLA Ops:
  0.0 18.8 %copy-start.2 = (bf16[2048,512]{1,0:T(8,128)(2,1)S(1)}, bf16[2048,512]{1,0:T(8,128)(2,1)}, u32[]{:S(2)}) copy-start(bf16[2048,512]{1,0:T(8,128)(2,1)} %own.3) | copy-start | bytes 6291460
  0.0 18.8 %collective-permute-start = (bf16[2048,512]{1,0:T(8,128)(2,1)}, bf16[2048,512]{1,0:T(8,128)(2,1)}, u32[]{:S(2)}, u32[]{:S(2)}) collective-permute-start(bf16[2048,512]{1,0:T(8,128)(2,1)} %own.3), channel_id=1, source_target_pairs={{0,1},{1,0},{2,3},{3,2},{4,5},{5,4},{6,7},{7,6},{8,9},{9,8},{10,11... | collective-permute-start | bytes 6291464 | tf_op jit(solution)/shard_map/ppermute | solution.py:285
  0.7 0.9 copy-start.3
  2.4 22.7 %all-to-all-start = ((f32[16,40,128]{2,1,0:T(8,128)}), f32[16,40,128]{2,1,0:T(8,128)S(1)}, u32[]{:S(2)}, u32[]{:S(2)}) async-start(f32[16,40,128]{2,1,0:T(8,128)} %shard_map.73), calls=%async_computation | async-start | bytes 655360 | tf_op jit(solution)/shard_map/all_to_all | solution.py:283
  15.6 0.8 copy-start.4
  17.2 0.8 copy-start.5
  18.0 0.8 copy-start.8
  22.0 1.9 %copy-start = (bf16[2,512,2048]{2,1,0:T(8,128)(2,1)}, bf16[2,512,2048]{2,1,0:T(8,128)(2,1)S(1)}, u32[]{:S(2)}) copy-start(bf16[2,512,2048]{2,1,0:T(8,128)(2,1)S(1)} %shard_map.75.pixels) | copy-start | bytes 12582916
  25.1 2.8 %collective-permute-start.1 = (bf16[40,16,128]{2,1,0:T(8,128)(2,1)S(1)}, bf16[40,16,128]{2,1,0:T(8,128)(2,1)S(1)}, u32[]{:S(2)}, u32[]{:S(2)}) collective-permute-start(bf16[40,16,128]{2,1,0:T(8,128)(2,1)S(1)} %get-tuple-element.28), channel_id=1, source_target_pairs={{0,1},{1,0},{2,3},{3,2},{4,5},{5,4},{6,7},{7,6},{8,9},{9,8},{10,11... | collective-permute-start | bytes 491528 | tf_op jit(solution)/shard_map/ppermute | solution.py:312
  28.6 18.1 %collective-permute-start.2 = (bf16[20,16,128]{2,1,0:T(8,128)(2,1)S(1)}, bf16[20,16,128]{2,1,0:T(8,128)(2,1)S(1)}, u32[]{:S(2)}, u32[]{:S(2)}) collective-permute-start(bf16[20,16,128]{2,1,0:T(8,128)(2,1)S(1)} %get-tuple-element.29), channel_id=1, source_target_pairs={{0,32},{32,64},{64,96},{96,128},{128,160},{160,192},{192,224},{1,3... | collective-permute-start | bytes 245768 | tf_op jit(solution)/shard_map/ppermute | solution.py:323
  30.9 15.8 %collective-permute-start.3 = (bf16[20,16,128]{2,1,0:T(8,128)(2,1)S(1)}, bf16[20,16,128]{2,1,0:T(8,128)(2,1)S(1)}, u32[]{:S(2)}, u32[]{:S(2)}) collective-permute-start(bf16[20,16,128]{2,1,0:T(8,128)(2,1)S(1)} %get-tuple-element.30), channel_id=1, source_target_pairs={{32,0},{64,32},{96,64},{128,96},{160,128},{192,160},{224,192},{33,... | collective-permute-start | bytes 245768 | tf_op jit(solution)/shard_map/ppermute | solution.py:324
  34.8 1.0 copy-start.6
  35.8 1.0 copy-start.9
  36.8 10.0 %copy-start.7 = (bf16[3,256,256]{2,1,0:T(8,128)(2,1)S(1)}, bf16[3,256,256]{2,1,0:T(8,128)(2,1)}, u32[]{:S(2)}) copy-start(bf16[3,256,256]{2,1,0:T(8,128)(2,1)} %copy-done.5) | copy-start | bytes 1179652
  46.7 14.8 %copy-start.1 = (bf16[2,512,2048]{2,1,0:T(8,128)(2,1)S(1)}, bf16[2,512,2048]{2,1,0:T(8,128)(2,1)}, u32[]{:S(2)}) copy-start(bf16[2,512,2048]{2,1,0:T(8,128)(2,1)} %copy-done) | copy-start | bytes 12582916
  61.5 8.5 %copy-start.10 = (f32[1,4,2048]{2,1,0:T(4,128)S(1)}, f32[1,4,2048]{2,1,0:T(4,128)}, u32[]{:S(2)}) copy-start(f32[1,4,2048]{2,1,0:T(4,128)} %param.13) | copy-start | bytes 98308
  63.1 17.1 %all-to-all-start.1 = ((bf16[16,8,1024]{2,1,0:T(8,128)(2,1)}), bf16[16,8,1024]{2,1,0:T(8,128)(2,1)S(1)}, u32[]{:S(2)}, u32[]{:S(2)}) async-start(bf16[16,8,1024]{2,1,0:T(8,128)(2,1)} %shard_map.80), calls=%async_computation.1 | async-start | bytes 524288 | tf_op jit(solution)/shard_map/all_to_all | solution.py:352
  97.3 4.5 %collective-permute-start.4 = (f32[64,512]{1,0:T(8,128)S(1)}, f32[64,512]{1,0:T(8,128)S(1)}, u32[]{:S(2)}, u32[]{:S(2)}) collective-permute-start(f32[64,512]{1,0:T(8,128)S(1)} %get-tuple-element.40), channel_id=1, source_target_pairs={{0,1},{1,0},{2,3},{3,2},{4,5},{5,4},{6,7},{7,6},{8,9},{9,8},{10,11... | collective-permute-start | bytes 393224 | tf_op jit(solution)/shard_map/ppermute | solution.py:365

commit v4 on v2

v4 whole, which is shorter than its diff:
```python
import jax
import jax.numpy as jnp
from jax import lax
from jax.experimental import pallas as pl
from jax.experimental.pallas import tpu as pltpu
from jax.sharding import Mesh, PartitionSpec as P

F32, BF16 = jnp.float32, jnp.bfloat16
VM = pl.BlockSpec(memory_space=pltpu.VMEM)
SM = pl.BlockSpec(memory_space=pltpu.SMEM)
SWAP = [(0, 1), (1, 0)]


def call(kernel, outs, scratch=(), specs=None, flops=0, nbytes=0, vmem=24, aliases=None):
    return pl.pallas_call(
        kernel,
        out_shape=outs,
        in_specs=specs,
        out_specs=jax.tree.map(lambda _: VM, outs),
        scratch_shapes=list(scratch),
        input_output_aliases=aliases or {},
        compiler_params=pltpu.CompilerParams(vmem_limit_bytes=vmem << 20),
        cost_estimate=pl.CostEstimate(flops=flops, bytes_accessed=nbytes, transcendentals=0),
    )


def shaped(shape, dtype):
    return jax.ShapeDtypeStruct(shape, dtype)


def iota(shape, dim):
    return lax.broadcasted_iota(jnp.int32, shape, dim)


def weights_kernel(lift, bias, mix, outw, a1, a2, a3):
    spread = (iota((256, 64), 0) >> 2 == iota((256, 64), 1)).astype(F32)
    spread_t = (iota((64, 256), 1) >> 2 == iota((64, 256), 0)).astype(F32).astype(BF16)
    taps = (iota((27, 256), 1) >> 3 == iota((27, 256), 0)).astype(F32).astype(BF16)
    row, col = iota((256, 256), 0) & 3, iota((256, 256), 1)
    tap = col >> 3

    def column(values):
        return jnp.sum(spread * values, axis=1, keepdims=True)

    for k in range(3):
        full = bias[k : k + 1, :]
        high = full.astype(BF16).astype(F32)
        mid = (full - high).astype(BF16).astype(F32)
        low = full - high - mid
        base = jnp.dot(spread.astype(BF16), lift[k], preferred_element_type=F32).astype(BF16)
        base = jnp.dot(base, taps, preferred_element_type=F32)
        for at, part in ((27, high), (28, mid), (29, low)):
            base = jnp.where(tap == at, column(part), base)
        for half in range(2):
            a1[k, half * 256 : half * 256 + 256] = jnp.where(
                row + 4 * half == (col & 7), base, 0.0
            ).astype(BF16)
        mixed = jnp.dot(spread.astype(BF16), mix[k], preferred_element_type=F32).astype(BF16)
        mixed = jnp.dot(mixed, spread_t, preferred_element_type=F32)
        a2[k] = jnp.where(row == (col & 3), mixed, 0.0).astype(BF16)
        a3[k] = jnp.broadcast_to(column(outw[...].astype(F32)[k : k + 1, :]), (256, 128))


def spread_plane(s, t, z, plane):
    zero = jnp.zeros((8, 128), F32)
    lane = iota((8, 128), 1)
    for dy in range(3):
        s[t, z, dy, 0:8] = zero
        s[t, z, dy, 136:144] = zero
    for j in range(8):
        pair = plane[16 * j : 16 * j + 16].astype(F32)
        for i in range(2):
            v = pair[8 * i : 8 * i + 8]
            at = slice(16 * j + 8 * i + 8, 16 * j + 8 * i + 16)
            s[t, z, 0, at] = jnp.where(lane == 0, 0.0, pltpu.roll(v, 1, 1))
            s[t, z, 1, at] = v
            s[t, z, 2, at] = jnp.where(lane == 127, 0.0, pltpu.roll(v, 127, 1))


def spread_kernel(core, mine, near, next_, s, first, last):
    c = core[0]
    for i, ref in enumerate((mine, near, next_)):
        first[i] = ref[0]
        last[i] = ref[3]

    def step(z, carry):
        spread_plane(s, 1, z + 1, mine[z])
        spread_plane(s, 2 - 2 * c, z + 1, near[z])
        spread_plane(s, 2 * c, z + 1, next_[z])
        return carry

    lax.fori_loop(0, 4, step, 0)


OFFSETS = (
    [(dt, 1, db, da) for dt in range(3) for da in range(3) for db in range(3)],
    [(dt, db, da, 1) for dt in range(3) for da in range(3) for db in range(3)],
    [(dt, da, 1, db) for dt in range(3) for da in range(3) for db in range(3)],
)


def corrected(s, a1, a2, a3, which, z, block):
    rows = []
    for dt, dz, dy, dx in OFFSETS[which]:
        at = 7 + dx + 16 * block
        rows.append(
            jnp.concatenate(
                [s[dt, z + dz, dy, at : at + 8], s[dt, z + dz, dy, at + 8 : at + 16]], axis=1
            )
        )
    rows.append(jnp.ones((24, 256), F32))
    rows.append(jnp.zeros((16, 256), F32))
    taps = jnp.concatenate(rows, axis=0).astype(BF16)
    first = jnp.dot(a1[which], taps, preferred_element_type=F32)
    first = jnp.maximum(first, 0.0).astype(BF16)
    w = a3[which]
    w = jnp.concatenate([w, w], axis=1)
    sums = []
    for half in range(2):
        second = jnp.dot(
            a2[which], first[half * 256 : half * 256 + 256], preferred_element_type=F32
        )
        second = jnp.maximum(second, 0.0) * w
        total = jnp.sum(second.reshape(32, 8, 256), axis=0)
        sums.append(total + pltpu.roll(total, 4, 0))
    return jnp.where(iota((8, 256), 0) < 4, sums[0], sums[1])


def xy_kernel(s, a1, a2, a3, out):
    def step(i, carry):
        for z in (2 * i, 2 * i + 1):
            for block in range(8):
                got = corrected(s, a1, a2, a3, 0, z, block)
                out[2 * block, z] = got[:, :128]
                out[2 * block + 1, z] = got[:, 128:]
        return carry

    lax.fori_loop(0, 2, step, 0)


def rest_kernel(core, vol, before, after, xy, a1, a2, a3, s_in, cons, s):
    c = core[0]
    for i, t in enumerate((1, 2 - 2 * c, 2 * c)):
        spread_plane(s, t, 0, before[i])
        spread_plane(s, t, 5, after[i])

    def step(z, carry):
        for block in range(8):
            got = corrected(s, a1, a2, a3, 1, z, block)
            got = got + corrected(s, a1, a2, a3, 2, z, block)
            for j in range(2):
                at = 2 * block + j
                total = xy[at, z] + got[:, 128 * j : 128 * j + 128]
                cons[at, z] = vol[z, 8 * at : 8 * at + 8] + total / 3.0
        return carry

    lax.fori_loop(0, 4, step, 0)


def transpose_kernel(core, own, pair, out):
    c = core[0]

    def step(j, carry):
        rays = pl.ds(pl.multiple_of(256 * j, 256), 256)
        out[c, :, rays] = own[rays, :].T
        out[1 - c, :, rays] = pair[rays, :].T
        return carry

    lax.fori_loop(0, 8, step, 0)


def project_kernel(blocks, pixels, out, cons, image, turned):
    for z in range(4):
        for x in range(8):
            got = blocks[pl.ds(z * 8 + x, 16, stride=32), :]
            cons[z * 8 + x] = got
            image[16 * z : 16 * z + 16, 128 * x : 128 * x + 128] = got.astype(BF16)
    for j in range(8):
        rays = slice(256 * j, 256 * j + 256)
        got = jnp.dot(image[:, 0:512], pixels[0, :, rays], preferred_element_type=F32)
        got = got + jnp.dot(image[:, 512:1024], pixels[1, :, rays], preferred_element_type=F32)
        for z in range(4):
            for n in range(2):
                turned[2 * (j % 4) + n, pl.ds(z * 2 + j // 4, 16, stride=8), :] = got[
                    16 * z : 16 * z + 16, 128 * n : 128 * n + 128
                ]
    for n in range(8):
        lanes = slice(128 * n, 128 * n + 128)
        for t in range(16):
            out[t, :, lanes] = turned[n, 8 * t : 8 * t + 8].astype(BF16)


def misfit_kernel(parts, measured, out):
    total = parts[0].astype(F32)
    for t in range(1, 16):
        total = total + parts[t].astype(F32)
    misfit = (total - measured[...]).astype(BF16)
    for t in range(16):
        out[t] = misfit


def far_kernel(core, misfit, pair, cons, far, rows, turned):
    for n in range(8):
        for t in range(16):
            turned[n, 8 * t : 8 * t + 8] = misfit[t, :, 128 * n : 128 * n + 128].astype(F32)
    for z in range(4):
        for half in range(2):
            for n in range(8):
                rows[16 * z : 16 * z + 16, 1024 * half + 128 * n : 1024 * half + 128 * n + 128] = (
                    turned[n, pl.ds(z * 2 + half, 16, stride=8), :].astype(BF16)
                )
    got = jnp.dot(rows[...], pair[...], preferred_element_type=F32)
    stepped(1 - core[0], cons, got, far)


def stepped(c, cons, gradient, out):
    for z in range(4):
        for x in range(4):
            at = (slice(16 * z, 16 * z + 16), slice(128 * x, 128 * x + 128))
            out[at] = cons[z * 8 + x + 4 * c] - gradient[at]


def near_kernel(core, rows, own, cons, near):
    got = jnp.dot(rows[...], own[...], preferred_element_type=F32)
    stepped(core[0], cons, got, near)


def merge_kernel(core, near, far, out, turned):
    def write(parity, rows):
        for z in range(4):
            for x in range(4):
                turned[x, pl.ds(4 * parity + z, 16, stride=8), :] = rows[
                    16 * z : 16 * z + 16, 128 * x : 128 * x + 128
                ]

    @pl.when(core[0] == 0)
    def _():
        write(0, near)
        write(1, far)

    @pl.when(core[0] == 1)
    def _():
        write(1, near)
        write(0, far)

    for x in range(4):
        for t in range(32):
            out[t, :, 128 * x : 128 * x + 128] = turned[x, 4 * t : 4 * t + 4]


def shards(volume, lift_weights, lift_bias, mix_weights, out_weights, projector, measured):
    core = lax.axis_index("c").reshape(1)
    coarse = volume[0].astype(BF16)
    near = lax.ppermute(coarse, "c", SWAP)
    up = [(2 * i + 1, 2 * i + 2) for i in range(15)]
    next_ = lax.ppermute(coarse, ("q", "c"), up + [(j, i) for i, j in up])
    pair = lax.ppermute(projector, "c", SWAP)

    a1, a2, a3 = call(
        weights_kernel,
        (shaped((3, 512, 256), BF16), shaped((3, 256, 256), BF16), shaped((3, 256, 128), F32)),
        specs=[VM] * 4,
        flops=10**8,
        nbytes=1 << 20,
    )(lift_weights, lift_bias, mix_weights, out_weights)
    planes, plane = shaped((3, 6, 3, 144, 128), F32), shaped((3, 128, 128), BF16)
    s, first, last = call(
        spread_kernel, (planes, plane, plane), specs=[SM] + [VM] * 3, nbytes=8 << 20
    )(core, coarse, near, next_)
    up = [(i, i + 1) for i in range(7)]
    before = lax.ppermute(last, "space", up)
    after = lax.ppermute(first, "space", [(j, i) for i, j in up])

    blocks = shaped((16, 4, 8, 128), F32)
    xy = call(xy_kernel, blocks, specs=[VM] * 4, flops=12 * 10**9, nbytes=1 << 20)(s, a1, a2, a3)
    consensus, _ = call(
        rest_kernel,
        (blocks, planes),
        specs=[SM] + [VM] * 8,
        flops=24 * 10**9,
        nbytes=1 << 20,
        aliases={8: 1},
    )(core, volume[0], before, after, xy, a1, a2, a3, s)
    frames = lax.all_to_all(
        consensus.reshape(16, 32, 128), "q", split_axis=0, concat_axis=0, tiled=True
    )
    pixels = call(
        transpose_kernel,
        shaped((2, 512, 2048), BF16),
        specs=[SM, VM, VM],
        nbytes=8 << 20,
    )(core, projector, pair)

    partial, cons = call(
        project_kernel,
        (shaped((16, 8, 1024), BF16), shaped((32, 16, 128), F32)),
        [pltpu.VMEM((64, 1024), BF16), pltpu.VMEM((8, 128, 128), F32)],
        [VM] * 2,
        flops=3 * 10**8,
        nbytes=5 << 20,
    )(frames.reshape(512, 128), pixels)
    parts = lax.all_to_all(partial, "q", split_axis=0, concat_axis=0, tiled=True)
    misfit = call(misfit_kernel, shaped((16, 8, 1024), BF16), specs=[VM] * 2)(
        parts, measured.reshape(8, 1024)
    )
    misfit = lax.all_to_all(misfit, "q", split_axis=0, concat_axis=0, tiled=True)
    far, rows = call(
        far_kernel,
        (shaped((64, 512), F32), shaped((64, 2048), BF16)),
        [pltpu.VMEM((8, 128, 128), F32)],
        [SM] + [VM] * 3,
        flops=15 * 10**7,
        nbytes=3 << 20,
    )(core, misfit, pair, cons)
    far = lax.ppermute(far, "c", SWAP)
    near = call(
        near_kernel,
        shaped((64, 512), F32),
        specs=[SM] + [VM] * 3,
        flops=15 * 10**7,
        nbytes=3 << 20,
    )(core, rows, projector, cons)
    return call(
        merge_kernel,
        shaped((32, 4, 512), F32),
        [pltpu.VMEM((4, 128, 128), F32)],
        [SM] + [VM] * 2,
    )(core, near, far)


def solution(mesh):
    fine = Mesh(mesh.devices.reshape(8, 16, 2), ("space", "q", "c"))
    tm = ("q", "c")
    placed = (
        P(tm, "space", None, None),
        P(),
        P(),
        P(),
        P(),
        P(None, tm),
        P(tm, "space", None),
    )
    return jax.shard_map(
        shards, mesh=fine, in_specs=placed, out_specs=P(None, "space", tm), check_vma=False
    )
```

time: 108 us -> 94 us (0.87)
  Pallas kernels: 41.4 us -> 26.1 us
  waiting for transfers between devices: 20.4 us -> 14.7 us
  local copies, waits for them, and re-layouts: 2.76 us -> 7.16 us
  starting transfers between devices: 26.6 us -> 28 us
    pallas_call x6 -> x4, Pallas kernels: 33.9 us -> 18.5 us  [the longest x1 11.3 us: shards(): call(rest_kernel, (blocks, planes), specs=[SM] + [VM] * 8, flops=24 * 10...]
    unnamed x10 -> x17, local copies, waits for them, and re-layouts: 0.98 us -> 7.14 us
    all_to_all x1, waiting for transfers between devices: 8.97 us -> 4.51 us  [shards(): lax.all_to_all(consensus.reshape(16, 32, 128), 'q', split_axis=0, concat_...]
    all_to_all x1, starting transfers between devices: 4.07 us -> 5.96 us  [shards(): lax.all_to_all(partial, 'q', split_axis=0, concat_axis=0, tiled=True)]
    ppermute x1 -> x2, starting transfers between devices: 2.88 us -> 4.21 us  [the longest x1 3.44 us: shards(): next_ = lax.ppermute(coarse, ('q', 'c'), up + [(j, i) for i, j in up])]
    all_to_all x1, waiting for transfers between devices: 10.9 us -> 9.66 us  [shards(): lax.all_to_all(partial, 'q', split_axis=0, concat_axis=0, tiled=True)]
    ppermute x1, starting transfers between devices: 1.24 us -> 0.1 us  [shards(): pair = lax.ppermute(projector, 'c', SWAP)]
  transfers between devices with their start and end apart: 7 -> 8, of which waited for: 3 -> 3; matrix products, arithmetic and copies ran while one was open for 2% -> 1% of each run, Pallas kernels for 31% -> 23%
where the time goes in v4:
time: 94 us; the launch traced here: 92.6 us
  starting transfers between devices  28 us (30%)
  Pallas kernels  26.1 us (28%)
  blocking collectives  15.4 us (16%)
  waiting for transfers between devices  14.7 us (16%)
  local copies, waits for them, and re-layouts  7.16 us (8%)
  other arithmetic  0.97 us (1%)
    all_to_all x1, blocking collectives, shards(): lax.all_to_all(misfit, 'q', split_axis=0, concat_axis=0, tiled=True)  15.4 us
    pallas_call x1, Pallas kernels, shards(): call(rest_kernel, (blocks, planes), specs=[SM] + [VM] * 8, flops=24 * 10...  11.3 us
    all_to_all x1, waiting for transfers between devices, shards(): lax.all_to_all(partial, 'q', split_axis=0, concat_axis=0, tiled=True)  9.66 us
    all_to_all x1, starting transfers between devices, shards(): lax.all_to_all(consensus.reshape(16, 32, 128), 'q', split_axis=0, concat_...  9.03 us
    unnamed x17, local copies, waits for them, and re-layouts  7.14 us
    all_to_all x1, starting transfers between devices, shards(): lax.all_to_all(partial, 'q', split_axis=0, concat_axis=0, tiled=True)  5.96 us
    pallas_call x1, Pallas kernels, shards(): call(xy_kernel, blocks, specs=[VM] * 4, flops=12 * 10 ** 9, nbytes=1 << 20)  5.1 us
    all_to_all x1, waiting for transfers between devices, shards(): lax.all_to_all(consensus.reshape(16, 32, 128), 'q', split_axis=0, concat_...  4.51 us
  transfers between devices with their start and end apart: 8, of which 3 were waited for; matrix products, arithmetic and copies ran while one was open for 1% of the time, Pallas kernels for 23%

profile of v4, /device:TPU:41, one launch (start us, length us, event | category | flops | bytes accessed | tf_op | source)
XLA Modules:
  0.0 92.6 jit_solution(15868551659779544961)
XLA Ops:
  0.0 1.0 %bitcast_convert_fusion.mine = bf16[4,128,128]{2,1,0:T(8,128)(2,1)S(1)} fusion(f32[1,4,128,128]{3,2,1,0:T(8,128)} %param.7), kind=kLoop, calls=%fused_computation | loop fusion | flops 65536 | bytes 393216 | tf_op jit(solution)/shard_map/convert_element_type | solution.py:253
  1.0 0.8 collective-permute-start
  1.7 3.4 %collective-permute-start.1 = (bf16[4,128,128]{2,1,0:T(8,128)(2,1)S(1)}, bf16[4,128,128]{2,1,0:T(8,128)(2,1)S(1)}, u32[]{:S(2)}, u32[]{:S(2)}) collective-permute-start(bf16[4,128,128]{2,1,0:T(8,128)(2,1)S(1)} %bitcast_convert_fusion.mine), channel_id=1, source_target_pairs={{1,2},{3,4},{5,6},{7,8},{9,10},{11,12},{13,14},{15,16},{17,18},{19... | collective-permute-start | bytes 393224 | tf_op jit(solution)/shard_map/ppermute | solution.py:256
  5.3 0.9 copy.9.lift
  6.2 0.8 copy-done.4
  7.0 0.7 copy-done.5
  7.6 0.7 copy-done.6
  8.3 0.9 %shard_map.74 = (bf16[3,512,256]{2,1,0:T(8,128)(2,1)S(1)}, bf16[3,256,256]{2,1,0:T(8,128)(2,1)S(1)}, f32[3,256,128]{2,1,0:T(8,128)S(1)}) custom-call(bf16[3,64,27]{2,1,0:T(8,128)(2,1)S(1)} %copy.9.lift, f32[3,64]{1,0:T(4,128)S(1)} %copy-done.5, bf16[3,64,64]{2,1,0:T(8,128)(2,1)S(1)} %copy-done.4, bf16[3,64]{1,0:T(4,128)(2,1)S(1)} %copy-done.6), custom_call_target="tpu_custom_call" | custom-call | flops 100000000 | bytes 1048576 | tf_op jit(solution)/shard_map/pallas_call | solution.py:259
  9.8 3.0 %collective-permute-start.2 = (bf16[3,128,128]{2,1,0:T(8,128)(2,1)S(1)}, bf16[3,128,128]{2,1,0:T(8,128)(2,1)S(1)}, u32[]{:S(2)}, u32[]{:S(2)}) collective-permute-start(bf16[3,128,128]{2,1,0:T(8,128)(2,1)S(1)} %get-tuple-element.16), channel_id=1, source_target_pairs={{0,32},{32,64},{64,96},{96,128},{128,160},{160,192},{192,224},{1,3... | collective-permute-start | bytes 294920 | tf_op jit(solution)/shard_map/ppermute | solution.py:271
  12.8 2.3 %collective-permute-start.3 = (bf16[3,128,128]{2,1,0:T(8,128)(2,1)S(1)}, bf16[3,128,128]{2,1,0:T(8,128)(2,1)S(1)}, u32[]{:S(2)}, u32[]{:S(2)}) collective-permute-start(bf16[3,128,128]{2,1,0:T(8,128)(2,1)S(1)} %get-tuple-element.17), channel_id=1, source_target_pairs={{32,0},{64,32},{96,64},{128,96},{160,128},{192,160},{224,192},{33,... | collective-permute-start | bytes 294920 | tf_op jit(solution)/shard_map/ppermute | solution.py:272
  15.1 5.1 %shard_map.75.xy = f32[16,4,8,128]{3,2,1,0:T(8,128)S(1)} custom-call(f32[3,6,3,144,128]{4,3,2,1,0:T(8,128)S(1)} %get-tuple-element.18.s.s_in, bf16[3,512,256]{2,1,0:T(8,128)(2,1)S(1)} %get-tuple-element.19.a1, bf16[3,256,256]{2,1,0:T(8,128)(2,1)S(1)} %get-tuple-element.20.a2, f32[3,256,128]{2,1,0:T(8,128)S(1)} %get-tuple-element.21.a3), custom_call_target="tpu_custom_call" | custom-call | flops 12000000000 | bytes 1048576 | tf_op jit(solution)/shard_map/pallas_call | solution.py:275
  20.3 11.3 %shard_map.76 = (f32[16,4,8,128]{3,2,1,0:T(8,128)}, f32[3,6,3,144,128]{4,3,2,1,0:T(8,128)S(1)}) custom-call(s32[1]{0:T(128)} %bitcast.core, f32[4,128,128]{2,1,0:T(8,128)S(1)} %bitcast.6, bf16[3,128,128]{2,1,0:T(8,128)(2,1)S(1)} %collective-permute-done.2.before, ...), custom_call_target="tpu_custom_call", output_to_operand_aliasing={{1}: (8, {})} | custom-call | flops 24000000000 | bytes 1048576 | tf_op jit(solution)/shard_map/pallas_call | solution.py:276
  31.5 9.0 %all-to-all-start = ((f32[16,32,128]{2,1,0:T(8,128)}), f32[16,32,128]{2,1,0:T(8,128)S(1)}, u32[]{:S(2)}, u32[]{:S(2)}) async-start(f32[16,32,128]{2,1,0:T(8,128)} %bitcast.2), calls=%async_computation | async-start | bytes 524288 | tf_op jit(solution)/shard_map/all_to_all | solution.py:284
  40.6 3.2 %shard_map.77.pixels = bf16[2,512,2048]{2,1,0:T(8,128)(2,1)S(1)} custom-call(s32[1]{0:T(128)} %bitcast.core, bf16[2048,512]{1,0:T(8,128)(2,1)S(1)} %copy-done.2, bf16[2048,512]{1,0:T(8,128)(2,1)} %collective-permute-done.4.pair), custom_call_target="tpu_custom_call" | custom-call | bytes 8388608 | tf_op jit(solution)/shard_map/pallas_call | solution.py:287
  43.8 1.9 %copy-done = bf16[2,512,2048]{2,1,0:T(8,128)(2,1)} copy-done((bf16[2,512,2048]{2,1,0:T(8,128)(2,1)}, bf16[2,512,2048]{2,1,0:T(8,128)(2,1)S(1)}, u32[]{:S(2)}) %copy-start) | copy-done | bytes 4194328
  45.7 4.5 %all-to-all-done = f32[16,32,128]{2,1,0:T(8,128)S(1)} async-done(((f32[16,32,128]{2,1,0:T(8,128)}), f32[16,32,128]{2,1,0:T(8,128)S(1)}, u32[]{:S(2)}, u32[]{:S(2)}) %all-to-all-start) | async-done | bytes 262176 | tf_op jit(solution)/shard_map/all_to_all | solution.py:284
  50.3 2.2 %copy-done.1 = bf16[2,512,2048]{2,1,0:T(8,128)(2,1)S(1)} copy-done((bf16[2,512,2048]{2,1,0:T(8,128)(2,1)S(1)}, bf16[2,512,2048]{2,1,0:T(8,128)(2,1)}, u32[]{:S(2)}) %copy-start.1) | copy-done | bytes 4194328
  52.4 1.6 %shard_map.78 = (bf16[16,8,1024]{2,1,0:T(8,128)(2,1)}, f32[32,16,128]{2,1,0:T(8,128)S(1)}) custom-call(f32[512,128]{1,0:T(8,128)S(1)} %bitcast.5, bf16[2,512,2048]{2,1,0:T(8,128)(2,1)S(1)} %copy-done.1), custom_call_target="tpu_custom_call" | custom-call | flops 300000000 | bytes 5242880 | tf_op jit(solution)/shard_map/pallas_call | solution.py:294
  54.1 6.0 %all-to-all-start.1 = ((bf16[16,8,1024]{2,1,0:T(8,128)(2,1)}), bf16[16,8,1024]{2,1,0:T(8,128)(2,1)S(1)}, u32[]{:S(2)}, u32[]{:S(2)}) async-start(bf16[16,8,1024]{2,1,0:T(8,128)(2,1)} %get-tuple-element.23), calls=%async_computation.1 | async-start | bytes 524288 | tf_op jit(solution)/shard_map/all_to_all | solution.py:302
  60.1 9.7 %all-to-all-done.1.parts = bf16[16,8,1024]{2,1,0:T(8,128)(2,1)S(1)} async-done(((bf16[16,8,1024]{2,1,0:T(8,128)(2,1)}), bf16[16,8,1024]{2,1,0:T(8,128)(2,1)S(1)}, u32[]{:S(2)}, u32[]{:S(2)}) %all-to-all-start.1) | async-done | bytes 262176 | tf_op jit(solution)/shard_map/all_to_all | solution.py:302
  69.8 15.4 %all_to_all.15.misfit = bf16[16,8,1024]{2,1,0:T(8,128)(2,1)S(1)} all-to-all(bf16[16,8,1024]{2,1,0:T(8,128)(2,1)S(1)} %shard_map.79), channel_id=1, replica_groups=mesh['space'=8,'q'=16,'c'=2] {'q'}, dimensions={0} | all-to-all | bytes 524288 | tf_op jit(solution)/shard_map/all_to_all | solution.py:306
  85.2 2.1 %shard_map.80 = (f32[64,512]{1,0:T(8,128)S(1)}, bf16[64,2048]{1,0:T(8,128)(2,1)S(1)}) custom-call(s32[1]{0:T(128)} %bitcast.core, bf16[16,8,1024]{2,1,0:T(8,128)(2,1)S(1)} %all_to_all.15.misfit, bf16[2048,512]{1,0:T(8,128)(2,1)} %collective-permute-done.4.pair, f32[32,16,128]{2,1,0:T(8,128)S(1)} %get-tuple-element.24.cons), custom_call_target="tpu_custom_call" | custom-call | flops 150000000 | bytes 3145728 | tf_op jit(solution)/shard_map/pallas_call | solution.py:307
  87.3 3.5 %collective-permute-start.5 = (f32[64,512]{1,0:T(8,128)S(1)}, f32[64,512]{1,0:T(8,128)S(1)}, u32[]{:S(2)}, u32[]{:S(2)}) collective-permute-start(f32[64,512]{1,0:T(8,128)S(1)} %get-tuple-element.26), channel_id=1, source_target_pairs={{0,1},{1,0},{2,3},{3,2},{4,5},{5,4},{6,7},{7,6},{8,9},{9,8},{10,11... | collective-permute-start | bytes 393224 | tf_op jit(solution)/shard_map/ppermute | solution.py:315
  91.8 0.8 shard_map.82
  (22 shorter events, 1.7 us)
Async XLA Ops:
  1.0 8.3 %collective-permute-start = (bf16[4,128,128]{2,1,0:T(8,128)(2,1)S(1)}, bf16[4,128,128]{2,1,0:T(8,128)(2,1)S(1)}, u32[]{:S(2)}, u32[]{:S(2)}) collective-permute-start(bf16[4,128,128]{2,1,0:T(8,128)(2,1)S(1)} %bitcast_convert_fusion.mine), channel_id=1, source_target_pairs={{0,1},{1,0},{2,3},{3,2},{4,5},{5,4},{6,7},{7,6},{8,9},{9,8},{10,11... | collective-permute-start | bytes 393224 | tf_op jit(solution)/shard_map/ppermute | solution.py:254
  1.7 7.5 %collective-permute-start.1 = (bf16[4,128,128]{2,1,0:T(8,128)(2,1)S(1)}, bf16[4,128,128]{2,1,0:T(8,128)(2,1)S(1)}, u32[]{:S(2)}, u32[]{:S(2)}) collective-permute-start(bf16[4,128,128]{2,1,0:T(8,128)(2,1)S(1)} %bitcast_convert_fusion.mine), channel_id=1, source_target_pairs={{1,2},{3,4},{5,6},{7,8},{9,10},{11,12},{13,14},{15,16},{17,18},{19... | collective-permute-start | bytes 393224 | tf_op jit(solution)/shard_map/ppermute | solution.py:256
  5.2 35.4 %collective-permute-start.4 = (bf16[2048,512]{1,0:T(8,128)(2,1)}, bf16[2048,512]{1,0:T(8,128)(2,1)}, u32[]{:S(2)}, u32[]{:S(2)}) collective-permute-start(bf16[2048,512]{1,0:T(8,128)(2,1)} %own.3), channel_id=1, source_target_pairs={{0,1},{1,0},{2,3},{3,2},{4,5},{5,4},{6,7},{7,6},{8,9},{9,8},{10,11... | collective-permute-start | bytes 6291464 | tf_op jit(solution)/shard_map/ppermute | solution.py:257
  6.1 0.8 copy-start.4
  6.9 0.7 copy-start.5
  7.6 0.7 copy-start.6
  9.8 10.4 %collective-permute-start.2 = (bf16[3,128,128]{2,1,0:T(8,128)(2,1)S(1)}, bf16[3,128,128]{2,1,0:T(8,128)(2,1)S(1)}, u32[]{:S(2)}, u32[]{:S(2)}) collective-permute-start(bf16[3,128,128]{2,1,0:T(8,128)(2,1)S(1)} %get-tuple-element.16), channel_id=1, source_target_pairs={{0,32},{32,64},{64,96},{96,128},{128,160},{160,192},{192,224},{1,3... | collective-permute-start | bytes 294920 | tf_op jit(solution)/shard_map/ppermute | solution.py:271
  12.8 7.4 %collective-permute-start.3 = (bf16[3,128,128]{2,1,0:T(8,128)(2,1)S(1)}, bf16[3,128,128]{2,1,0:T(8,128)(2,1)S(1)}, u32[]{:S(2)}, u32[]{:S(2)}) collective-permute-start(bf16[3,128,128]{2,1,0:T(8,128)(2,1)S(1)} %get-tuple-element.17), channel_id=1, source_target_pairs={{32,0},{64,32},{96,64},{128,96},{160,128},{192,160},{224,192},{33,... | collective-permute-start | bytes 294920 | tf_op jit(solution)/shard_map/ppermute | solution.py:272
  15.1 5.1 %copy-start.3 = (f32[1,4,128,128]{3,2,1,0:T(8,128)S(1)}, f32[1,4,128,128]{3,2,1,0:T(8,128)}, u32[]{:S(2)}) copy-start(f32[1,4,128,128]{3,2,1,0:T(8,128)} %param.7) | copy-start | bytes 786436
  20.3 20.3 %copy-start.2 = (bf16[2048,512]{1,0:T(8,128)(2,1)S(1)}, bf16[2048,512]{1,0:T(8,128)(2,1)}, u32[]{:S(2)}) copy-start(bf16[2048,512]{1,0:T(8,128)(2,1)} %own.3) | copy-start | bytes 6291460
  31.5 18.7 %all-to-all-start = ((f32[16,32,128]{2,1,0:T(8,128)}), f32[16,32,128]{2,1,0:T(8,128)S(1)}, u32[]{:S(2)}, u32[]{:S(2)}) async-start(f32[16,32,128]{2,1,0:T(8,128)} %bitcast.2), calls=%async_computation | async-start | bytes 524288 | tf_op jit(solution)/shard_map/all_to_all | solution.py:284
  40.6 19.5 %copy-start.7 = (f32[1,4,2048]{2,1,0:T(4,128)S(1)}, f32[1,4,2048]{2,1,0:T(4,128)}, u32[]{:S(2)}) copy-start(f32[1,4,2048]{2,1,0:T(4,128)} %param.13) | copy-start | bytes 98308
  43.8 1.9 %copy-start = (bf16[2,512,2048]{2,1,0:T(8,128)(2,1)}, bf16[2,512,2048]{2,1,0:T(8,128)(2,1)S(1)}, u32[]{:S(2)}) copy-start(bf16[2,512,2048]{2,1,0:T(8,128)(2,1)S(1)} %shard_map.77.pixels) | copy-start | bytes 12582916
  50.2 2.2 %copy-start.1 = (bf16[2,512,2048]{2,1,0:T(8,128)(2,1)S(1)}, bf16[2,512,2048]{2,1,0:T(8,128)(2,1)}, u32[]{:S(2)}) copy-start(bf16[2,512,2048]{2,1,0:T(8,128)(2,1)} %copy-done) | copy-start | bytes 12582916
  54.1 15.6 %all-to-all-start.1 = ((bf16[16,8,1024]{2,1,0:T(8,128)(2,1)}), bf16[16,8,1024]{2,1,0:T(8,128)(2,1)S(1)}, u32[]{:S(2)}, u32[]{:S(2)}) async-start(bf16[16,8,1024]{2,1,0:T(8,128)(2,1)} %get-tuple-element.23), calls=%async_computation.1 | async-start | bytes 524288 | tf_op jit(solution)/shard_map/all_to_all | solution.py:302
  87.3 4.5 %collective-permute-start.5 = (f32[64,512]{1,0:T(8,128)S(1)}, f32[64,512]{1,0:T(8,128)S(1)}, u32[]{:S(2)}, u32[]{:S(2)}) collective-permute-start(f32[64,512]{1,0:T(8,128)S(1)} %get-tuple-element.26), channel_id=1, source_target_pairs={{0,1},{1,0},{2,3},{3,2},{4,5},{5,4},{6,7},{7,6},{8,9},{9,8},{10,11... | collective-permute-start | bytes 393224 | tf_op jit(solution)/shard_map/ppermute | solution.py:315

commit v5 on v4

--- a/solution.py
+++ b/solution.py
@@ -8,7 +8,9 @@
 F32, BF16 = jnp.float32, jnp.bfloat16
 VM = pl.BlockSpec(memory_space=pltpu.VMEM)
 SM = pl.BlockSpec(memory_space=pltpu.SMEM)
+HB = pl.BlockSpec(memory_space=pltpu.HBM)
 SWAP = [(0, 1), (1, 0)]
+NT = (((1,), (1,)), ((), ()))
 
 
 def call(kernel, outs, scratch=(), specs=None, flops=0, nbytes=0, vmem=24, aliases=None):
@@ -32,22 +34,23 @@
     return lax.broadcasted_iota(jnp.int32, shape, dim)
 
 
-def weights_kernel(lift, bias, mix, outw, a1, a2, a3):
+def weights_kernel(matrices, vectors, a1, a2, a3):
     spread = (iota((256, 64), 0) >> 2 == iota((256, 64), 1)).astype(F32)
     spread_t = (iota((64, 256), 1) >> 2 == iota((64, 256), 0)).astype(F32).astype(BF16)
     taps = (iota((27, 256), 1) >> 3 == iota((27, 256), 0)).astype(F32).astype(BF16)
     row, col = iota((256, 256), 0) & 3, iota((256, 256), 1)
     tap = col >> 3
+    spread_b = spread.astype(BF16)
 
     def column(values):
         return jnp.sum(spread * values, axis=1, keepdims=True)
 
     for k in range(3):
-        full = bias[k : k + 1, :]
+        full = vectors[0, k : k + 1]
         high = full.astype(BF16).astype(F32)
         mid = (full - high).astype(BF16).astype(F32)
         low = full - high - mid
-        base = jnp.dot(spread.astype(BF16), lift[k], preferred_element_type=F32).astype(BF16)
+        base = lax.dot_general(spread_b, matrices[k, 64:91], NT, preferred_element_type=F32).astype(BF16)
         base = jnp.dot(base, taps, preferred_element_type=F32)
         for at, part in ((27, high), (28, mid), (29, low)):
             base = jnp.where(tap == at, column(part), base)
@@ -55,10 +58,10 @@
             a1[k, half * 256 : half * 256 + 256] = jnp.where(
                 row + 4 * half == (col & 7), base, 0.0
             ).astype(BF16)
-        mixed = jnp.dot(spread.astype(BF16), mix[k], preferred_element_type=F32).astype(BF16)
+        mixed = jnp.dot(spread_b, matrices[k, 0:64], preferred_element_type=F32).astype(BF16)
         mixed = jnp.dot(mixed, spread_t, preferred_element_type=F32)
         a2[k] = jnp.where(row == (col & 3), mixed, 0.0).astype(BF16)
-        a3[k] = jnp.broadcast_to(column(outw[...].astype(F32)[k : k + 1, :]), (256, 128))
+        a3[k] = jnp.broadcast_to(column(vectors[1, k : k + 1]), (256, 128))
 
 
 def spread_plane(s, t, z, plane):
@@ -77,11 +80,11 @@
             s[t, z, 2, at] = jnp.where(lane == 127, 0.0, pltpu.roll(v, 127, 1))
 
 
-def spread_kernel(core, mine, near, next_, s, first, last):
-    c = core[0]
+def spread_kernel(core, parity, mine, near, next_, s, to_near, to_next):
+    c, odd = core[0], parity[0]
     for i, ref in enumerate((mine, near, next_)):
-        first[i] = ref[0]
-        last[i] = ref[3]
+        to_near[i] = ref[3 - 3 * odd]
+        to_next[i] = ref[3 * odd]
 
     def step(z, carry):
         spread_plane(s, 1, z + 1, mine[z])
@@ -138,11 +141,11 @@
     lax.fori_loop(0, 2, step, 0)
 
 
-def rest_kernel(core, vol, before, after, xy, a1, a2, a3, s_in, cons, s):
-    c = core[0]
+def rest_kernel(core, parity, vol, near, next_, xy, a1, a2, a3, s_in, cons, s):
+    c, odd = core[0], parity[0]
     for i, t in enumerate((1, 2 - 2 * c, 2 * c)):
-        spread_plane(s, t, 0, before[i])
-        spread_plane(s, t, 5, after[i])
+        spread_plane(s, t, 5 - 5 * odd, near[i])
+        spread_plane(s, t, 5 * odd, next_[i])
 
     def step(z, carry):
         for block in range(8):
@@ -162,23 +165,26 @@
 
     def step(j, carry):
         rays = pl.ds(pl.multiple_of(256 * j, 256), 256)
-        out[c, :, rays] = own[rays, :].T
-        out[1 - c, :, rays] = pair[rays, :].T
+        out[j, c] = own[rays, :].T
+        out[j, 1 - c] = pair[rays, :].T
         return carry
 
     lax.fori_loop(0, 8, step, 0)
 
 
-def project_kernel(blocks, pixels, out, cons, image, turned):
+def project_kernel(blocks, pixels, out, cons, image, turned, held, sems):
+    copies = [pltpu.make_async_copy(pixels.at[j], held.at[j], sems.at[j]) for j in range(8)]
+    for copy in copies:
+        copy.start()
     for z in range(4):
         for x in range(8):
             got = blocks[pl.ds(z * 8 + x, 16, stride=32), :]
             cons[z * 8 + x] = got
             image[16 * z : 16 * z + 16, 128 * x : 128 * x + 128] = got.astype(BF16)
     for j in range(8):
-        rays = slice(256 * j, 256 * j + 256)
-        got = jnp.dot(image[:, 0:512], pixels[0, :, rays], preferred_element_type=F32)
-        got = got + jnp.dot(image[:, 512:1024], pixels[1, :, rays], preferred_element_type=F32)
+        copies[j].wait()
+        got = jnp.dot(image[:, 0:512], held[j, 0], preferred_element_type=F32)
+        got = got + jnp.dot(image[:, 512:1024], held[j, 1], preferred_element_type=F32)
         for z in range(4):
             for n in range(2):
                 turned[2 * (j % 4) + n, pl.ds(z * 2 + j // 4, 16, stride=8), :] = got[
@@ -199,7 +205,13 @@
         out[t] = misfit
 
 
-def far_kernel(core, misfit, pair, cons, far, rows, turned):
+def far_kernel(core, misfit, pair, cons, far, rows, turned, held, sems):
+    copies = [
+        pltpu.make_async_copy(pair.at[pl.ds(512 * j, 512)], held.at[j], sems.at[j])
+        for j in range(4)
+    ]
+    for copy in copies:
+        copy.start()
     for n in range(8):
         for t in range(16):
             turned[n, 8 * t : 8 * t + 8] = misfit[t, :, 128 * n : 128 * n + 128].astype(F32)
@@ -209,7 +221,11 @@
                 rows[16 * z : 16 * z + 16, 1024 * half + 128 * n : 1024 * half + 128 * n + 128] = (
                     turned[n, pl.ds(z * 2 + half, 16, stride=8), :].astype(BF16)
                 )
-    got = jnp.dot(rows[...], pair[...], preferred_element_type=F32)
+    got = jnp.zeros((64, 512), F32)
+    for j in range(4):
+        copies[j].wait()
+        left = rows[:, 512 * j : 512 * j + 512]
+        got = got + jnp.dot(left, held[j], preferred_element_type=F32)
     stepped(1 - core[0], cons, got, far)
 
 
@@ -250,6 +266,7 @@
 
 def shards(volume, lift_weights, lift_bias, mix_weights, out_weights, projector, measured):
     core = lax.axis_index("c").reshape(1)
+    parity = (lax.axis_index("space") & 1).reshape(1)
     coarse = volume[0].astype(BF16)
     near = lax.ppermute(coarse, "c", SWAP)
     up = [(2 * i + 1, 2 * i + 2) for i in range(15)]
@@ -259,34 +276,37 @@
     a1, a2, a3 = call(
         weights_kernel,
         (shaped((3, 512, 256), BF16), shaped((3, 256, 256), BF16), shaped((3, 256, 128), F32)),
-        specs=[VM] * 4,
+        specs=[VM] * 2,
         flops=10**8,
         nbytes=1 << 20,
-    )(lift_weights, lift_bias, mix_weights, out_weights)
+    )(
+        jnp.concatenate([mix_weights, lift_weights.transpose(0, 2, 1)], axis=1),
+        jnp.stack([lift_bias, out_weights.astype(F32)]),
+    )
     planes, plane = shaped((3, 6, 3, 144, 128), F32), shaped((3, 128, 128), BF16)
-    s, first, last = call(
-        spread_kernel, (planes, plane, plane), specs=[SM] + [VM] * 3, nbytes=8 << 20
-    )(core, coarse, near, next_)
-    up = [(i, i + 1) for i in range(7)]
-    before = lax.ppermute(last, "space", up)
-    after = lax.ppermute(first, "space", [(j, i) for i, j in up])
+    s, to_near, to_next = call(
+        spread_kernel, (planes, plane, plane), specs=[SM] * 2 + [VM] * 3, nbytes=8 << 20
+    )(core, parity, coarse, near, next_)
+    z_near = lax.ppermute(to_near, "space", [(i, i ^ 1) for i in range(8)])
+    up = [(2 * i + 1, 2 * i + 2) for i in range(3)]
+    z_next = lax.ppermute(to_next, "space", up + [(j, i) for i, j in up])
 
     blocks = shaped((16, 4, 8, 128), F32)
     xy = call(xy_kernel, blocks, specs=[VM] * 4, flops=12 * 10**9, nbytes=1 << 20)(s, a1, a2, a3)
     consensus, _ = call(
         rest_kernel,
         (blocks, planes),
-        specs=[SM] + [VM] * 8,
+        specs=[SM] * 2 + [VM] * 8,
         flops=24 * 10**9,
         nbytes=1 << 20,
-        aliases={8: 1},
-    )(core, volume[0], before, after, xy, a1, a2, a3, s)
+        aliases={9: 1},
+    )(core, parity, volume[0], z_near, z_next, xy, a1, a2, a3, s)
     frames = lax.all_to_all(
         consensus.reshape(16, 32, 128), "q", split_axis=0, concat_axis=0, tiled=True
     )
     pixels = call(
         transpose_kernel,
-        shaped((2, 512, 2048), BF16),
+        shaped((8, 2, 512, 256), BF16),
         specs=[SM, VM, VM],
         nbytes=8 << 20,
     )(core, projector, pair)
@@ -294,10 +314,16 @@
     partial, cons = call(
         project_kernel,
         (shaped((16, 8, 1024), BF16), shaped((32, 16, 128), F32)),
-        [pltpu.VMEM((64, 1024), BF16), pltpu.VMEM((8, 128, 128), F32)],
-        [VM] * 2,
+        [
+            pltpu.VMEM((64, 1024), BF16),
+            pltpu.VMEM((8, 128, 128), F32),
+            pltpu.VMEM((8, 2, 512, 256), BF16),
+            pltpu.SemaphoreType.DMA((8,)),
+        ],
+        [VM, HB],
         flops=3 * 10**8,
         nbytes=5 << 20,
+        vmem=52,
     )(frames.reshape(512, 128), pixels)
     parts = lax.all_to_all(partial, "q", split_axis=0, concat_axis=0, tiled=True)
     misfit = call(misfit_kernel, shaped((16, 8, 1024), BF16), specs=[VM] * 2)(
@@ -307,8 +333,12 @@
     far, rows = call(
         far_kernel,
         (shaped((64, 512), F32), shaped((64, 2048), BF16)),
-        [pltpu.VMEM((8, 128, 128), F32)],
-        [SM] + [VM] * 3,
+        [
+            pltpu.VMEM((8, 128, 128), F32),
+            pltpu.VMEM((4, 512, 512), BF16),
+            pltpu.SemaphoreType.DMA((4,)),
+        ],
+        [SM, VM, HB, VM],
         flops=15 * 10**7,
         nbytes=3 << 20,
     )(core, misfit, pair, cons)

time: 94 us -> 92 us (0.979); the launches traced: 92.6 us -> 91.5 us
  local copies, waits for them, and re-layouts: 7.16 us -> 1.98 us
  other arithmetic: 0.97 us -> 3.17 us
  Pallas kernels: 26.1 us -> 28.1 us
    unnamed x17 -> x8, local copies, waits for them, and re-layouts: 7.14 us -> 1.97 us
    pallas_call x1, Pallas kernels: 1.64 us -> 4.02 us  [shards(): call(project_kernel, (shaped((16, 8, 1024), BF16), shaped((32, 16, 128),...]
    another operation x0 -> x2, other arithmetic: none -> 1.37 us  [shards(): jnp.stack([lift_bias, out_weights.astype(F32)])]
  transfers between devices with their start and end apart: 8 -> 8, of which waited for: 3 -> 3; matrix products, arithmetic and copies ran while one was open for 1% -> 2% of each run, Pallas kernels for 23% -> 23%
where the time goes in v5:
time: 92 us; the launch traced here: 91.5 us
  Pallas kernels  28.1 us (31%)
  starting transfers between devices  27.9 us (30%)
  blocking collectives  15.4 us (17%)
  waiting for transfers between devices  14.8 us (16%)
  other arithmetic  3.17 us (3%)
  local copies, waits for them, and re-layouts  1.98 us (2%)
    all_to_all x1, blocking collectives, shards(): lax.all_to_all(misfit, 'q', split_axis=0, concat_axis=0, tiled=True)  15.4 us
    pallas_call x1, Pallas kernels, shards(): call(rest_kernel, (blocks, planes), specs=[SM] * 2 + [VM] * 8, flops=24 *...  11.3 us
    all_to_all x1, starting transfers between devices, shards(): lax.all_to_all(consensus.reshape(16, 32, 128), 'q', split_axis=0, concat_...  9.84 us
    all_to_all x1, waiting for transfers between devices, shards(): lax.all_to_all(partial, 'q', split_axis=0, concat_axis=0, tiled=True)  9.66 us
    all_to_all x1, starting transfers between devices, shards(): lax.all_to_all(partial, 'q', split_axis=0, concat_axis=0, tiled=True)  5.97 us
    pallas_call x1, Pallas kernels, shards(): call(xy_kernel, blocks, specs=[VM] * 4, flops=12 * 10 ** 9, nbytes=1 << 20)  5.1 us
    all_to_all x1, waiting for transfers between devices, shards(): lax.all_to_all(consensus.reshape(16, 32, 128), 'q', split_axis=0, concat_...  4.6 us
    pallas_call x1, Pallas kernels, shards(): call(project_kernel, (shaped((16, 8, 1024), BF16), shaped((32, 16, 128),...  4.02 us
  transfers between devices with their start and end apart: 8, of which 3 were waited for; matrix products, arithmetic and copies ran while one was open for 2% of the time, Pallas kernels for 23%

profile of v5, /device:TPU:41, one launch (start us, length us, event | category | flops | bytes accessed | tf_op | source)
XLA Modules:
  0.0 91.5 jit_solution(3593871323816445964)
XLA Ops:
  0.0 1.0 %bitcast_convert_fusion.1.mine = bf16[4,128,128]{2,1,0:T(8,128)(2,1)S(1)} fusion(f32[1,4,128,128]{3,2,1,0:T(8,128)} %param.7), kind=kLoop, calls=%fused_computation.3 | loop fusion | flops 65536 | bytes 393216 | tf_op jit(solution)/shard_map/convert_element_type | solution.py:270
  1.0 0.8 collective-permute-start
  1.7 3.4 %collective-permute-start.1 = (bf16[4,128,128]{2,1,0:T(8,128)(2,1)S(1)}, bf16[4,128,128]{2,1,0:T(8,128)(2,1)S(1)}, u32[]{:S(2)}, u32[]{:S(2)}) collective-permute-start(bf16[4,128,128]{2,1,0:T(8,128)(2,1)S(1)} %bitcast_convert_fusion.1.mine), channel_id=1, source_target_pairs={{1,2},{3,4},{5,6},{7,8},{9,10},{11,12},{13,14},{15,16},{17,18},{19... | collective-permute-start | bytes 393224 | tf_op jit(solution)/shard_map/ppermute | solution.py:273
  5.3 0.7 bitcast_convert_fusion
  6.0 0.7 pad_maximum_fusion.1.vectors
  6.7 0.8 pad_maximum_fusion.matrices
  7.5 1.0 %shard_map.74 = (bf16[3,512,256]{2,1,0:T(8,128)(2,1)S(1)}, bf16[3,256,256]{2,1,0:T(8,128)(2,1)S(1)}, f32[3,256,128]{2,1,0:T(8,128)S(1)}) custom-call(bf16[3,91,64]{2,1,0:T(8,128)(2,1)S(1)} %pad_maximum_fusion.matrices, f32[2,3,64]{2,1,0:T(4,128)S(1)} %pad_maximum_fusion.1.vectors), custom_call_target="tpu_custom_call" | custom-call | flops 100000000 | bytes 1048576 | tf_op jit(solution)/shard_map/pallas_call | solution.py:276
  8.5 0.5 shard_map.73
  9.0 0.7 collective-permute-start.2
  9.7 3.7 %collective-permute-start.3 = (bf16[3,128,128]{2,1,0:T(8,128)(2,1)S(1)}, bf16[3,128,128]{2,1,0:T(8,128)(2,1)S(1)}, u32[]{:S(2)}, u32[]{:S(2)}) collective-permute-start(bf16[3,128,128]{2,1,0:T(8,128)(2,1)S(1)} %get-tuple-element.17), channel_id=1, source_target_pairs={{32,64},{96,128},{160,192},{64,32},{128,96},{192,160},{33,65},{97,... | collective-permute-start | bytes 294920 | tf_op jit(solution)/shard_map/ppermute | solution.py:292
  13.4 5.1 %shard_map.75.xy = f32[16,4,8,128]{3,2,1,0:T(8,128)S(1)} custom-call(f32[3,6,3,144,128]{4,3,2,1,0:T(8,128)S(1)} %get-tuple-element.18.s.s_in, bf16[3,512,256]{2,1,0:T(8,128)(2,1)S(1)} %get-tuple-element.19.a1, bf16[3,256,256]{2,1,0:T(8,128)(2,1)S(1)} %get-tuple-element.20.a2, f32[3,256,128]{2,1,0:T(8,128)S(1)} %get-tuple-element.21.a3), custom_call_target="tpu_custom_call" | custom-call | flops 12000000000 | bytes 1048576 | tf_op jit(solution)/shard_map/pallas_call | solution.py:295
  18.5 11.3 %shard_map.76 = (f32[16,4,8,128]{3,2,1,0:T(8,128)}, f32[3,6,3,144,128]{4,3,2,1,0:T(8,128)S(1)}) custom-call(s32[1]{0:T(128)} %bitcast.core, s32[1]{0:T(128)} %bitcast.1.parity, f32[4,128,128]{2,1,0:T(8,128)S(1)} %bitcast.12, bf16[3,128,128]{2,1,0:T(8,128)(2,1)S(1)} %collective-permute-done.2.near, ...), custom_call_target="tpu_custom_call", output_to_operand_aliasing={{1}: (9, {})} | custom-call | flops 24000000000 | bytes 1048576 | tf_op jit(solution)/shard_map/pallas_call | solution.py:296
  29.8 9.8 %all-to-all-start = ((f32[16,32,128]{2,1,0:T(8,128)}), f32[16,32,128]{2,1,0:T(8,128)S(1)}, u32[]{:S(2)}, u32[]{:S(2)}) async-start(f32[16,32,128]{2,1,0:T(8,128)} %bitcast.6), calls=%async_computation | async-start | bytes 524288 | tf_op jit(solution)/shard_map/all_to_all | solution.py:304
  39.7 3.1 %shard_map.77.pixels = bf16[8,2,512,256]{3,2,1,0:T(8,128)(2,1)S(1)} custom-call(s32[1]{0:T(128)} %bitcast.core, bf16[2048,512]{1,0:T(8,128)(2,1)S(1)} %copy-done.1, bf16[2048,512]{1,0:T(8,128)(2,1)} %collective-permute-done.4.pair), custom_call_target="tpu_custom_call" | custom-call | bytes 8388608 | tf_op jit(solution)/shard_map/pallas_call | solution.py:307
  42.8 1.9 %copy-done = bf16[8,2,512,256]{3,2,1,0:T(8,128)(2,1)} copy-done((bf16[8,2,512,256]{3,2,1,0:T(8,128)(2,1)}, bf16[8,2,512,256]{3,2,1,0:T(8,128)(2,1)S(1)}, u32[]{:S(2)}) %copy-start) | copy-done | bytes 4194328
  44.7 4.6 %all-to-all-done = f32[16,32,128]{2,1,0:T(8,128)S(1)} async-done(((f32[16,32,128]{2,1,0:T(8,128)}), f32[16,32,128]{2,1,0:T(8,128)S(1)}, u32[]{:S(2)}, u32[]{:S(2)}) %all-to-all-start) | async-done | bytes 262176 | tf_op jit(solution)/shard_map/all_to_all | solution.py:304
  49.3 4.0 %shard_map.78 = (bf16[16,8,1024]{2,1,0:T(8,128)(2,1)}, f32[32,16,128]{2,1,0:T(8,128)S(1)}) custom-call(f32[512,128]{1,0:T(8,128)S(1)} %bitcast.11, bf16[8,2,512,256]{3,2,1,0:T(8,128)(2,1)} %copy-done), custom_call_target="tpu_custom_call" | custom-call | flops 300000000 | bytes 5242880 | tf_op jit(solution)/shard_map/pallas_call | solution.py:314
  53.4 6.0 %all-to-all-start.1 = ((bf16[16,8,1024]{2,1,0:T(8,128)(2,1)}), bf16[16,8,1024]{2,1,0:T(8,128)(2,1)S(1)}, u32[]{:S(2)}, u32[]{:S(2)}) async-start(bf16[16,8,1024]{2,1,0:T(8,128)(2,1)} %get-tuple-element.23), calls=%async_computation.1 | async-start | bytes 524288 | tf_op jit(solution)/shard_map/all_to_all | solution.py:328
  59.4 9.7 %all-to-all-done.1.parts = bf16[16,8,1024]{2,1,0:T(8,128)(2,1)S(1)} async-done(((bf16[16,8,1024]{2,1,0:T(8,128)(2,1)}), bf16[16,8,1024]{2,1,0:T(8,128)(2,1)S(1)}, u32[]{:S(2)}, u32[]{:S(2)}) %all-to-all-start.1) | async-done | bytes 262176 | tf_op jit(solution)/shard_map/all_to_all | solution.py:328
  69.1 15.4 %all_to_all.15.misfit = bf16[16,8,1024]{2,1,0:T(8,128)(2,1)S(1)} all-to-all(bf16[16,8,1024]{2,1,0:T(8,128)(2,1)S(1)} %shard_map.79), channel_id=1, replica_groups=mesh['space'=8,'q'=16,'c'=2] {'q'}, dimensions={0} | all-to-all | bytes 524288 | tf_op jit(solution)/shard_map/all_to_all | solution.py:332
  84.5 1.8 %shard_map.80 = (f32[64,512]{1,0:T(8,128)S(1)}, bf16[64,2048]{1,0:T(8,128)(2,1)S(1)}) custom-call(s32[1]{0:T(128)} %bitcast.core, bf16[16,8,1024]{2,1,0:T(8,128)(2,1)S(1)} %all_to_all.15.misfit, bf16[2048,512]{1,0:T(8,128)(2,1)} %collective-permute-done.4.pair, f32[32,16,128]{2,1,0:T(8,128)S(1)} %get-tuple-element.24.cons), custom_call_target="tpu_custom_call" | custom-call | flops 150000000 | bytes 3145728 | tf_op jit(solution)/shard_map/pallas_call | solution.py:333
  86.3 3.5 %collective-permute-start.5 = (f32[64,512]{1,0:T(8,128)S(1)}, f32[64,512]{1,0:T(8,128)S(1)}, u32[]{:S(2)}, u32[]{:S(2)}) collective-permute-start(f32[64,512]{1,0:T(8,128)S(1)} %get-tuple-element.26), channel_id=1, source_target_pairs={{0,1},{1,0},{2,3},{3,2},{4,5},{5,4},{6,7},{7,6},{8,9},{9,8},{10,11... | collective-permute-start | bytes 393224 | tf_op jit(solution)/shard_map/ppermute | solution.py:345
  90.2 0.5 collective-permute-done.5.far
  90.7 0.8 shard_map.82
  (16 shorter events, 0.7 us)
Async XLA Ops:
  1.0 7.5 %collective-permute-start = (bf16[4,128,128]{2,1,0:T(8,128)(2,1)S(1)}, bf16[4,128,128]{2,1,0:T(8,128)(2,1)S(1)}, u32[]{:S(2)}, u32[]{:S(2)}) collective-permute-start(bf16[4,128,128]{2,1,0:T(8,128)(2,1)S(1)} %bitcast_convert_fusion.1.mine), channel_id=1, source_target_pairs={{0,1},{1,0},{2,3},{3,2},{4,5},{5,4},{6,7},{7,6},{8,9},{9,8},{10,11... | collective-permute-start | bytes 393224 | tf_op jit(solution)/shard_map/ppermute | solution.py:271
  1.7 6.7 %collective-permute-start.1 = (bf16[4,128,128]{2,1,0:T(8,128)(2,1)S(1)}, bf16[4,128,128]{2,1,0:T(8,128)(2,1)S(1)}, u32[]{:S(2)}, u32[]{:S(2)}) collective-permute-start(bf16[4,128,128]{2,1,0:T(8,128)(2,1)S(1)} %bitcast_convert_fusion.1.mine), channel_id=1, source_target_pairs={{1,2},{3,4},{5,6},{7,8},{9,10},{11,12},{13,14},{15,16},{17,18},{19... | collective-permute-start | bytes 393224 | tf_op jit(solution)/shard_map/ppermute | solution.py:273
  5.2 34.5 %collective-permute-start.4 = (bf16[2048,512]{1,0:T(8,128)(2,1)}, bf16[2048,512]{1,0:T(8,128)(2,1)}, u32[]{:S(2)}, u32[]{:S(2)}) collective-permute-start(bf16[2048,512]{1,0:T(8,128)(2,1)} %own.3), channel_id=1, source_target_pairs={{0,1},{1,0},{2,3},{3,2},{4,5},{5,4},{6,7},{7,6},{8,9},{9,8},{10,11... | collective-permute-start | bytes 6291464 | tf_op jit(solution)/shard_map/ppermute | solution.py:274
  9.0 9.5 %collective-permute-start.2 = (bf16[3,128,128]{2,1,0:T(8,128)(2,1)S(1)}, bf16[3,128,128]{2,1,0:T(8,128)(2,1)S(1)}, u32[]{:S(2)}, u32[]{:S(2)}) collective-permute-start(bf16[3,128,128]{2,1,0:T(8,128)(2,1)S(1)} %get-tuple-element.16), channel_id=1, source_target_pairs={{0,32},{32,0},{64,96},{96,64},{128,160},{160,128},{192,224},{224,1... | collective-permute-start | bytes 294920 | tf_op jit(solution)/shard_map/ppermute | solution.py:290
  9.7 8.8 %collective-permute-start.3 = (bf16[3,128,128]{2,1,0:T(8,128)(2,1)S(1)}, bf16[3,128,128]{2,1,0:T(8,128)(2,1)S(1)}, u32[]{:S(2)}, u32[]{:S(2)}) collective-permute-start(bf16[3,128,128]{2,1,0:T(8,128)(2,1)S(1)} %get-tuple-element.17), channel_id=1, source_target_pairs={{32,64},{96,128},{160,192},{64,32},{128,96},{192,160},{33,65},{97,... | collective-permute-start | bytes 294920 | tf_op jit(solution)/shard_map/ppermute | solution.py:292
  13.4 5.1 %copy-start.2 = (f32[1,4,128,128]{3,2,1,0:T(8,128)S(1)}, f32[1,4,128,128]{3,2,1,0:T(8,128)}, u32[]{:S(2)}) copy-start(f32[1,4,128,128]{3,2,1,0:T(8,128)} %param.7) | copy-start | bytes 786436
  18.5 21.1 %copy-start.1 = (bf16[2048,512]{1,0:T(8,128)(2,1)S(1)}, bf16[2048,512]{1,0:T(8,128)(2,1)}, u32[]{:S(2)}) copy-start(bf16[2048,512]{1,0:T(8,128)(2,1)} %own.3) | copy-start | bytes 6291460
  29.8 19.5 %all-to-all-start = ((f32[16,32,128]{2,1,0:T(8,128)}), f32[16,32,128]{2,1,0:T(8,128)S(1)}, u32[]{:S(2)}, u32[]{:S(2)}) async-start(f32[16,32,128]{2,1,0:T(8,128)} %bitcast.6), calls=%async_computation | async-start | bytes 524288 | tf_op jit(solution)/shard_map/all_to_all | solution.py:304
  42.8 2.0 %copy-start = (bf16[8,2,512,256]{3,2,1,0:T(8,128)(2,1)}, bf16[8,2,512,256]{3,2,1,0:T(8,128)(2,1)S(1)}, u32[]{:S(2)}) copy-start(bf16[8,2,512,256]{3,2,1,0:T(8,128)(2,1)S(1)} %shard_map.77.pixels) | copy-start | bytes 12582916
  44.7 14.6 %copy-start.3 = (f32[1,4,2048]{2,1,0:T(4,128)S(1)}, f32[1,4,2048]{2,1,0:T(4,128)}, u32[]{:S(2)}) copy-start(f32[1,4,2048]{2,1,0:T(4,128)} %param.13) | copy-start | bytes 98308
  53.4 15.7 %all-to-all-start.1 = ((bf16[16,8,1024]{2,1,0:T(8,128)(2,1)}), bf16[16,8,1024]{2,1,0:T(8,128)(2,1)S(1)}, u32[]{:S(2)}, u32[]{:S(2)}) async-start(bf16[16,8,1024]{2,1,0:T(8,128)(2,1)} %get-tuple-element.23), calls=%async_computation.1 | async-start | bytes 524288 | tf_op jit(solution)/shard_map/all_to_all | solution.py:328
  86.3 4.4 %collective-permute-start.5 = (f32[64,512]{1,0:T(8,128)S(1)}, f32[64,512]{1,0:T(8,128)S(1)}, u32[]{:S(2)}, u32[]{:S(2)}) collective-permute-start(f32[64,512]{1,0:T(8,128)S(1)} %get-tuple-element.26), channel_id=1, source_target_pairs={{0,1},{1,0},{2,3},{3,2},{4,5},{5,4},{6,7},{7,6},{8,9},{9,8},{10,11... | collective-permute-start | bytes 393224 | tf_op jit(solution)/shard_map/ppermute | solution.py:345

commit v6 on v5

--- a/solution.py
+++ b/solution.py
@@ -160,31 +160,36 @@
     lax.fori_loop(0, 4, step, 0)
 
 
-def transpose_kernel(core, own, pair, out):
-    c = core[0]
-
+def transpose_kernel(block, out):
     def step(j, carry):
-        rays = pl.ds(pl.multiple_of(256 * j, 256), 256)
-        out[j, c] = own[rays, :].T
-        out[j, 1 - c] = pair[rays, :].T
+        out[j] = block[pl.ds(pl.multiple_of(256 * j, 256), 256), :].T
         return carry
 
     lax.fori_loop(0, 8, step, 0)
 
 
-def project_kernel(blocks, pixels, out, cons, image, turned, held, sems):
-    copies = [pltpu.make_async_copy(pixels.at[j], held.at[j], sems.at[j]) for j in range(8)]
-    for copy in copies:
+def project_kernel(core, blocks, own, pair, out, cons, image, turned, held, sems):
+    copies = [
+        pltpu.make_async_copy((own, pair)[i % 2].at[i // 2], held.at[i], sems.at[i])
+        for i in range(16)
+    ]
+    for copy in copies[:4]:
         copy.start()
     for z in range(4):
         for x in range(8):
             got = blocks[pl.ds(z * 8 + x, 16, stride=32), :]
             cons[z * 8 + x] = got
-            image[16 * z : 16 * z + 16, 128 * x : 128 * x + 128] = got.astype(BF16)
+            at = (slice(16 * z, 16 * z + 16), slice(128 * (x % 4), 128 * (x % 4) + 128))
+            image[x // 4, at[0], at[1]] = got.astype(BF16)
+    c = core[0]
+    mine, theirs = image[c], image[1 - c]
     for j in range(8):
-        copies[j].wait()
-        got = jnp.dot(image[:, 0:512], held[j, 0], preferred_element_type=F32)
-        got = got + jnp.dot(image[:, 512:1024], held[j, 1], preferred_element_type=F32)
+        for i in (2 * j, 2 * j + 1):
+            if i + 4 < 16:
+                copies[i + 4].start()
+            copies[i].wait()
+        got = jnp.dot(mine, held[2 * j], preferred_element_type=F32)
+        got = got + jnp.dot(theirs, held[2 * j + 1], preferred_element_type=F32)
         for z in range(4):
             for n in range(2):
                 turned[2 * (j % 4) + n, pl.ds(z * 2 + j // 4, 16, stride=8), :] = got[
@@ -271,8 +276,6 @@
     near = lax.ppermute(coarse, "c", SWAP)
     up = [(2 * i + 1, 2 * i + 2) for i in range(15)]
     next_ = lax.ppermute(coarse, ("q", "c"), up + [(j, i) for i, j in up])
-    pair = lax.ppermute(projector, "c", SWAP)
-
     a1, a2, a3 = call(
         weights_kernel,
         (shaped((3, 512, 256), BF16), shaped((3, 256, 256), BF16), shaped((3, 256, 128), F32)),
@@ -287,10 +290,12 @@
     s, to_near, to_next = call(
         spread_kernel, (planes, plane, plane), specs=[SM] * 2 + [VM] * 3, nbytes=8 << 20
     )(core, parity, coarse, near, next_)
+    to_near, later = lax.optimization_barrier((to_near, projector))
     z_near = lax.ppermute(to_near, "space", [(i, i ^ 1) for i in range(8)])
     up = [(2 * i + 1, 2 * i + 2) for i in range(3)]
     z_next = lax.ppermute(to_next, "space", up + [(j, i) for i, j in up])
 
+    pair = lax.ppermute(later, "c", SWAP)
     blocks = shaped((16, 4, 8, 128), F32)
     xy = call(xy_kernel, blocks, specs=[VM] * 4, flops=12 * 10**9, nbytes=1 << 20)(s, a1, a2, a3)
     consensus, _ = call(
@@ -304,27 +309,25 @@
     frames = lax.all_to_all(
         consensus.reshape(16, 32, 128), "q", split_axis=0, concat_axis=0, tiled=True
     )
-    pixels = call(
-        transpose_kernel,
-        shaped((8, 2, 512, 256), BF16),
-        specs=[SM, VM, VM],
-        nbytes=8 << 20,
-    )(core, projector, pair)
+    turned = [
+        call(transpose_kernel, shaped((8, 512, 256), BF16), specs=[VM], nbytes=4 << 20)(block)
+        for block in (pair, projector)
+    ]
 
     partial, cons = call(
         project_kernel,
         (shaped((16, 8, 1024), BF16), shaped((32, 16, 128), F32)),
         [
-            pltpu.VMEM((64, 1024), BF16),
+            pltpu.VMEM((2, 64, 512), BF16),
             pltpu.VMEM((8, 128, 128), F32),
-            pltpu.VMEM((8, 2, 512, 256), BF16),
-            pltpu.SemaphoreType.DMA((8,)),
+            pltpu.VMEM((16, 512, 256), BF16),
+            pltpu.SemaphoreType.DMA((16,)),
         ],
-        [VM, HB],
+        [SM, VM, HB, HB],
         flops=3 * 10**8,
         nbytes=5 << 20,
         vmem=52,
-    )(frames.reshape(512, 128), pixels)
+    )(core, frames.reshape(512, 128), turned[1], turned[0])
     parts = lax.all_to_all(partial, "q", split_axis=0, concat_axis=0, tiled=True)
     misfit = call(misfit_kernel, shaped((16, 8, 1024), BF16), specs=[VM] * 2)(
         parts, measured.reshape(8, 1024)

time: 92 us -> 95.4 us (1.037)
  Pallas kernels: 28.1 us -> 29.7 us
    pallas_call x1, Pallas kernels: 4.02 us -> 5.26 us  [shards(): call(project_kernel, (shaped((16, 8, 1024), BF16), shaped((32, 16, 128),...]
    all_to_all x1, starting transfers between devices: 9.84 us -> 11 us  [shards(): lax.all_to_all(consensus.reshape(16, 32, 128), 'q', split_axis=0, concat_...]
    unnamed x8 -> x10, local copies, waits for them, and re-layouts: 1.97 us -> 2.67 us
    pallas_call x1 -> x2, Pallas kernels: 3.1 us -> 3.53 us  [shards(): call(transpose_kernel, shaped((8, 512, 256), BF16), specs=[VM], nbytes=4...]
where the time goes in v6:
time: 95.4 us; the launch traced here: 94.5 us
  Pallas kernels  29.7 us (31%)
  starting transfers between devices  28.4 us (30%)
  waiting for transfers between devices  15.5 us (16%)
  blocking collectives  14.9 us (16%)
  other arithmetic  3.17 us (3%)
  local copies, waits for them, and re-layouts  2.69 us (3%)
    all_to_all x1, blocking collectives, shards(): lax.all_to_all(misfit, 'q', split_axis=0, concat_axis=0, tiled=True)  14.9 us
    pallas_call x1, Pallas kernels, shards(): call(rest_kernel, (blocks, planes), specs=[SM] * 2 + [VM] * 8, flops=24 *...  11.3 us
    all_to_all x1, starting transfers between devices, shards(): lax.all_to_all(consensus.reshape(16, 32, 128), 'q', split_axis=0, concat_...  11 us
    all_to_all x1, waiting for transfers between devices, shards(): lax.all_to_all(partial, 'q', split_axis=0, concat_axis=0, tiled=True)  10.2 us
    pallas_call x1, Pallas kernels, shards(): call(project_kernel, (shaped((16, 8, 1024), BF16), shaped((32, 16, 128),...  5.26 us
    pallas_call x1, Pallas kernels, shards(): call(xy_kernel, blocks, specs=[VM] * 4, flops=12 * 10 ** 9, nbytes=1 << 20)  5.09 us
    all_to_all x1, starting transfers between devices, shards(): lax.all_to_all(partial, 'q', split_axis=0, concat_axis=0, tiled=True)  5.06 us
    all_to_all x1, waiting for transfers between devices, shards(): lax.all_to_all(consensus.reshape(16, 32, 128), 'q', split_axis=0, concat_...  4.78 us
  transfers between devices with their start and end apart: 8, of which 3 were waited for; matrix products, arithmetic and copies ran while one was open for 2% of the time, Pallas kernels for 23%

profile of v6, /device:TPU:41, one launch (start us, length us, event | category | flops | bytes accessed | tf_op | source)
XLA Modules:
  0.0 94.5 jit_solution(811221749340335432)
XLA Ops:
  0.0 1.0 %bitcast_convert_fusion.1.mine = bf16[4,128,128]{2,1,0:T(8,128)(2,1)S(1)} fusion(f32[1,4,128,128]{3,2,1,0:T(8,128)} %param.7), kind=kLoop, calls=%fused_computation.3 | loop fusion | flops 65536 | bytes 393216 | tf_op jit(solution)/shard_map/convert_element_type | solution.py:275
  1.0 0.8 collective-permute-start
  1.7 3.4 %collective-permute-start.1 = (bf16[4,128,128]{2,1,0:T(8,128)(2,1)S(1)}, bf16[4,128,128]{2,1,0:T(8,128)(2,1)S(1)}, u32[]{:S(2)}, u32[]{:S(2)}) collective-permute-start(bf16[4,128,128]{2,1,0:T(8,128)(2,1)S(1)} %bitcast_convert_fusion.1.mine), channel_id=1, source_target_pairs={{1,2},{3,4},{5,6},{7,8},{9,10},{11,12},{13,14},{15,16},{17,18},{19... | collective-permute-start | bytes 393224 | tf_op jit(solution)/shard_map/ppermute | solution.py:278
  5.2 0.7 bitcast_convert_fusion
  5.9 0.7 pad_maximum_fusion.1.vectors
  6.6 0.8 pad_maximum_fusion.matrices
  7.4 0.9 shard_map.74
  8.4 0.5 shard_map.73
  9.1 4.1 %collective-permute-start.3 = (bf16[3,128,128]{2,1,0:T(8,128)(2,1)S(1)}, bf16[3,128,128]{2,1,0:T(8,128)(2,1)S(1)}, u32[]{:S(2)}, u32[]{:S(2)}) collective-permute-start(bf16[3,128,128]{2,1,0:T(8,128)(2,1)S(1)} %get-tuple-element.20), channel_id=1, source_target_pairs={{32,64},{96,128},{160,192},{64,32},{128,96},{192,160},{33,65},{97,... | collective-permute-start | bytes 294920 | tf_op jit(solution)/shard_map/ppermute | solution.py:296
  13.6 5.1 %shard_map.75.xy = f32[16,4,8,128]{3,2,1,0:T(8,128)S(1)} custom-call(f32[3,6,3,144,128]{4,3,2,1,0:T(8,128)S(1)} %get-tuple-element.21.s.s_in, bf16[3,512,256]{2,1,0:T(8,128)(2,1)S(1)} %get-tuple-element.22.a1, bf16[3,256,256]{2,1,0:T(8,128)(2,1)S(1)} %get-tuple-element.23.a2, f32[3,256,128]{2,1,0:T(8,128)S(1)} %get-tuple-element.24.a3), custom_call_target="tpu_custom_call" | custom-call | flops 12000000000 | bytes 1048576 | tf_op jit(solution)/shard_map/pallas_call | solution.py:300
  18.7 11.3 %shard_map.76 = (f32[16,4,8,128]{3,2,1,0:T(8,128)}, f32[3,6,3,144,128]{4,3,2,1,0:T(8,128)S(1)}) custom-call(s32[1]{0:T(128)} %bitcast.core, s32[1]{0:T(128)} %bitcast.1.parity, f32[4,128,128]{2,1,0:T(8,128)S(1)} %bitcast.12, bf16[3,128,128]{2,1,0:T(8,128)(2,1)S(1)} %collective-permute-done.2.near, ...), custom_call_target="tpu_custom_call", output_to_operand_aliasing={{1}: (9, {})} | custom-call | flops 24000000000 | bytes 1048576 | tf_op jit(solution)/shard_map/pallas_call | solution.py:301
  30.0 11.0 %all-to-all-start = ((f32[16,32,128]{2,1,0:T(8,128)}), f32[16,32,128]{2,1,0:T(8,128)S(1)}, u32[]{:S(2)}, u32[]{:S(2)}) async-start(f32[16,32,128]{2,1,0:T(8,128)} %bitcast.6), calls=%async_computation | async-start | bytes 524288 | tf_op jit(solution)/shard_map/all_to_all | solution.py:309
  41.0 1.0 %shard_map.77.own = bf16[8,512,256]{2,1,0:T(8,128)(2,1)S(1)} custom-call(bf16[2048,512]{1,0:T(8,128)(2,1)S(1)} %copy-done), custom_call_target="tpu_custom_call" | custom-call | bytes 4194304 | tf_op jit(solution)/shard_map/pallas_call | solution.py:313
  42.0 1.3 %copy-done.1 = bf16[8,512,256]{2,1,0:T(8,128)(2,1)} copy-done((bf16[8,512,256]{2,1,0:T(8,128)(2,1)}, bf16[8,512,256]{2,1,0:T(8,128)(2,1)S(1)}, u32[]{:S(2)}) %copy-start.1) | copy-done | bytes 2097176
  43.3 2.6 %shard_map.78.pair = bf16[8,512,256]{2,1,0:T(8,128)(2,1)S(1)} custom-call(bf16[2048,512]{1,0:T(8,128)(2,1)} %collective-permute-done.4.block.pair), custom_call_target="tpu_custom_call" | custom-call | bytes 4194304 | tf_op jit(solution)/shard_map/pallas_call | solution.py:313
  45.8 1.3 %copy-done.2 = bf16[8,512,256]{2,1,0:T(8,128)(2,1)} copy-done((bf16[8,512,256]{2,1,0:T(8,128)(2,1)}, bf16[8,512,256]{2,1,0:T(8,128)(2,1)S(1)}, u32[]{:S(2)}) %copy-start.2) | copy-done | bytes 2097176
  47.2 4.8 %all-to-all-done = f32[16,32,128]{2,1,0:T(8,128)S(1)} async-done(((f32[16,32,128]{2,1,0:T(8,128)}), f32[16,32,128]{2,1,0:T(8,128)S(1)}, u32[]{:S(2)}, u32[]{:S(2)}) %all-to-all-start) | async-done | bytes 262176 | tf_op jit(solution)/shard_map/all_to_all | solution.py:309
  52.0 5.3 %shard_map.79 = (bf16[16,8,1024]{2,1,0:T(8,128)(2,1)}, f32[32,16,128]{2,1,0:T(8,128)S(1)}) custom-call(s32[1]{0:T(128)} %bitcast.core, f32[512,128]{1,0:T(8,128)S(1)} %bitcast.11, bf16[8,512,256]{2,1,0:T(8,128)(2,1)} %copy-done.1, bf16[8,512,256]{2,1,0:T(8,128)(2,1)} %copy-done.2), custom_call_target="tpu_custom_call" | custom-call | flops 300000000 | bytes 5242880 | tf_op jit(solution)/shard_map/pallas_call | solution.py:317
  57.3 5.1 %all-to-all-start.1 = ((bf16[16,8,1024]{2,1,0:T(8,128)(2,1)}), bf16[16,8,1024]{2,1,0:T(8,128)(2,1)S(1)}, u32[]{:S(2)}, u32[]{:S(2)}) async-start(bf16[16,8,1024]{2,1,0:T(8,128)(2,1)} %get-tuple-element.27), calls=%async_computation.1 | async-start | bytes 524288 | tf_op jit(solution)/shard_map/all_to_all | solution.py:331
  62.3 10.2 %all-to-all-done.1.parts = bf16[16,8,1024]{2,1,0:T(8,128)(2,1)S(1)} async-done(((bf16[16,8,1024]{2,1,0:T(8,128)(2,1)}), bf16[16,8,1024]{2,1,0:T(8,128)(2,1)S(1)}, u32[]{:S(2)}, u32[]{:S(2)}) %all-to-all-start.1) | async-done | bytes 262176 | tf_op jit(solution)/shard_map/all_to_all | solution.py:331
  72.6 14.9 %all_to_all.15.misfit = bf16[16,8,1024]{2,1,0:T(8,128)(2,1)S(1)} all-to-all(bf16[16,8,1024]{2,1,0:T(8,128)(2,1)S(1)} %shard_map.80), channel_id=1, replica_groups=mesh['space'=8,'q'=16,'c'=2] {'q'}, dimensions={0} | all-to-all | bytes 524288 | tf_op jit(solution)/shard_map/all_to_all | solution.py:335
  87.5 1.8 %shard_map.81 = (f32[64,512]{1,0:T(8,128)S(1)}, bf16[64,2048]{1,0:T(8,128)(2,1)S(1)}) custom-call(s32[1]{0:T(128)} %bitcast.core, bf16[16,8,1024]{2,1,0:T(8,128)(2,1)S(1)} %all_to_all.15.misfit, bf16[2048,512]{1,0:T(8,128)(2,1)} %collective-permute-done.4.block.pair, f32[32,16,128]{2,1,0:T(8,128)S(1)} %get-tuple-element.28.cons), custom_call_target="tpu_custom_call" | custom-call | flops 150000000 | bytes 3145728 | tf_op jit(solution)/shard_map/pallas_call | solution.py:336
  89.3 3.5 %collective-permute-start.5 = (f32[64,512]{1,0:T(8,128)S(1)}, f32[64,512]{1,0:T(8,128)S(1)}, u32[]{:S(2)}, u32[]{:S(2)}) collective-permute-start(f32[64,512]{1,0:T(8,128)S(1)} %get-tuple-element.30), channel_id=1, source_target_pairs={{0,1},{1,0},{2,3},{3,2},{4,5},{5,4},{6,7},{7,6},{8,9},{9,8},{10,11... | collective-permute-start | bytes 393224 | tf_op jit(solution)/shard_map/ppermute | solution.py:348
  93.7 0.8 shard_map.83
  (19 shorter events, 1.6 us)
Async XLA Ops:
  1.0 7.4 %collective-permute-start = (bf16[4,128,128]{2,1,0:T(8,128)(2,1)S(1)}, bf16[4,128,128]{2,1,0:T(8,128)(2,1)S(1)}, u32[]{:S(2)}, u32[]{:S(2)}) collective-permute-start(bf16[4,128,128]{2,1,0:T(8,128)(2,1)S(1)} %bitcast_convert_fusion.1.mine), channel_id=1, source_target_pairs={{0,1},{1,0},{2,3},{3,2},{4,5},{5,4},{6,7},{7,6},{8,9},{9,8},{10,11... | collective-permute-start | bytes 393224 | tf_op jit(solution)/shard_map/ppermute | solution.py:276
  1.7 6.6 %collective-permute-start.1 = (bf16[4,128,128]{2,1,0:T(8,128)(2,1)S(1)}, bf16[4,128,128]{2,1,0:T(8,128)(2,1)S(1)}, u32[]{:S(2)}, u32[]{:S(2)}) collective-permute-start(bf16[4,128,128]{2,1,0:T(8,128)(2,1)S(1)} %bitcast_convert_fusion.1.mine), channel_id=1, source_target_pairs={{1,2},{3,4},{5,6},{7,8},{9,10},{11,12},{13,14},{15,16},{17,18},{19... | collective-permute-start | bytes 393224 | tf_op jit(solution)/shard_map/ppermute | solution.py:278
  8.9 9.8 %collective-permute-start.2 = (bf16[3,128,128]{2,1,0:T(8,128)(2,1)S(1)}, bf16[3,128,128]{2,1,0:T(8,128)(2,1)S(1)}, u32[]{:S(2)}, u32[]{:S(2)}) collective-permute-start(bf16[3,128,128]{2,1,0:T(8,128)(2,1)S(1)} %get-tuple-element.19), channel_id=1, source_target_pairs={{0,32},{32,0},{64,96},{96,64},{128,160},{160,128},{192,224},{224,1... | collective-permute-start | bytes 294920 | tf_op jit(solution)/shard_map/ppermute | solution.py:294
  9.1 9.6 %collective-permute-start.3 = (bf16[3,128,128]{2,1,0:T(8,128)(2,1)S(1)}, bf16[3,128,128]{2,1,0:T(8,128)(2,1)S(1)}, u32[]{:S(2)}, u32[]{:S(2)}) collective-permute-start(bf16[3,128,128]{2,1,0:T(8,128)(2,1)S(1)} %get-tuple-element.20), channel_id=1, source_target_pairs={{32,64},{96,128},{160,192},{64,32},{128,96},{192,160},{33,65},{97,... | collective-permute-start | bytes 294920 | tf_op jit(solution)/shard_map/ppermute | solution.py:296
  13.3 30.0 %collective-permute-start.4 = (bf16[2048,512]{1,0:T(8,128)(2,1)}, bf16[2048,512]{1,0:T(8,128)(2,1)}, u32[]{:S(2)}, u32[]{:S(2)}) collective-permute-start(bf16[2048,512]{1,0:T(8,128)(2,1)} %own.1), channel_id=1, source_target_pairs={{0,1},{1,0},{2,3},{3,2},{4,5},{5,4},{6,7},{7,6},{8,9},{9,8},{10,11... | collective-permute-start | bytes 6291464 | tf_op jit(solution)/shard_map/ppermute | solution.py:298
  13.6 5.1 %copy-start.3 = (f32[1,4,128,128]{3,2,1,0:T(8,128)S(1)}, f32[1,4,128,128]{3,2,1,0:T(8,128)}, u32[]{:S(2)}) copy-start(f32[1,4,128,128]{3,2,1,0:T(8,128)} %param.7) | copy-start | bytes 786436
  18.7 22.3 %copy-start = (bf16[2048,512]{1,0:T(8,128)(2,1)S(1)}, bf16[2048,512]{1,0:T(8,128)(2,1)}, u32[]{:S(2)}) copy-start(bf16[2048,512]{1,0:T(8,128)(2,1)} %own.1) | copy-start | bytes 6291460
  30.0 22.0 %all-to-all-start = ((f32[16,32,128]{2,1,0:T(8,128)}), f32[16,32,128]{2,1,0:T(8,128)S(1)}, u32[]{:S(2)}, u32[]{:S(2)}) async-start(f32[16,32,128]{2,1,0:T(8,128)} %bitcast.6), calls=%async_computation | async-start | bytes 524288 | tf_op jit(solution)/shard_map/all_to_all | solution.py:309
  42.0 1.3 %copy-start.1 = (bf16[8,512,256]{2,1,0:T(8,128)(2,1)}, bf16[8,512,256]{2,1,0:T(8,128)(2,1)S(1)}, u32[]{:S(2)}) copy-start(bf16[8,512,256]{2,1,0:T(8,128)(2,1)S(1)} %shard_map.77.own) | copy-start | bytes 6291460
  45.8 1.4 %copy-start.2 = (bf16[8,512,256]{2,1,0:T(8,128)(2,1)}, bf16[8,512,256]{2,1,0:T(8,128)(2,1)S(1)}, u32[]{:S(2)}) copy-start(bf16[8,512,256]{2,1,0:T(8,128)(2,1)S(1)} %shard_map.78.pair) | copy-start | bytes 6291460
  52.0 10.3 %copy-start.4 = (f32[1,4,2048]{2,1,0:T(4,128)S(1)}, f32[1,4,2048]{2,1,0:T(4,128)}, u32[]{:S(2)}) copy-start(f32[1,4,2048]{2,1,0:T(4,128)} %param.13) | copy-start | bytes 98308
  57.3 15.3 %all-to-all-start.1 = ((bf16[16,8,1024]{2,1,0:T(8,128)(2,1)}), bf16[16,8,1024]{2,1,0:T(8,128)(2,1)S(1)}, u32[]{:S(2)}, u32[]{:S(2)}) async-start(bf16[16,8,1024]{2,1,0:T(8,128)(2,1)} %get-tuple-element.27), calls=%async_computation.1 | async-start | bytes 524288 | tf_op jit(solution)/shard_map/all_to_all | solution.py:331
  89.3 4.4 %collective-permute-start.5 = (f32[64,512]{1,0:T(8,128)S(1)}, f32[64,512]{1,0:T(8,128)S(1)}, u32[]{:S(2)}, u32[]{:S(2)}) collective-permute-start(f32[64,512]{1,0:T(8,128)S(1)} %get-tuple-element.30), channel_id=1, source_target_pairs={{0,1},{1,0},{2,3},{3,2},{4,5},{5,4},{6,7},{7,6},{8,9},{9,8},{10,11... | collective-permute-start | bytes 393224 | tf_op jit(solution)/shard_map/ppermute | solution.py:348

commit v7 on v5

--- a/solution.py
+++ b/solution.py
@@ -130,15 +130,11 @@
 
 
 def xy_kernel(s, a1, a2, a3, out):
-    def step(i, carry):
-        for z in (2 * i, 2 * i + 1):
-            for block in range(8):
-                got = corrected(s, a1, a2, a3, 0, z, block)
-                out[2 * block, z] = got[:, :128]
-                out[2 * block + 1, z] = got[:, 128:]
-        return carry
-
-    lax.fori_loop(0, 2, step, 0)
+    for z in range(4):
+        for block in range(8):
+            got = corrected(s, a1, a2, a3, 0, z, block)
+            out[2 * block, z] = got[:, :128]
+            out[2 * block + 1, z] = got[:, 128:]
 
 
 def rest_kernel(core, parity, vol, near, next_, xy, a1, a2, a3, s_in, cons, s):
@@ -147,44 +143,46 @@
         spread_plane(s, t, 5 - 5 * odd, near[i])
         spread_plane(s, t, 5 * odd, next_[i])
 
-    def step(z, carry):
-        for block in range(8):
-            got = corrected(s, a1, a2, a3, 1, z, block)
-            got = got + corrected(s, a1, a2, a3, 2, z, block)
-            for j in range(2):
-                at = 2 * block + j
-                total = xy[at, z] + got[:, 128 * j : 128 * j + 128]
-                cons[at, z] = vol[z, 8 * at : 8 * at + 8] + total / 3.0
+    def step(i, carry):
+        for z in (2 * i, 2 * i + 1):
+            for block in range(8):
+                got = corrected(s, a1, a2, a3, 1, z, block)
+                got = got + corrected(s, a1, a2, a3, 2, z, block)
+                for j in range(2):
+                    at = 2 * block + j
+                    total = xy[at, z] + got[:, 128 * j : 128 * j + 128]
+                    cons[at, z] = vol[z, 8 * at : 8 * at + 8] + total / 3.0
         return carry
 
-    lax.fori_loop(0, 4, step, 0)
-
-
-def transpose_kernel(core, own, pair, out):
-    c = core[0]
-
+    lax.fori_loop(0, 2, step, 0)
+
+
+def transpose_kernel(block, out):
     def step(j, carry):
-        rays = pl.ds(pl.multiple_of(256 * j, 256), 256)
-        out[j, c] = own[rays, :].T
-        out[j, 1 - c] = pair[rays, :].T
+        out[j] = block[pl.ds(pl.multiple_of(256 * j, 256), 256), :].T
         return carry
 
     lax.fori_loop(0, 8, step, 0)
 
 
-def project_kernel(blocks, pixels, out, cons, image, turned, held, sems):
-    copies = [pltpu.make_async_copy(pixels.at[j], held.at[j], sems.at[j]) for j in range(8)]
+def project_kernel(core, blocks, own, pair, out, cons, image, turned, part, held, sems):
+    copies = [pltpu.make_async_copy(pair.at[j], held.at[j], sems.at[j]) for j in range(8)]
     for copy in copies:
         copy.start()
     for z in range(4):
         for x in range(8):
             got = blocks[pl.ds(z * 8 + x, 16, stride=32), :]
             cons[z * 8 + x] = got
-            image[16 * z : 16 * z + 16, 128 * x : 128 * x + 128] = got.astype(BF16)
+            lanes = slice(128 * (x % 4), 128 * (x % 4) + 128)
+            image[x // 4, 16 * z : 16 * z + 16, lanes] = got.astype(BF16)
+    c = core[0]
+    mine, theirs = image[c], image[1 - c]
+    for j in range(8):
+        rays = slice(256 * j, 256 * j + 256)
+        part[j] = lax.dot_general(mine, own[rays], NT, preferred_element_type=F32)
     for j in range(8):
         copies[j].wait()
-        got = jnp.dot(image[:, 0:512], held[j, 0], preferred_element_type=F32)
-        got = got + jnp.dot(image[:, 512:1024], held[j, 1], preferred_element_type=F32)
+        got = part[j] + jnp.dot(theirs, held[j], preferred_element_type=F32)
         for z in range(4):
             for n in range(2):
                 turned[2 * (j % 4) + n, pl.ds(z * 2 + j // 4, 16, stride=8), :] = got[
@@ -304,27 +302,23 @@
     frames = lax.all_to_all(
         consensus.reshape(16, 32, 128), "q", split_axis=0, concat_axis=0, tiled=True
     )
-    pixels = call(
-        transpose_kernel,
-        shaped((8, 2, 512, 256), BF16),
-        specs=[SM, VM, VM],
-        nbytes=8 << 20,
-    )(core, projector, pair)
+    turned = call(transpose_kernel, shaped((8, 512, 256), BF16), specs=[VM], nbytes=4 << 20)(pair)
 
     partial, cons = call(
         project_kernel,
         (shaped((16, 8, 1024), BF16), shaped((32, 16, 128), F32)),
         [
-            pltpu.VMEM((64, 1024), BF16),
+            pltpu.VMEM((2, 64, 512), BF16),
             pltpu.VMEM((8, 128, 128), F32),
-            pltpu.VMEM((8, 2, 512, 256), BF16),
+            pltpu.VMEM((8, 64, 256), F32),
+            pltpu.VMEM((8, 512, 256), BF16),
             pltpu.SemaphoreType.DMA((8,)),
         ],
-        [VM, HB],
+        [SM, VM, VM, HB],
         flops=3 * 10**8,
         nbytes=5 << 20,
-        vmem=52,
-    )(frames.reshape(512, 128), pixels)
+        vmem=48,
+    )(core, frames.reshape(512, 128), projector, turned)
     parts = lax.all_to_all(partial, "q", split_axis=0, concat_axis=0, tiled=True)
     misfit = call(misfit_kernel, shaped((16, 8, 1024), BF16), specs=[VM] * 2)(
         parts, measured.reshape(8, 1024)

time: 92 us -> 91.9 us (level)
  Pallas kernels: 28.1 us -> 25.8 us
  waiting for transfers between devices: 14.8 us -> 15.8 us
  local copies, waits for them, and re-layouts: 1.98 us -> 2.93 us
    all_to_all x1, waiting for transfers between devices: 4.6 us -> 5.64 us  [shards(): lax.all_to_all(consensus.reshape(16, 32, 128), 'q', split_axis=0, concat_...]
    unnamed x8 -> x10, local copies, waits for them, and re-layouts: 1.97 us -> 2.91 us
  transfers between devices with their start and end apart: 8 -> 8, of which waited for: 3 -> 3; matrix products, arithmetic and copies ran while one was open for 2% -> 2% of each run, Pallas kernels for 23% -> 22%
where the time goes in v7:
time: 91.9 us; the launch traced here: 91.4 us
  starting transfers between devices  28.1 us (31%)
  Pallas kernels  25.8 us (28%)
  waiting for transfers between devices  15.8 us (17%)
  blocking collectives  15.4 us (17%)
  other arithmetic  3.17 us (3%)
  local copies, waits for them, and re-layouts  2.93 us (3%)
    all_to_all x1, blocking collectives, shards(): lax.all_to_all(misfit, 'q', split_axis=0, concat_axis=0, tiled=True)  15.4 us
    pallas_call x1, Pallas kernels, shards(): call(rest_kernel, (blocks, planes), specs=[SM] * 2 + [VM] * 8, flops=24 *...  10.5 us
    all_to_all x1, starting transfers between devices, shards(): lax.all_to_all(consensus.reshape(16, 32, 128), 'q', split_axis=0, concat_...  9.84 us
    all_to_all x1, waiting for transfers between devices, shards(): lax.all_to_all(partial, 'q', split_axis=0, concat_axis=0, tiled=True)  9.66 us
    all_to_all x1, starting transfers between devices, shards(): lax.all_to_all(partial, 'q', split_axis=0, concat_axis=0, tiled=True)  5.97 us
    all_to_all x1, waiting for transfers between devices, shards(): lax.all_to_all(consensus.reshape(16, 32, 128), 'q', split_axis=0, concat_...  5.64 us
    pallas_call x1, Pallas kernels, shards(): call(xy_kernel, blocks, specs=[VM] * 4, flops=12 * 10 ** 9, nbytes=1 << 20)  4.75 us
    ppermute x1, starting transfers between devices, shards(): z_next = lax.ppermute(to_next, 'space', up + [(j, i) for i, j in up])  3.89 us
  transfers between devices with their start and end apart: 8, of which 3 were waited for; matrix products, arithmetic and copies ran while one was open for 2% of the time, Pallas kernels for 22%

profile of v7, /device:TPU:41, one launch (start us, length us, event | category | flops | bytes accessed | tf_op | source)
XLA Modules:
  0.0 91.4 jit_solution(9502158508483813856)
XLA Ops:
  0.0 1.0 %bitcast_convert_fusion.1.mine = bf16[4,128,128]{2,1,0:T(8,128)(2,1)S(1)} fusion(f32[1,4,128,128]{3,2,1,0:T(8,128)} %param.7), kind=kLoop, calls=%fused_computation.3 | loop fusion | flops 65536 | bytes 393216 | tf_op jit(solution)/shard_map/convert_element_type | solution.py:268
  1.0 0.8 collective-permute-start
  1.7 3.4 %collective-permute-start.1 = (bf16[4,128,128]{2,1,0:T(8,128)(2,1)S(1)}, bf16[4,128,128]{2,1,0:T(8,128)(2,1)S(1)}, u32[]{:S(2)}, u32[]{:S(2)}) collective-permute-start(bf16[4,128,128]{2,1,0:T(8,128)(2,1)S(1)} %bitcast_convert_fusion.1.mine), channel_id=1, source_target_pairs={{1,2},{3,4},{5,6},{7,8},{9,10},{11,12},{13,14},{15,16},{17,18},{19... | collective-permute-start | bytes 393224 | tf_op jit(solution)/shard_map/ppermute | solution.py:271
  5.3 0.7 bitcast_convert_fusion
  6.0 0.7 pad_maximum_fusion.1.vectors
  6.7 0.8 pad_maximum_fusion.matrices
  7.5 0.9 %shard_map.74 = (bf16[3,512,256]{2,1,0:T(8,128)(2,1)S(1)}, bf16[3,256,256]{2,1,0:T(8,128)(2,1)S(1)}, f32[3,256,128]{2,1,0:T(8,128)S(1)}) custom-call(bf16[3,91,64]{2,1,0:T(8,128)(2,1)S(1)} %pad_maximum_fusion.matrices, f32[2,3,64]{2,1,0:T(4,128)S(1)} %pad_maximum_fusion.1.vectors), custom_call_target="tpu_custom_call" | custom-call | flops 100000000 | bytes 1048576 | tf_op jit(solution)/shard_map/pallas_call | solution.py:274
  8.5 0.5 shard_map.73
  9.0 0.7 collective-permute-start.2
  9.7 3.9 %collective-permute-start.3 = (bf16[3,128,128]{2,1,0:T(8,128)(2,1)S(1)}, bf16[3,128,128]{2,1,0:T(8,128)(2,1)S(1)}, u32[]{:S(2)}, u32[]{:S(2)}) collective-permute-start(bf16[3,128,128]{2,1,0:T(8,128)(2,1)S(1)} %get-tuple-element.17), channel_id=1, source_target_pairs={{32,64},{96,128},{160,192},{64,32},{128,96},{192,160},{33,65},{97,... | collective-permute-start | bytes 294920 | tf_op jit(solution)/shard_map/ppermute | solution.py:290
  13.6 4.8 %shard_map.75.xy = f32[16,4,8,128]{3,2,1,0:T(8,128)S(1)} custom-call(f32[3,6,3,144,128]{4,3,2,1,0:T(8,128)S(1)} %get-tuple-element.18.s.s_in, bf16[3,512,256]{2,1,0:T(8,128)(2,1)S(1)} %get-tuple-element.19.a1, bf16[3,256,256]{2,1,0:T(8,128)(2,1)S(1)} %get-tuple-element.20.a2, f32[3,256,128]{2,1,0:T(8,128)S(1)} %get-tuple-element.21.a3), custom_call_target="tpu_custom_call" | custom-call | flops 12000000000 | bytes 1048576 | tf_op jit(solution)/shard_map/pallas_call | solution.py:293
  18.4 10.5 %shard_map.76 = (f32[16,4,8,128]{3,2,1,0:T(8,128)}, f32[3,6,3,144,128]{4,3,2,1,0:T(8,128)S(1)}) custom-call(s32[1]{0:T(128)} %bitcast.core, s32[1]{0:T(128)} %bitcast.1.parity, f32[4,128,128]{2,1,0:T(8,128)S(1)} %bitcast.12, bf16[3,128,128]{2,1,0:T(8,128)(2,1)S(1)} %collective-permute-done.2.near, ...), custom_call_target="tpu_custom_call", output_to_operand_aliasing={{1}: (9, {})} | custom-call | flops 24000000000 | bytes 1048576 | tf_op jit(solution)/shard_map/pallas_call | solution.py:294
  28.8 9.8 %all-to-all-start = ((f32[16,32,128]{2,1,0:T(8,128)}), f32[16,32,128]{2,1,0:T(8,128)S(1)}, u32[]{:S(2)}, u32[]{:S(2)}) async-start(f32[16,32,128]{2,1,0:T(8,128)} %bitcast.6), calls=%async_computation | async-start | bytes 524288 | tf_op jit(solution)/shard_map/all_to_all | solution.py:302
  38.7 2.7 %shard_map.77.pair = bf16[8,512,256]{2,1,0:T(8,128)(2,1)S(1)} custom-call(bf16[2048,512]{1,0:T(8,128)(2,1)} %collective-permute-done.4.block.pair), custom_call_target="tpu_custom_call" | custom-call | bytes 4194304 | tf_op jit(solution)/shard_map/pallas_call | solution.py:305
  41.4 1.3 %copy-done.1 = bf16[8,512,256]{2,1,0:T(8,128)(2,1)} copy-done((bf16[8,512,256]{2,1,0:T(8,128)(2,1)}, bf16[8,512,256]{2,1,0:T(8,128)(2,1)S(1)}, u32[]{:S(2)}) %copy-start.1) | copy-done | bytes 2097176
  42.7 5.6 %all-to-all-done = f32[16,32,128]{2,1,0:T(8,128)S(1)} async-done(((f32[16,32,128]{2,1,0:T(8,128)}), f32[16,32,128]{2,1,0:T(8,128)S(1)}, u32[]{:S(2)}, u32[]{:S(2)}) %all-to-all-start) | async-done | bytes 262176 | tf_op jit(solution)/shard_map/all_to_all | solution.py:302
  48.4 1.6 %copy-done.2 = bf16[8,512,256]{2,1,0:T(8,128)(2,1)S(1)} copy-done((bf16[8,512,256]{2,1,0:T(8,128)(2,1)S(1)}, bf16[8,512,256]{2,1,0:T(8,128)(2,1)}, u32[]{:S(2)}) %copy-start.2) | copy-done | bytes 2097176
  49.9 3.3 %shard_map.78 = (bf16[16,8,1024]{2,1,0:T(8,128)(2,1)}, f32[32,16,128]{2,1,0:T(8,128)S(1)}) custom-call(s32[1]{0:T(128)} %bitcast.core, f32[512,128]{1,0:T(8,128)S(1)} %bitcast.11, bf16[2048,512]{1,0:T(8,128)(2,1)S(1)} %copy-done, bf16[8,512,256]{2,1,0:T(8,128)(2,1)S(1)} %copy-done.2), custom_call_target="tpu_custom_call" | custom-call | flops 300000000 | bytes 5242880 | tf_op jit(solution)/shard_map/pallas_call | solution.py:307
  53.3 6.0 %all-to-all-start.1 = ((bf16[16,8,1024]{2,1,0:T(8,128)(2,1)}), bf16[16,8,1024]{2,1,0:T(8,128)(2,1)S(1)}, u32[]{:S(2)}, u32[]{:S(2)}) async-start(bf16[16,8,1024]{2,1,0:T(8,128)(2,1)} %get-tuple-element.23), calls=%async_computation.1 | async-start | bytes 524288 | tf_op jit(solution)/shard_map/all_to_all | solution.py:322
  59.3 9.7 %all-to-all-done.1.parts = bf16[16,8,1024]{2,1,0:T(8,128)(2,1)S(1)} async-done(((bf16[16,8,1024]{2,1,0:T(8,128)(2,1)}), bf16[16,8,1024]{2,1,0:T(8,128)(2,1)S(1)}, u32[]{:S(2)}, u32[]{:S(2)}) %all-to-all-start.1) | async-done | bytes 262176 | tf_op jit(solution)/shard_map/all_to_all | solution.py:322
  69.0 15.4 %all_to_all.15.misfit = bf16[16,8,1024]{2,1,0:T(8,128)(2,1)S(1)} all-to-all(bf16[16,8,1024]{2,1,0:T(8,128)(2,1)S(1)} %shard_map.79), channel_id=1, replica_groups=mesh['space'=8,'q'=16,'c'=2] {'q'}, dimensions={0} | all-to-all | bytes 524288 | tf_op jit(solution)/shard_map/all_to_all | solution.py:326
  84.4 1.8 %shard_map.80 = (f32[64,512]{1,0:T(8,128)S(1)}, bf16[64,2048]{1,0:T(8,128)(2,1)S(1)}) custom-call(s32[1]{0:T(128)} %bitcast.core, bf16[16,8,1024]{2,1,0:T(8,128)(2,1)S(1)} %all_to_all.15.misfit, bf16[2048,512]{1,0:T(8,128)(2,1)} %collective-permute-done.4.block.pair, f32[32,16,128]{2,1,0:T(8,128)S(1)} %get-tuple-element.24.cons), custom_call_target="tpu_custom_call" | custom-call | flops 150000000 | bytes 3145728 | tf_op jit(solution)/shard_map/pallas_call | solution.py:327
  86.2 3.5 %collective-permute-start.5 = (f32[64,512]{1,0:T(8,128)S(1)}, f32[64,512]{1,0:T(8,128)S(1)}, u32[]{:S(2)}, u32[]{:S(2)}) collective-permute-start(f32[64,512]{1,0:T(8,128)S(1)} %get-tuple-element.26), channel_id=1, source_target_pairs={{0,1},{1,0},{2,3},{3,2},{4,5},{5,4},{6,7},{7,6},{8,9},{9,8},{10,11... | collective-permute-start | bytes 393224 | tf_op jit(solution)/shard_map/ppermute | solution.py:339
  90.6 0.8 shard_map.82
  (18 shorter events, 1.2 us)
Async XLA Ops:
  1.0 7.5 %collective-permute-start = (bf16[4,128,128]{2,1,0:T(8,128)(2,1)S(1)}, bf16[4,128,128]{2,1,0:T(8,128)(2,1)S(1)}, u32[]{:S(2)}, u32[]{:S(2)}) collective-permute-start(bf16[4,128,128]{2,1,0:T(8,128)(2,1)S(1)} %bitcast_convert_fusion.1.mine), channel_id=1, source_target_pairs={{0,1},{1,0},{2,3},{3,2},{4,5},{5,4},{6,7},{7,6},{8,9},{9,8},{10,11... | collective-permute-start | bytes 393224 | tf_op jit(solution)/shard_map/ppermute | solution.py:269
  1.7 6.7 %collective-permute-start.1 = (bf16[4,128,128]{2,1,0:T(8,128)(2,1)S(1)}, bf16[4,128,128]{2,1,0:T(8,128)(2,1)S(1)}, u32[]{:S(2)}, u32[]{:S(2)}) collective-permute-start(bf16[4,128,128]{2,1,0:T(8,128)(2,1)S(1)} %bitcast_convert_fusion.1.mine), channel_id=1, source_target_pairs={{1,2},{3,4},{5,6},{7,8},{9,10},{11,12},{13,14},{15,16},{17,18},{19... | collective-permute-start | bytes 393224 | tf_op jit(solution)/shard_map/ppermute | solution.py:271
  5.2 33.5 %collective-permute-start.4 = (bf16[2048,512]{1,0:T(8,128)(2,1)}, bf16[2048,512]{1,0:T(8,128)(2,1)}, u32[]{:S(2)}, u32[]{:S(2)}) collective-permute-start(bf16[2048,512]{1,0:T(8,128)(2,1)} %own.3), channel_id=1, source_target_pairs={{0,1},{1,0},{2,3},{3,2},{4,5},{5,4},{6,7},{7,6},{8,9},{9,8},{10,11... | collective-permute-start | bytes 6291464 | tf_op jit(solution)/shard_map/ppermute | solution.py:272
  9.0 9.3 %collective-permute-start.2 = (bf16[3,128,128]{2,1,0:T(8,128)(2,1)S(1)}, bf16[3,128,128]{2,1,0:T(8,128)(2,1)S(1)}, u32[]{:S(2)}, u32[]{:S(2)}) collective-permute-start(bf16[3,128,128]{2,1,0:T(8,128)(2,1)S(1)} %get-tuple-element.16), channel_id=1, source_target_pairs={{0,32},{32,0},{64,96},{96,64},{128,160},{160,128},{192,224},{224,1... | collective-permute-start | bytes 294920 | tf_op jit(solution)/shard_map/ppermute | solution.py:288
  9.7 8.7 %collective-permute-start.3 = (bf16[3,128,128]{2,1,0:T(8,128)(2,1)S(1)}, bf16[3,128,128]{2,1,0:T(8,128)(2,1)S(1)}, u32[]{:S(2)}, u32[]{:S(2)}) collective-permute-start(bf16[3,128,128]{2,1,0:T(8,128)(2,1)S(1)} %get-tuple-element.17), channel_id=1, source_target_pairs={{32,64},{96,128},{160,192},{64,32},{128,96},{192,160},{33,65},{97,... | collective-permute-start | bytes 294920 | tf_op jit(solution)/shard_map/ppermute | solution.py:290
  13.6 4.8 %copy-start.3 = (f32[1,4,128,128]{3,2,1,0:T(8,128)S(1)}, f32[1,4,128,128]{3,2,1,0:T(8,128)}, u32[]{:S(2)}) copy-start(f32[1,4,128,128]{3,2,1,0:T(8,128)} %param.7) | copy-start | bytes 786436
  28.8 19.5 %all-to-all-start = ((f32[16,32,128]{2,1,0:T(8,128)}), f32[16,32,128]{2,1,0:T(8,128)S(1)}, u32[]{:S(2)}, u32[]{:S(2)}) async-start(f32[16,32,128]{2,1,0:T(8,128)} %bitcast.6), calls=%async_computation | async-start | bytes 524288 | tf_op jit(solution)/shard_map/all_to_all | solution.py:302
  38.7 9.7 %copy-start = (bf16[2048,512]{1,0:T(8,128)(2,1)S(1)}, bf16[2048,512]{1,0:T(8,128)(2,1)}, u32[]{:S(2)}) copy-start(bf16[2048,512]{1,0:T(8,128)(2,1)} %own.3) | copy-start | bytes 6291460
  41.4 1.3 %copy-start.1 = (bf16[8,512,256]{2,1,0:T(8,128)(2,1)}, bf16[8,512,256]{2,1,0:T(8,128)(2,1)S(1)}, u32[]{:S(2)}) copy-start(bf16[8,512,256]{2,1,0:T(8,128)(2,1)S(1)} %shard_map.77.pair) | copy-start | bytes 6291460
  48.4 1.6 %copy-start.2 = (bf16[8,512,256]{2,1,0:T(8,128)(2,1)S(1)}, bf16[8,512,256]{2,1,0:T(8,128)(2,1)}, u32[]{:S(2)}) copy-start(bf16[8,512,256]{2,1,0:T(8,128)(2,1)} %copy-done.1) | copy-start | bytes 6291460
  49.9 9.3 %copy-start.4 = (f32[1,4,2048]{2,1,0:T(4,128)S(1)}, f32[1,4,2048]{2,1,0:T(4,128)}, u32[]{:S(2)}) copy-start(f32[1,4,2048]{2,1,0:T(4,128)} %param.13) | copy-start | bytes 98308
  53.3 15.7 %all-to-all-start.1 = ((bf16[16,8,1024]{2,1,0:T(8,128)(2,1)}), bf16[16,8,1024]{2,1,0:T(8,128)(2,1)S(1)}, u32[]{:S(2)}, u32[]{:S(2)}) async-start(bf16[16,8,1024]{2,1,0:T(8,128)(2,1)} %get-tuple-element.23), calls=%async_computation.1 | async-start | bytes 524288 | tf_op jit(solution)/shard_map/all_to_all | solution.py:322
  86.2 4.4 %collective-permute-start.5 = (f32[64,512]{1,0:T(8,128)S(1)}, f32[64,512]{1,0:T(8,128)S(1)}, u32[]{:S(2)}, u32[]{:S(2)}) collective-permute-start(f32[64,512]{1,0:T(8,128)S(1)} %get-tuple-element.26), channel_id=1, source_target_pairs={{0,1},{1,0},{2,3},{3,2},{4,5},{5,4},{6,7},{7,6},{8,9},{9,8},{10,11... | collective-permute-start | bytes 393224 | tf_op jit(solution)/shard_map/ppermute | solution.py:339

commit v8 on v5

--- a/solution.py
+++ b/solution.py
@@ -130,15 +130,11 @@
 
 
 def xy_kernel(s, a1, a2, a3, out):
-    def step(i, carry):
-        for z in (2 * i, 2 * i + 1):
-            for block in range(8):
-                got = corrected(s, a1, a2, a3, 0, z, block)
-                out[2 * block, z] = got[:, :128]
-                out[2 * block + 1, z] = got[:, 128:]
-        return carry
-
-    lax.fori_loop(0, 2, step, 0)
+    for z in range(4):
+        for block in range(8):
+            got = corrected(s, a1, a2, a3, 0, z, block)
+            out[2 * block, z] = got[:, :128]
+            out[2 * block + 1, z] = got[:, 128:]
 
 
 def rest_kernel(core, parity, vol, near, next_, xy, a1, a2, a3, s_in, cons, s):
@@ -147,17 +143,18 @@
         spread_plane(s, t, 5 - 5 * odd, near[i])
         spread_plane(s, t, 5 * odd, next_[i])
 
-    def step(z, carry):
-        for block in range(8):
-            got = corrected(s, a1, a2, a3, 1, z, block)
-            got = got + corrected(s, a1, a2, a3, 2, z, block)
-            for j in range(2):
-                at = 2 * block + j
-                total = xy[at, z] + got[:, 128 * j : 128 * j + 128]
-                cons[at, z] = vol[z, 8 * at : 8 * at + 8] + total / 3.0
+    def step(i, carry):
+        for z in (2 * i, 2 * i + 1):
+            for block in range(8):
+                got = corrected(s, a1, a2, a3, 1, z, block)
+                got = got + corrected(s, a1, a2, a3, 2, z, block)
+                for j in range(2):
+                    at = 2 * block + j
+                    total = xy[at, z] + got[:, 128 * j : 128 * j + 128]
+                    cons[at, z] = vol[z, 8 * at : 8 * at + 8] + total / 3.0
         return carry
 
-    lax.fori_loop(0, 4, step, 0)
+    lax.fori_loop(0, 2, step, 0)
 
 
 def transpose_kernel(core, own, pair, out):
@@ -173,7 +170,11 @@
 
 
 def project_kernel(blocks, pixels, out, cons, image, turned, held, sems):
-    copies = [pltpu.make_async_copy(pixels.at[j], held.at[j], sems.at[j]) for j in range(8)]
+    halves = [pl.ds(4 * i, 4) for i in range(2)]
+    copies = [
+        pltpu.make_async_copy(pixels.at[half], held.at[half], sems.at[i])
+        for i, half in enumerate(halves)
+    ]
     for copy in copies:
         copy.start()
     for z in range(4):
@@ -182,7 +183,8 @@
             cons[z * 8 + x] = got
             image[16 * z : 16 * z + 16, 128 * x : 128 * x + 128] = got.astype(BF16)
     for j in range(8):
-        copies[j].wait()
+        if j % 4 == 0:
+            copies[j // 4].wait()
         got = jnp.dot(image[:, 0:512], held[j, 0], preferred_element_type=F32)
         got = got + jnp.dot(image[:, 512:1024], held[j, 1], preferred_element_type=F32)
         for z in range(4):
@@ -318,7 +320,7 @@
             pltpu.VMEM((64, 1024), BF16),
             pltpu.VMEM((8, 128, 128), F32),
             pltpu.VMEM((8, 2, 512, 256), BF16),
-            pltpu.SemaphoreType.DMA((8,)),
+            pltpu.SemaphoreType.DMA((2,)),
         ],
         [VM, HB],
         flops=3 * 10**8,

time: 92 us -> 90.5 us (0.984)
  Pallas kernels: 28.1 us -> 26.3 us
where the time goes in v8:
time: 90.5 us; the launch traced here: 90 us
  starting transfers between devices  28.1 us (31%)
  Pallas kernels  26.3 us (29%)
  blocking collectives  15.4 us (17%)
  waiting for transfers between devices  14.8 us (16%)
  other arithmetic  3.17 us (4%)
  local copies, waits for them, and re-layouts  1.98 us (2%)
    all_to_all x1, blocking collectives, shards(): lax.all_to_all(misfit, 'q', split_axis=0, concat_axis=0, tiled=True)  15.4 us
    pallas_call x1, Pallas kernels, shards(): call(rest_kernel, (blocks, planes), specs=[SM] * 2 + [VM] * 8, flops=24 *...  10.5 us
    all_to_all x1, starting transfers between devices, shards(): lax.all_to_all(consensus.reshape(16, 32, 128), 'q', split_axis=0, concat_...  9.84 us
    all_to_all x1, waiting for transfers between devices, shards(): lax.all_to_all(partial, 'q', split_axis=0, concat_axis=0, tiled=True)  9.66 us
    all_to_all x1, starting transfers between devices, shards(): lax.all_to_all(partial, 'q', split_axis=0, concat_axis=0, tiled=True)  5.97 us
    pallas_call x1, Pallas kernels, shards(): call(xy_kernel, blocks, specs=[VM] * 4, flops=12 * 10 ** 9, nbytes=1 << 20)  4.75 us
    all_to_all x1, waiting for transfers between devices, shards(): lax.all_to_all(consensus.reshape(16, 32, 128), 'q', split_axis=0, concat_...  4.6 us
    ppermute x1, starting transfers between devices, shards(): z_next = lax.ppermute(to_next, 'space', up + [(j, i) for i, j in up])  3.89 us
  transfers between devices with their start and end apart: 8, of which 3 were waited for; matrix products, arithmetic and copies ran while one was open for 2% of the time, Pallas kernels for 23%

profile of v8, /device:TPU:41, one launch (start us, length us, event | category | flops | bytes accessed | tf_op | source)
XLA Modules:
  0.0 90.0 jit_solution(275821573876530921)
XLA Ops:
  0.0 1.0 %bitcast_convert_fusion.1.mine = bf16[4,128,128]{2,1,0:T(8,128)(2,1)S(1)} fusion(f32[1,4,128,128]{3,2,1,0:T(8,128)} %param.7), kind=kLoop, calls=%fused_computation.3 | loop fusion | flops 65536 | bytes 393216 | tf_op jit(solution)/shard_map/convert_element_type | solution.py:272
  1.0 0.8 collective-permute-start
  1.7 3.4 %collective-permute-start.1 = (bf16[4,128,128]{2,1,0:T(8,128)(2,1)S(1)}, bf16[4,128,128]{2,1,0:T(8,128)(2,1)S(1)}, u32[]{:S(2)}, u32[]{:S(2)}) collective-permute-start(bf16[4,128,128]{2,1,0:T(8,128)(2,1)S(1)} %bitcast_convert_fusion.1.mine), channel_id=1, source_target_pairs={{1,2},{3,4},{5,6},{7,8},{9,10},{11,12},{13,14},{15,16},{17,18},{19... | collective-permute-start | bytes 393224 | tf_op jit(solution)/shard_map/ppermute | solution.py:275
  5.3 0.7 bitcast_convert_fusion
  6.0 0.7 pad_maximum_fusion.1.vectors
  6.7 0.8 pad_maximum_fusion.matrices
  7.5 0.9 %shard_map.74 = (bf16[3,512,256]{2,1,0:T(8,128)(2,1)S(1)}, bf16[3,256,256]{2,1,0:T(8,128)(2,1)S(1)}, f32[3,256,128]{2,1,0:T(8,128)S(1)}) custom-call(bf16[3,91,64]{2,1,0:T(8,128)(2,1)S(1)} %pad_maximum_fusion.matrices, f32[2,3,64]{2,1,0:T(4,128)S(1)} %pad_maximum_fusion.1.vectors), custom_call_target="tpu_custom_call" | custom-call | flops 100000000 | bytes 1048576 | tf_op jit(solution)/shard_map/pallas_call | solution.py:278
  8.5 0.5 shard_map.73
  9.0 0.7 collective-permute-start.2
  9.7 3.9 %collective-permute-start.3 = (bf16[3,128,128]{2,1,0:T(8,128)(2,1)S(1)}, bf16[3,128,128]{2,1,0:T(8,128)(2,1)S(1)}, u32[]{:S(2)}, u32[]{:S(2)}) collective-permute-start(bf16[3,128,128]{2,1,0:T(8,128)(2,1)S(1)} %get-tuple-element.17), channel_id=1, source_target_pairs={{32,64},{96,128},{160,192},{64,32},{128,96},{192,160},{33,65},{97,... | collective-permute-start | bytes 294920 | tf_op jit(solution)/shard_map/ppermute | solution.py:294
  13.6 4.8 %shard_map.75.xy = f32[16,4,8,128]{3,2,1,0:T(8,128)S(1)} custom-call(f32[3,6,3,144,128]{4,3,2,1,0:T(8,128)S(1)} %get-tuple-element.18.s.s_in, bf16[3,512,256]{2,1,0:T(8,128)(2,1)S(1)} %get-tuple-element.19.a1, bf16[3,256,256]{2,1,0:T(8,128)(2,1)S(1)} %get-tuple-element.20.a2, f32[3,256,128]{2,1,0:T(8,128)S(1)} %get-tuple-element.21.a3), custom_call_target="tpu_custom_call" | custom-call | flops 12000000000 | bytes 1048576 | tf_op jit(solution)/shard_map/pallas_call | solution.py:297
  18.4 10.5 %shard_map.76 = (f32[16,4,8,128]{3,2,1,0:T(8,128)}, f32[3,6,3,144,128]{4,3,2,1,0:T(8,128)S(1)}) custom-call(s32[1]{0:T(128)} %bitcast.core, s32[1]{0:T(128)} %bitcast.1.parity, f32[4,128,128]{2,1,0:T(8,128)S(1)} %bitcast.12, bf16[3,128,128]{2,1,0:T(8,128)(2,1)S(1)} %collective-permute-done.2.near, ...), custom_call_target="tpu_custom_call", output_to_operand_aliasing={{1}: (9, {})} | custom-call | flops 24000000000 | bytes 1048576 | tf_op jit(solution)/shard_map/pallas_call | solution.py:298
  28.8 9.8 %all-to-all-start = ((f32[16,32,128]{2,1,0:T(8,128)}), f32[16,32,128]{2,1,0:T(8,128)S(1)}, u32[]{:S(2)}, u32[]{:S(2)}) async-start(f32[16,32,128]{2,1,0:T(8,128)} %bitcast.6), calls=%async_computation | async-start | bytes 524288 | tf_op jit(solution)/shard_map/all_to_all | solution.py:306
  38.7 3.1 %shard_map.77.pixels = bf16[8,2,512,256]{3,2,1,0:T(8,128)(2,1)S(1)} custom-call(s32[1]{0:T(128)} %bitcast.core, bf16[2048,512]{1,0:T(8,128)(2,1)S(1)} %copy-done.1, bf16[2048,512]{1,0:T(8,128)(2,1)} %collective-permute-done.4.pair), custom_call_target="tpu_custom_call" | custom-call | bytes 8388608 | tf_op jit(solution)/shard_map/pallas_call | solution.py:309
  41.8 1.9 %copy-done = bf16[8,2,512,256]{3,2,1,0:T(8,128)(2,1)} copy-done((bf16[8,2,512,256]{3,2,1,0:T(8,128)(2,1)}, bf16[8,2,512,256]{3,2,1,0:T(8,128)(2,1)S(1)}, u32[]{:S(2)}) %copy-start) | copy-done | bytes 4194328
  43.8 4.6 %all-to-all-done = f32[16,32,128]{2,1,0:T(8,128)S(1)} async-done(((f32[16,32,128]{2,1,0:T(8,128)}), f32[16,32,128]{2,1,0:T(8,128)S(1)}, u32[]{:S(2)}, u32[]{:S(2)}) %all-to-all-start) | async-done | bytes 262176 | tf_op jit(solution)/shard_map/all_to_all | solution.py:306
  48.4 3.5 %shard_map.78 = (bf16[16,8,1024]{2,1,0:T(8,128)(2,1)}, f32[32,16,128]{2,1,0:T(8,128)S(1)}) custom-call(f32[512,128]{1,0:T(8,128)S(1)} %bitcast.11, bf16[8,2,512,256]{3,2,1,0:T(8,128)(2,1)} %copy-done), custom_call_target="tpu_custom_call" | custom-call | flops 300000000 | bytes 5242880 | tf_op jit(solution)/shard_map/pallas_call | solution.py:316
  51.8 6.0 %all-to-all-start.1 = ((bf16[16,8,1024]{2,1,0:T(8,128)(2,1)}), bf16[16,8,1024]{2,1,0:T(8,128)(2,1)S(1)}, u32[]{:S(2)}, u32[]{:S(2)}) async-start(bf16[16,8,1024]{2,1,0:T(8,128)(2,1)} %get-tuple-element.23), calls=%async_computation.1 | async-start | bytes 524288 | tf_op jit(solution)/shard_map/all_to_all | solution.py:330
  57.8 9.7 %all-to-all-done.1.parts = bf16[16,8,1024]{2,1,0:T(8,128)(2,1)S(1)} async-done(((bf16[16,8,1024]{2,1,0:T(8,128)(2,1)}), bf16[16,8,1024]{2,1,0:T(8,128)(2,1)S(1)}, u32[]{:S(2)}, u32[]{:S(2)}) %all-to-all-start.1) | async-done | bytes 262176 | tf_op jit(solution)/shard_map/all_to_all | solution.py:330
  67.6 15.4 %all_to_all.15.misfit = bf16[16,8,1024]{2,1,0:T(8,128)(2,1)S(1)} all-to-all(bf16[16,8,1024]{2,1,0:T(8,128)(2,1)S(1)} %shard_map.79), channel_id=1, replica_groups=mesh['space'=8,'q'=16,'c'=2] {'q'}, dimensions={0} | all-to-all | bytes 524288 | tf_op jit(solution)/shard_map/all_to_all | solution.py:334
  83.0 1.8 %shard_map.80 = (f32[64,512]{1,0:T(8,128)S(1)}, bf16[64,2048]{1,0:T(8,128)(2,1)S(1)}) custom-call(s32[1]{0:T(128)} %bitcast.core, bf16[16,8,1024]{2,1,0:T(8,128)(2,1)S(1)} %all_to_all.15.misfit, bf16[2048,512]{1,0:T(8,128)(2,1)} %collective-permute-done.4.pair, f32[32,16,128]{2,1,0:T(8,128)S(1)} %get-tuple-element.24.cons), custom_call_target="tpu_custom_call" | custom-call | flops 150000000 | bytes 3145728 | tf_op jit(solution)/shard_map/pallas_call | solution.py:335
  84.7 3.5 %collective-permute-start.5 = (f32[64,512]{1,0:T(8,128)S(1)}, f32[64,512]{1,0:T(8,128)S(1)}, u32[]{:S(2)}, u32[]{:S(2)}) collective-permute-start(f32[64,512]{1,0:T(8,128)S(1)} %get-tuple-element.26), channel_id=1, source_target_pairs={{0,1},{1,0},{2,3},{3,2},{4,5},{5,4},{6,7},{7,6},{8,9},{9,8},{10,11... | collective-permute-start | bytes 393224 | tf_op jit(solution)/shard_map/ppermute | solution.py:347
  88.7 0.5 collective-permute-done.5.far
  89.2 0.8 shard_map.82
  (16 shorter events, 0.7 us)
Async XLA Ops:
  1.0 7.5 %collective-permute-start = (bf16[4,128,128]{2,1,0:T(8,128)(2,1)S(1)}, bf16[4,128,128]{2,1,0:T(8,128)(2,1)S(1)}, u32[]{:S(2)}, u32[]{:S(2)}) collective-permute-start(bf16[4,128,128]{2,1,0:T(8,128)(2,1)S(1)} %bitcast_convert_fusion.1.mine), channel_id=1, source_target_pairs={{0,1},{1,0},{2,3},{3,2},{4,5},{5,4},{6,7},{7,6},{8,9},{9,8},{10,11... | collective-permute-start | bytes 393224 | tf_op jit(solution)/shard_map/ppermute | solution.py:273
  1.7 6.7 %collective-permute-start.1 = (bf16[4,128,128]{2,1,0:T(8,128)(2,1)S(1)}, bf16[4,128,128]{2,1,0:T(8,128)(2,1)S(1)}, u32[]{:S(2)}, u32[]{:S(2)}) collective-permute-start(bf16[4,128,128]{2,1,0:T(8,128)(2,1)S(1)} %bitcast_convert_fusion.1.mine), channel_id=1, source_target_pairs={{1,2},{3,4},{5,6},{7,8},{9,10},{11,12},{13,14},{15,16},{17,18},{19... | collective-permute-start | bytes 393224 | tf_op jit(solution)/shard_map/ppermute | solution.py:275
  5.2 33.5 %collective-permute-start.4 = (bf16[2048,512]{1,0:T(8,128)(2,1)}, bf16[2048,512]{1,0:T(8,128)(2,1)}, u32[]{:S(2)}, u32[]{:S(2)}) collective-permute-start(bf16[2048,512]{1,0:T(8,128)(2,1)} %own.3), channel_id=1, source_target_pairs={{0,1},{1,0},{2,3},{3,2},{4,5},{5,4},{6,7},{7,6},{8,9},{9,8},{10,11... | collective-permute-start | bytes 6291464 | tf_op jit(solution)/shard_map/ppermute | solution.py:276
  9.0 9.3 %collective-permute-start.2 = (bf16[3,128,128]{2,1,0:T(8,128)(2,1)S(1)}, bf16[3,128,128]{2,1,0:T(8,128)(2,1)S(1)}, u32[]{:S(2)}, u32[]{:S(2)}) collective-permute-start(bf16[3,128,128]{2,1,0:T(8,128)(2,1)S(1)} %get-tuple-element.16), channel_id=1, source_target_pairs={{0,32},{32,0},{64,96},{96,64},{128,160},{160,128},{192,224},{224,1... | collective-permute-start | bytes 294920 | tf_op jit(solution)/shard_map/ppermute | solution.py:292
  9.7 8.7 %collective-permute-start.3 = (bf16[3,128,128]{2,1,0:T(8,128)(2,1)S(1)}, bf16[3,128,128]{2,1,0:T(8,128)(2,1)S(1)}, u32[]{:S(2)}, u32[]{:S(2)}) collective-permute-start(bf16[3,128,128]{2,1,0:T(8,128)(2,1)S(1)} %get-tuple-element.17), channel_id=1, source_target_pairs={{32,64},{96,128},{160,192},{64,32},{128,96},{192,160},{33,65},{97,... | collective-permute-start | bytes 294920 | tf_op jit(solution)/shard_map/ppermute | solution.py:294
  13.6 4.8 %copy-start.2 = (f32[1,4,128,128]{3,2,1,0:T(8,128)S(1)}, f32[1,4,128,128]{3,2,1,0:T(8,128)}, u32[]{:S(2)}) copy-start(f32[1,4,128,128]{3,2,1,0:T(8,128)} %param.7) | copy-start | bytes 786436
  18.4 20.3 %copy-start.1 = (bf16[2048,512]{1,0:T(8,128)(2,1)S(1)}, bf16[2048,512]{1,0:T(8,128)(2,1)}, u32[]{:S(2)}) copy-start(bf16[2048,512]{1,0:T(8,128)(2,1)} %own.3) | copy-start | bytes 6291460
  28.8 19.5 %all-to-all-start = ((f32[16,32,128]{2,1,0:T(8,128)}), f32[16,32,128]{2,1,0:T(8,128)S(1)}, u32[]{:S(2)}, u32[]{:S(2)}) async-start(f32[16,32,128]{2,1,0:T(8,128)} %bitcast.6), calls=%async_computation | async-start | bytes 524288 | tf_op jit(solution)/shard_map/all_to_all | solution.py:306
  41.8 2.0 %copy-start = (bf16[8,2,512,256]{3,2,1,0:T(8,128)(2,1)}, bf16[8,2,512,256]{3,2,1,0:T(8,128)(2,1)S(1)}, u32[]{:S(2)}) copy-start(bf16[8,2,512,256]{3,2,1,0:T(8,128)(2,1)S(1)} %shard_map.77.pixels) | copy-start | bytes 12582916
  43.8 14.1 %copy-start.3 = (f32[1,4,2048]{2,1,0:T(4,128)S(1)}, f32[1,4,2048]{2,1,0:T(4,128)}, u32[]{:S(2)}) copy-start(f32[1,4,2048]{2,1,0:T(4,128)} %param.13) | copy-start | bytes 98308
  51.8 15.7 %all-to-all-start.1 = ((bf16[16,8,1024]{2,1,0:T(8,128)(2,1)}), bf16[16,8,1024]{2,1,0:T(8,128)(2,1)S(1)}, u32[]{:S(2)}, u32[]{:S(2)}) async-start(bf16[16,8,1024]{2,1,0:T(8,128)(2,1)} %get-tuple-element.23), calls=%async_computation.1 | async-start | bytes 524288 | tf_op jit(solution)/shard_map/all_to_all | solution.py:330
  84.7 4.4 %collective-permute-start.5 = (f32[64,512]{1,0:T(8,128)S(1)}, f32[64,512]{1,0:T(8,128)S(1)}, u32[]{:S(2)}, u32[]{:S(2)}) collective-permute-start(f32[64,512]{1,0:T(8,128)S(1)} %get-tuple-element.26), channel_id=1, source_target_pairs={{0,1},{1,0},{2,3},{3,2},{4,5},{5,4},{6,7},{7,6},{8,9},{9,8},{10,11... | collective-permute-start | bytes 393224 | tf_op jit(solution)/shard_map/ppermute | solution.py:347

commit v9 on v8

--- a/solution.py
+++ b/solution.py
@@ -143,18 +143,14 @@
         spread_plane(s, t, 5 - 5 * odd, near[i])
         spread_plane(s, t, 5 * odd, next_[i])
 
-    def step(i, carry):
-        for z in (2 * i, 2 * i + 1):
-            for block in range(8):
-                got = corrected(s, a1, a2, a3, 1, z, block)
-                got = got + corrected(s, a1, a2, a3, 2, z, block)
-                for j in range(2):
-                    at = 2 * block + j
-                    total = xy[at, z] + got[:, 128 * j : 128 * j + 128]
-                    cons[at, z] = vol[z, 8 * at : 8 * at + 8] + total / 3.0
-        return carry
-
-    lax.fori_loop(0, 2, step, 0)
+    for z in range(4):
+        for block in range(8):
+            got = corrected(s, a1, a2, a3, 1, z, block)
+            got = got + corrected(s, a1, a2, a3, 2, z, block)
+            for j in range(2):
+                at = 2 * block + j
+                total = xy[at, z] + got[:, 128 * j : 128 * j + 128]
+                cons[at, z] = vol[z, 8 * at : 8 * at + 8] + total / 3.0
 
 
 def transpose_kernel(core, own, pair, out):
@@ -209,8 +205,8 @@
 
 def far_kernel(core, misfit, pair, cons, far, rows, turned, held, sems):
     copies = [
-        pltpu.make_async_copy(pair.at[pl.ds(512 * j, 512)], held.at[j], sems.at[j])
-        for j in range(4)
+        pltpu.make_async_copy(pair.at[pl.ds(1024 * j, 1024)], held.at[j], sems.at[j])
+        for j in range(2)
     ]
     for copy in copies:
         copy.start()
@@ -224,9 +220,9 @@
                     turned[n, pl.ds(z * 2 + half, 16, stride=8), :].astype(BF16)
                 )
     got = jnp.zeros((64, 512), F32)
-    for j in range(4):
+    for j in range(2):
         copies[j].wait()
-        left = rows[:, 512 * j : 512 * j + 512]
+        left = rows[:, 1024 * j : 1024 * j + 1024]
         got = got + jnp.dot(left, held[j], preferred_element_type=F32)
     stepped(1 - core[0], cons, got, far)
 
@@ -337,8 +333,8 @@
         (shaped((64, 512), F32), shaped((64, 2048), BF16)),
         [
             pltpu.VMEM((8, 128, 128), F32),
-            pltpu.VMEM((4, 512, 512), BF16),
-            pltpu.SemaphoreType.DMA((4,)),
+            pltpu.VMEM((2, 1024, 512), BF16),
+            pltpu.SemaphoreType.DMA((2,)),
         ],
         [SM, VM, HB, VM],
         flops=15 * 10**7,

time: 90.5 us -> 90.8 us (level)
  transfers between devices with their start and end apart: 8 -> 8, of which waited for: 3 -> 3; matrix products, arithmetic and copies ran while one was open for 2% -> 2% of each run, Pallas kernels for 23% -> 22%
where the time goes in v9:
time: 90.8 us; the launch traced here: 90.3 us
  starting transfers between devices  28.1 us (31%)
  Pallas kernels  26.6 us (29%)
  blocking collectives  15.4 us (17%)
  waiting for transfers between devices  14.8 us (16%)
  other arithmetic  3.17 us (3%)
  local copies, waits for them, and re-layouts  1.98 us (2%)
    all_to_all x1, blocking collectives, shards(): lax.all_to_all(misfit, 'q', split_axis=0, concat_axis=0, tiled=True)  15.4 us
    pallas_call x1, Pallas kernels, shards(): call(rest_kernel, (blocks, planes), specs=[SM] * 2 + [VM] * 8, flops=24 *...  10.5 us
    all_to_all x1, starting transfers between devices, shards(): lax.all_to_all(consensus.reshape(16, 32, 128), 'q', split_axis=0, concat_...  9.84 us
    all_to_all x1, waiting for transfers between devices, shards(): lax.all_to_all(partial, 'q', split_axis=0, concat_axis=0, tiled=True)  9.66 us
    all_to_all x1, starting transfers between devices, shards(): lax.all_to_all(partial, 'q', split_axis=0, concat_axis=0, tiled=True)  5.97 us
    pallas_call x1, Pallas kernels, shards(): call(xy_kernel, blocks, specs=[VM] * 4, flops=12 * 10 ** 9, nbytes=1 << 20)  4.75 us
    all_to_all x1, waiting for transfers between devices, shards(): lax.all_to_all(consensus.reshape(16, 32, 128), 'q', split_axis=0, concat_...  4.6 us
    ppermute x1, starting transfers between devices, shards(): z_next = lax.ppermute(to_next, 'space', up + [(j, i) for i, j in up])  3.89 us
  transfers between devices with their start and end apart: 8, of which 3 were waited for; matrix products, arithmetic and copies ran while one was open for 2% of the time, Pallas kernels for 22%

profile of v9, /device:TPU:41, one launch (start us, length us, event | category | flops | bytes accessed | tf_op | source)
XLA Modules:
  0.0 90.3 jit_solution(256241261769438448)
XLA Ops:
  0.0 1.0 %bitcast_convert_fusion.1.mine = bf16[4,128,128]{2,1,0:T(8,128)(2,1)S(1)} fusion(f32[1,4,128,128]{3,2,1,0:T(8,128)} %param.7), kind=kLoop, calls=%fused_computation.3 | loop fusion | flops 65536 | bytes 393216 | tf_op jit(solution)/shard_map/convert_element_type | solution.py:268
  1.0 0.8 collective-permute-start
  1.7 3.4 %collective-permute-start.1 = (bf16[4,128,128]{2,1,0:T(8,128)(2,1)S(1)}, bf16[4,128,128]{2,1,0:T(8,128)(2,1)S(1)}, u32[]{:S(2)}, u32[]{:S(2)}) collective-permute-start(bf16[4,128,128]{2,1,0:T(8,128)(2,1)S(1)} %bitcast_convert_fusion.1.mine), channel_id=1, source_target_pairs={{1,2},{3,4},{5,6},{7,8},{9,10},{11,12},{13,14},{15,16},{17,18},{19... | collective-permute-start | bytes 393224 | tf_op jit(solution)/shard_map/ppermute | solution.py:271
  5.3 0.7 bitcast_convert_fusion
  6.0 0.7 pad_maximum_fusion.1.vectors
  6.7 0.8 pad_maximum_fusion.matrices
  7.5 0.9 %shard_map.74 = (bf16[3,512,256]{2,1,0:T(8,128)(2,1)S(1)}, bf16[3,256,256]{2,1,0:T(8,128)(2,1)S(1)}, f32[3,256,128]{2,1,0:T(8,128)S(1)}) custom-call(bf16[3,91,64]{2,1,0:T(8,128)(2,1)S(1)} %pad_maximum_fusion.matrices, f32[2,3,64]{2,1,0:T(4,128)S(1)} %pad_maximum_fusion.1.vectors), custom_call_target="tpu_custom_call" | custom-call | flops 100000000 | bytes 1048576 | tf_op jit(solution)/shard_map/pallas_call | solution.py:274
  8.5 0.5 shard_map.73
  9.0 0.7 collective-permute-start.2
  9.7 3.9 %collective-permute-start.3 = (bf16[3,128,128]{2,1,0:T(8,128)(2,1)S(1)}, bf16[3,128,128]{2,1,0:T(8,128)(2,1)S(1)}, u32[]{:S(2)}, u32[]{:S(2)}) collective-permute-start(bf16[3,128,128]{2,1,0:T(8,128)(2,1)S(1)} %get-tuple-element.17), channel_id=1, source_target_pairs={{32,64},{96,128},{160,192},{64,32},{128,96},{192,160},{33,65},{97,... | collective-permute-start | bytes 294920 | tf_op jit(solution)/shard_map/ppermute | solution.py:290
  13.6 4.8 %shard_map.75.xy = f32[16,4,8,128]{3,2,1,0:T(8,128)S(1)} custom-call(f32[3,6,3,144,128]{4,3,2,1,0:T(8,128)S(1)} %get-tuple-element.18.s.s_in, bf16[3,512,256]{2,1,0:T(8,128)(2,1)S(1)} %get-tuple-element.19.a1, bf16[3,256,256]{2,1,0:T(8,128)(2,1)S(1)} %get-tuple-element.20.a2, f32[3,256,128]{2,1,0:T(8,128)S(1)} %get-tuple-element.21.a3), custom_call_target="tpu_custom_call" | custom-call | flops 12000000000 | bytes 1048576 | tf_op jit(solution)/shard_map/pallas_call | solution.py:293
  18.4 10.5 %shard_map.76 = (f32[16,4,8,128]{3,2,1,0:T(8,128)}, f32[3,6,3,144,128]{4,3,2,1,0:T(8,128)S(1)}) custom-call(s32[1]{0:T(128)} %bitcast.core, s32[1]{0:T(128)} %bitcast.1.parity, f32[4,128,128]{2,1,0:T(8,128)S(1)} %bitcast.12, bf16[3,128,128]{2,1,0:T(8,128)(2,1)S(1)} %collective-permute-done.2.near, ...), custom_call_target="tpu_custom_call", output_to_operand_aliasing={{1}: (9, {})} | custom-call | flops 24000000000 | bytes 1048576 | tf_op jit(solution)/shard_map/pallas_call | solution.py:294
  28.8 9.8 %all-to-all-start = ((f32[16,32,128]{2,1,0:T(8,128)}), f32[16,32,128]{2,1,0:T(8,128)S(1)}, u32[]{:S(2)}, u32[]{:S(2)}) async-start(f32[16,32,128]{2,1,0:T(8,128)} %bitcast.6), calls=%async_computation | async-start | bytes 524288 | tf_op jit(solution)/shard_map/all_to_all | solution.py:302
  38.7 3.1 %shard_map.77.pixels = bf16[8,2,512,256]{3,2,1,0:T(8,128)(2,1)S(1)} custom-call(s32[1]{0:T(128)} %bitcast.core, bf16[2048,512]{1,0:T(8,128)(2,1)S(1)} %copy-done.1, bf16[2048,512]{1,0:T(8,128)(2,1)} %collective-permute-done.4.pair), custom_call_target="tpu_custom_call" | custom-call | bytes 8388608 | tf_op jit(solution)/shard_map/pallas_call | solution.py:305
  41.8 1.9 %copy-done = bf16[8,2,512,256]{3,2,1,0:T(8,128)(2,1)} copy-done((bf16[8,2,512,256]{3,2,1,0:T(8,128)(2,1)}, bf16[8,2,512,256]{3,2,1,0:T(8,128)(2,1)S(1)}, u32[]{:S(2)}) %copy-start) | copy-done | bytes 4194328
  43.8 4.6 %all-to-all-done = f32[16,32,128]{2,1,0:T(8,128)S(1)} async-done(((f32[16,32,128]{2,1,0:T(8,128)}), f32[16,32,128]{2,1,0:T(8,128)S(1)}, u32[]{:S(2)}, u32[]{:S(2)}) %all-to-all-start) | async-done | bytes 262176 | tf_op jit(solution)/shard_map/all_to_all | solution.py:302
  48.4 3.5 %shard_map.78 = (bf16[16,8,1024]{2,1,0:T(8,128)(2,1)}, f32[32,16,128]{2,1,0:T(8,128)S(1)}) custom-call(f32[512,128]{1,0:T(8,128)S(1)} %bitcast.11, bf16[8,2,512,256]{3,2,1,0:T(8,128)(2,1)} %copy-done), custom_call_target="tpu_custom_call" | custom-call | flops 300000000 | bytes 5242880 | tf_op jit(solution)/shard_map/pallas_call | solution.py:312
  51.8 6.0 %all-to-all-start.1 = ((bf16[16,8,1024]{2,1,0:T(8,128)(2,1)}), bf16[16,8,1024]{2,1,0:T(8,128)(2,1)S(1)}, u32[]{:S(2)}, u32[]{:S(2)}) async-start(bf16[16,8,1024]{2,1,0:T(8,128)(2,1)} %get-tuple-element.23), calls=%async_computation.1 | async-start | bytes 524288 | tf_op jit(solution)/shard_map/all_to_all | solution.py:326
  57.8 9.7 %all-to-all-done.1.parts = bf16[16,8,1024]{2,1,0:T(8,128)(2,1)S(1)} async-done(((bf16[16,8,1024]{2,1,0:T(8,128)(2,1)}), bf16[16,8,1024]{2,1,0:T(8,128)(2,1)S(1)}, u32[]{:S(2)}, u32[]{:S(2)}) %all-to-all-start.1) | async-done | bytes 262176 | tf_op jit(solution)/shard_map/all_to_all | solution.py:326
  67.5 15.4 %all_to_all.15.misfit = bf16[16,8,1024]{2,1,0:T(8,128)(2,1)S(1)} all-to-all(bf16[16,8,1024]{2,1,0:T(8,128)(2,1)S(1)} %shard_map.79), channel_id=1, replica_groups=mesh['space'=8,'q'=16,'c'=2] {'q'}, dimensions={0} | all-to-all | bytes 524288 | tf_op jit(solution)/shard_map/all_to_all | solution.py:330
  83.0 2.0 %shard_map.80 = (f32[64,512]{1,0:T(8,128)S(1)}, bf16[64,2048]{1,0:T(8,128)(2,1)S(1)}) custom-call(s32[1]{0:T(128)} %bitcast.core, bf16[16,8,1024]{2,1,0:T(8,128)(2,1)S(1)} %all_to_all.15.misfit, bf16[2048,512]{1,0:T(8,128)(2,1)} %collective-permute-done.4.pair, f32[32,16,128]{2,1,0:T(8,128)S(1)} %get-tuple-element.24.cons), custom_call_target="tpu_custom_call" | custom-call | flops 150000000 | bytes 3145728 | tf_op jit(solution)/shard_map/pallas_call | solution.py:331
  85.0 3.5 %collective-permute-start.5 = (f32[64,512]{1,0:T(8,128)S(1)}, f32[64,512]{1,0:T(8,128)S(1)}, u32[]{:S(2)}, u32[]{:S(2)}) collective-permute-start(f32[64,512]{1,0:T(8,128)S(1)} %get-tuple-element.26), channel_id=1, source_target_pairs={{0,1},{1,0},{2,3},{3,2},{4,5},{5,4},{6,7},{7,6},{8,9},{9,8},{10,11... | collective-permute-start | bytes 393224 | tf_op jit(solution)/shard_map/ppermute | solution.py:343
  89.0 0.5 collective-permute-done.5.far
  89.5 0.8 shard_map.82
  (16 shorter events, 0.7 us)
Async XLA Ops:
  1.0 7.5 %collective-permute-start = (bf16[4,128,128]{2,1,0:T(8,128)(2,1)S(1)}, bf16[4,128,128]{2,1,0:T(8,128)(2,1)S(1)}, u32[]{:S(2)}, u32[]{:S(2)}) collective-permute-start(bf16[4,128,128]{2,1,0:T(8,128)(2,1)S(1)} %bitcast_convert_fusion.1.mine), channel_id=1, source_target_pairs={{0,1},{1,0},{2,3},{3,2},{4,5},{5,4},{6,7},{7,6},{8,9},{9,8},{10,11... | collective-permute-start | bytes 393224 | tf_op jit(solution)/shard_map/ppermute | solution.py:269
  1.7 6.7 %collective-permute-start.1 = (bf16[4,128,128]{2,1,0:T(8,128)(2,1)S(1)}, bf16[4,128,128]{2,1,0:T(8,128)(2,1)S(1)}, u32[]{:S(2)}, u32[]{:S(2)}) collective-permute-start(bf16[4,128,128]{2,1,0:T(8,128)(2,1)S(1)} %bitcast_convert_fusion.1.mine), channel_id=1, source_target_pairs={{1,2},{3,4},{5,6},{7,8},{9,10},{11,12},{13,14},{15,16},{17,18},{19... | collective-permute-start | bytes 393224 | tf_op jit(solution)/shard_map/ppermute | solution.py:271
  5.2 33.5 %collective-permute-start.4 = (bf16[2048,512]{1,0:T(8,128)(2,1)}, bf16[2048,512]{1,0:T(8,128)(2,1)}, u32[]{:S(2)}, u32[]{:S(2)}) collective-permute-start(bf16[2048,512]{1,0:T(8,128)(2,1)} %own.3), channel_id=1, source_target_pairs={{0,1},{1,0},{2,3},{3,2},{4,5},{5,4},{6,7},{7,6},{8,9},{9,8},{10,11... | collective-permute-start | bytes 6291464 | tf_op jit(solution)/shard_map/ppermute | solution.py:272
  9.0 9.3 %collective-permute-start.2 = (bf16[3,128,128]{2,1,0:T(8,128)(2,1)S(1)}, bf16[3,128,128]{2,1,0:T(8,128)(2,1)S(1)}, u32[]{:S(2)}, u32[]{:S(2)}) collective-permute-start(bf16[3,128,128]{2,1,0:T(8,128)(2,1)S(1)} %get-tuple-element.16), channel_id=1, source_target_pairs={{0,32},{32,0},{64,96},{96,64},{128,160},{160,128},{192,224},{224,1... | collective-permute-start | bytes 294920 | tf_op jit(solution)/shard_map/ppermute | solution.py:288
  9.7 8.7 %collective-permute-start.3 = (bf16[3,128,128]{2,1,0:T(8,128)(2,1)S(1)}, bf16[3,128,128]{2,1,0:T(8,128)(2,1)S(1)}, u32[]{:S(2)}, u32[]{:S(2)}) collective-permute-start(bf16[3,128,128]{2,1,0:T(8,128)(2,1)S(1)} %get-tuple-element.17), channel_id=1, source_target_pairs={{32,64},{96,128},{160,192},{64,32},{128,96},{192,160},{33,65},{97,... | collective-permute-start | bytes 294920 | tf_op jit(solution)/shard_map/ppermute | solution.py:290
  13.6 4.8 %copy-start.2 = (f32[1,4,128,128]{3,2,1,0:T(8,128)S(1)}, f32[1,4,128,128]{3,2,1,0:T(8,128)}, u32[]{:S(2)}) copy-start(f32[1,4,128,128]{3,2,1,0:T(8,128)} %param.7) | copy-start | bytes 786436
  18.4 20.3 %copy-start.1 = (bf16[2048,512]{1,0:T(8,128)(2,1)S(1)}, bf16[2048,512]{1,0:T(8,128)(2,1)}, u32[]{:S(2)}) copy-start(bf16[2048,512]{1,0:T(8,128)(2,1)} %own.3) | copy-start | bytes 6291460
  28.8 19.5 %all-to-all-start = ((f32[16,32,128]{2,1,0:T(8,128)}), f32[16,32,128]{2,1,0:T(8,128)S(1)}, u32[]{:S(2)}, u32[]{:S(2)}) async-start(f32[16,32,128]{2,1,0:T(8,128)} %bitcast.6), calls=%async_computation | async-start | bytes 524288 | tf_op jit(solution)/shard_map/all_to_all | solution.py:302
  41.8 2.0 %copy-start = (bf16[8,2,512,256]{3,2,1,0:T(8,128)(2,1)}, bf16[8,2,512,256]{3,2,1,0:T(8,128)(2,1)S(1)}, u32[]{:S(2)}) copy-start(bf16[8,2,512,256]{3,2,1,0:T(8,128)(2,1)S(1)} %shard_map.77.pixels) | copy-start | bytes 12582916
  43.8 14.1 %copy-start.3 = (f32[1,4,2048]{2,1,0:T(4,128)S(1)}, f32[1,4,2048]{2,1,0:T(4,128)}, u32[]{:S(2)}) copy-start(f32[1,4,2048]{2,1,0:T(4,128)} %param.13) | copy-start | bytes 98308
  51.8 15.7 %all-to-all-start.1 = ((bf16[16,8,1024]{2,1,0:T(8,128)(2,1)}), bf16[16,8,1024]{2,1,0:T(8,128)(2,1)S(1)}, u32[]{:S(2)}, u32[]{:S(2)}) async-start(bf16[16,8,1024]{2,1,0:T(8,128)(2,1)} %get-tuple-element.23), calls=%async_computation.1 | async-start | bytes 524288 | tf_op jit(solution)/shard_map/all_to_all | solution.py:326
  85.0 4.4 %collective-permute-start.5 = (f32[64,512]{1,0:T(8,128)S(1)}, f32[64,512]{1,0:T(8,128)S(1)}, u32[]{:S(2)}, u32[]{:S(2)}) collective-permute-start(f32[64,512]{1,0:T(8,128)S(1)} %get-tuple-element.26), channel_id=1, source_target_pairs={{0,1},{1,0},{2,3},{3,2},{4,5},{5,4},{6,7},{7,6},{8,9},{9,8},{10,11... | collective-permute-start | bytes 393224 | tf_op jit(solution)/shard_map/ppermute | solution.py:343
